TPU v7x, 32 devices: a whole 2x2x4 slice. The times are simulated.
32 devices in a mesh: dp: 8 (over z, core), mp: 4 (over y, x).
Axes of the slice: x: 2, y: 2, z: 4, core: 2. Of those that a mesh axis runs over, the one named last changes fastest.
Arguments:
- prefix_tokens: bfloat16 [6528, 2048], P('dp', 'mp'), may hold values from -6 to 6
- action_tokens: bfloat16 [400, 1024], P('dp', 'mp'), may hold values from -6 to 6
- camera_counts: int32 [8], P('dp'), may hold values from 1 to 3
- text_lengths: int32 [8], P('dp'), may hold values from 1 to 48
- prefix_attn_gain: float32 [2048], P('mp'), may hold values from 0.5 to 1.5
- prefix_query_proj: bfloat16 [2048, 2048], P('dp', 'mp'), may hold values from -0.125 to 0.125
- prefix_kv_proj: bfloat16 [2048, 512], P('dp', 'mp'), may hold values from -0.125 to 0.125
- prefix_out_proj: bfloat16 [2048, 2048], P('mp', 'dp'), may hold values from -2.5 to 2.5
- prefix_ffn_gain: float32 [2048], P('mp'), may hold values from 0.5 to 1.5
- prefix_gate_proj: bfloat16 [2048, 16384], P('dp', 'mp'), may hold values from -0.125 to 0.125
- prefix_up_proj: bfloat16 [2048, 16384], P('dp', 'mp'), may hold values from -0.125 to 0.125
- prefix_down_proj: bfloat16 [16384, 2048], P('mp', 'dp'), may hold values from -0.046875 to 0.046875
- action_attn_gain: float32 [1024], P('mp'), may hold values from 0.5 to 1.5
- action_query_proj: bfloat16 [1024, 2048], P('dp', 'mp'), may hold values from -0.1875 to 0.1875
- action_kv_proj: bfloat16 [1024, 512], P('dp', 'mp'), may hold values from -0.1875 to 0.1875
- action_out_proj: bfloat16 [2048, 1024], P('mp', 'dp'), may hold values from -2.5 to 2.5
- action_ffn_gain: float32 [1024], P('mp'), may hold values from 0.5 to 1.5
- action_gate_proj: bfloat16 [1024, 4096], P('dp', 'mp'), may hold values from -0.1875 to 0.1875
- action_up_proj: bfloat16 [1024, 4096], P('dp', 'mp'), may hold values from -0.1875 to 0.1875
- action_down_proj: bfloat16 [4096, 1024], P('mp', 'dp'), may hold values from -0.09375 to 0.09375
- prefix_cotangent: bfloat16 [6528, 2048], P('dp', 'mp'), may hold values from -6 to 6
- action_cotangent: bfloat16 [400, 1024], P('dp', 'mp'), may hold values from -6 to 6
Outputs:
- prefix_output: float32 [6528, 2048], P('dp', 'mp')
- action_output: float32 [400, 1024], P('dp', 'mp')
- prefix_gradient: float32 [6528, 2048], P('dp', 'mp')
- action_gradient: float32 [400, 1024], P('dp', 'mp')
- grad_prefix_attn_gain: float32 [2048], P('mp')
- grad_prefix_query_proj: float32 [2048, 2048], P('dp', 'mp')
- grad_prefix_kv_proj: float32 [2048, 512], P('dp', 'mp')
- grad_prefix_out_proj: float32 [2048, 2048], P('mp', 'dp')
- grad_prefix_ffn_gain: float32 [2048], P('mp')
- grad_prefix_gate_proj: float32 [2048, 16384], P('dp', 'mp')
- grad_prefix_up_proj: float32 [2048, 16384], P('dp', 'mp')
- grad_prefix_down_proj: float32 [16384, 2048], P('mp', 'dp')
- grad_action_attn_gain: float32 [1024], P('mp')
- grad_action_query_proj: float32 [1024, 2048], P('dp', 'mp')
- grad_action_kv_proj: float32 [1024, 512], P('dp', 'mp')
- grad_action_out_proj: float32 [2048, 1024], P('mp', 'dp')
- grad_action_ffn_gain: float32 [1024], P('mp')
- grad_action_gate_proj: float32 [1024, 4096], P('dp', 'mp')
- grad_action_up_proj: float32 [1024, 4096], P('dp', 'mp')
- grad_action_down_proj: float32 [4096, 1024], P('mp', 'dp')
All inputs are finite; a program needn't handle non-finite values.
Results may differ from a plain program's by a relative error of at most 0.02.
Values may be sent and summed in bfloat16 or wider, within the bound.
No kernel may reach another device: no remote copies, remote signals or barrier semaphores. Data moves between devices by JAX's collectives and lax.ppermute only.
A program may use at most 320 MiB of HBM per device.

v0:
```python
import jax
import jax.numpy as jnp
from jax import lax
from jax.sharding import PartitionSpec as P

HD = 256
IMG = 256
CAMS = 3


EPSILON = 1e-06
MASKED = -1e30


def matmul(matrix, factor):
    return jnp.dot(matrix, factor, preferred_element_type=jnp.float32)


def matmul_tn(matrix, factor):
    return lax.dot_general(
        matrix, factor, (((0,), (0,)), ((), ())), preferred_element_type=jnp.float32
    )


def matmul_nt(matrix, factor):
    return lax.dot_general(
        matrix, factor, (((1,), (1,)), ((), ())), preferred_element_type=jnp.float32
    )


def inverse_rms(inputs):
    return lax.rsqrt(jnp.mean(inputs * inputs, axis=1, keepdims=True) + EPSILON)


def spread(first, second, third, fourth):
    return (
        lax.all_gather(first, "mp", axis=1, tiled=True),
        lax.all_gather(second, "mp", axis=1, tiled=True),
        lax.all_gather(third, "mp", axis=0, tiled=True),
        lax.all_gather(fourth, "mp", axis=0, tiled=True),
    )


def combine(first, second):
    return (
        lax.psum_scatter(first, "mp", scatter_dimension=1, tiled=True),
        lax.psum_scatter(second, "mp", scatter_dimension=1, tiled=True),
    )


def collect(first, second):
    return (
        lax.all_gather(first, "mp", axis=1, tiled=True),
        lax.all_gather(second, "mp", axis=1, tiled=True),
    )


def valid_keys(camera_counts, text_lengths, length):
    position = lax.broadcasted_iota(jnp.int32, (camera_counts.shape[0], length), 1)
    image_end = camera_counts[:, None] * IMG
    text_start = CAMS * IMG
    return (position < image_end) | (position >= text_start) & (
        position < text_start + text_lengths[:, None]
    )


def masked_scores(queries, key_rows, key_mask):
    factor = key_rows.shape[-1] ** (-0.5)
    scores = (
        jnp.einsum("eqhd,ekd->ehqk", queries, key_rows, preferred_element_type=jnp.float32) * factor
    )
    return jnp.where(key_mask[:, None, None, :], scores, MASKED)


def attention_forward(queries, key_rows, value_rows, key_mask):
    scores = masked_scores(queries, key_rows, key_mask)
    highest = jnp.max(scores, axis=-1, keepdims=True)
    exp_terms = jnp.exp(scores - highest)
    totals = jnp.sum(exp_terms, axis=-1, keepdims=True)
    attn_low = (exp_terms / totals).astype(jnp.bfloat16)
    mixed = jnp.einsum("ehqk,ekd->eqhd", attn_low, value_rows, preferred_element_type=jnp.float32)
    return (mixed.astype(jnp.bfloat16), highest + jnp.log(totals))


def attention_backward(queries, key_rows, value_rows, key_mask, log_totals, grad_mixed):
    factor = key_rows.shape[-1] ** (-0.5)
    attn_weights = jnp.exp(masked_scores(queries, key_rows, key_mask) - log_totals)
    grad_attn = jnp.einsum(
        "eqhd,ekd->ehqk", grad_mixed, value_rows, preferred_element_type=jnp.float32
    )
    inner = jnp.sum(attn_weights * grad_attn, axis=-1, keepdims=True)
    grad_scores = (attn_weights * (grad_attn - inner)).astype(jnp.bfloat16)
    grad_queries = (
        jnp.einsum("ehqk,ekd->eqhd", grad_scores, key_rows, preferred_element_type=jnp.float32)
        * factor
    )
    grad_keys = (
        jnp.einsum("ehqk,eqhd->ekd", grad_scores, queries, preferred_element_type=jnp.float32)
        * factor
    )
    grad_values = jnp.einsum(
        "ehqk,eqhd->ekd",
        attn_weights.astype(jnp.bfloat16),
        grad_mixed,
        preferred_element_type=jnp.float32,
    )
    return (grad_queries, grad_keys, grad_values)


def gelu_back(gate_val, upval, grad_hidden):
    product, pullback = jax.vjp(
        lambda first, second: jax.nn.gelu(first, approximate=True) * second, gate_val, upval
    )
    grad_gate, grad_upval = pullback(grad_hidden)
    return (grad_gate.astype(jnp.bfloat16), grad_upval.astype(jnp.bfloat16))


def norm_back(
    part_pre,
    part_act,
    local_pre,
    local_act,
    whole_pre,
    whole_act,
    inv_pre,
    inv_act,
    gain_pre,
    gain_act,
):
    width_pre = whole_pre.shape[1]
    width_act = whole_act.shape[1]
    share_pre, share_act = (
        lax.psum_scatter(
            part_pre.astype(jnp.bfloat16), "mp", scatter_dimension=1, tiled=True
        ).astype(jnp.float32),
        lax.psum_scatter(
            part_act.astype(jnp.bfloat16), "mp", scatter_dimension=1, tiled=True
        ).astype(jnp.float32),
    )
    inner_pre = jnp.sum(share_pre * gain_pre * local_pre, axis=1, keepdims=True)
    inner_act = jnp.sum(share_act * gain_act * local_act, axis=1, keepdims=True)
    inner_pre, inner_act = lax.psum((inner_pre, inner_act), "mp")
    back_pre = inv_pre * gain_pre * share_pre - local_pre * inv_pre**3 * inner_pre / width_pre
    back_act = inv_act * gain_act * share_act - local_act * inv_act**3 * inner_act / width_act
    grad_gain_pre = jnp.sum(share_pre * local_pre * inv_pre, axis=0)
    grad_gain_act = jnp.sum(share_act * local_act * inv_act, axis=0)
    return (back_pre, back_act, grad_gain_pre, grad_gain_act)


def per_device(
    prefix_tokens,
    action_tokens,
    camera_counts,
    text_lengths,
    prefix_attn_gain,
    prefix_query_proj,
    prefix_kv_proj,
    prefix_out_proj,
    prefix_ffn_gain,
    prefix_gate_proj,
    prefix_up_proj,
    prefix_down_proj,
    action_attn_gain,
    action_query_proj,
    action_kv_proj,
    action_out_proj,
    action_ffn_gain,
    action_gate_proj,
    action_up_proj,
    action_down_proj,
    prefix_cotangent,
    action_cotangent,
):
    episodes = camera_counts.shape[0]
    prefix_rows = prefix_tokens.shape[0]
    action_rows = action_tokens.shape[0]
    prefix_len = prefix_rows // episodes
    action_len = action_rows // episodes
    local_heads = prefix_query_proj.shape[1] // HD
    prefix_mask = valid_keys(camera_counts, text_lengths, prefix_len)
    action_mask = jnp.concatenate(
        [prefix_mask, jnp.ones((episodes, action_len), jnp.bool_)], axis=1
    )
    (
        query_pre,
        keyval_pre,
        outproj_pre,
        gate_pre,
        upward_pre,
        downward_pre,
        query_act,
        keyval_act,
        outproj_act,
        gate_act,
        upward_act,
        downward_act,
    ) = (
        lax.all_gather(prefix_query_proj, "dp", axis=0, tiled=True),
        lax.all_gather(prefix_kv_proj, "dp", axis=0, tiled=True),
        lax.all_gather(prefix_out_proj, "dp", axis=1, tiled=True),
        lax.all_gather(prefix_gate_proj, "dp", axis=0, tiled=True),
        lax.all_gather(prefix_up_proj, "dp", axis=0, tiled=True),
        lax.all_gather(prefix_down_proj, "dp", axis=1, tiled=True),
        lax.all_gather(action_query_proj, "dp", axis=0, tiled=True),
        lax.all_gather(action_kv_proj, "dp", axis=0, tiled=True),
        lax.all_gather(action_out_proj, "dp", axis=1, tiled=True),
        lax.all_gather(action_gate_proj, "dp", axis=0, tiled=True),
        lax.all_gather(action_up_proj, "dp", axis=0, tiled=True),
        lax.all_gather(action_down_proj, "dp", axis=1, tiled=True),
    )
    local_pre = prefix_tokens.astype(jnp.float32)
    local_act = action_tokens.astype(jnp.float32)
    inputs_pre, inputs_act, gain_pre, gain_act = spread(
        local_pre, local_act, prefix_attn_gain, action_attn_gain
    )
    inv_pre = inverse_rms(inputs_pre)
    inv_act = inverse_rms(inputs_act)
    normed_pre = (inputs_pre * inv_pre * gain_pre).astype(jnp.bfloat16)
    normed_act = (inputs_act * inv_act * gain_act).astype(jnp.bfloat16)
    heads_pre = (
        matmul(normed_pre, query_pre)
        .astype(jnp.bfloat16)
        .reshape(episodes, prefix_len, local_heads, HD)
    )
    heads_act = (
        matmul(normed_act, query_act)
        .astype(jnp.bfloat16)
        .reshape(episodes, action_len, local_heads, HD)
    )
    kvpart_pre = matmul(normed_pre, keyval_pre).astype(jnp.bfloat16)
    kvpart_act = matmul(normed_act, keyval_act).astype(jnp.bfloat16)
    kvall_pre, kvall_act = (
        lax.all_gather(kvpart_pre, "mp", axis=1, tiled=True),
        lax.all_gather(kvpart_act, "mp", axis=1, tiled=True),
    )
    kvall_pre = kvall_pre.reshape(episodes, prefix_len, 2 * HD)
    kvall_act = kvall_act.reshape(episodes, action_len, 2 * HD)
    keys_pre = kvall_pre[:, :, :HD]
    values_pre = kvall_pre[:, :, HD:]
    keys_all = jnp.concatenate([keys_pre, kvall_act[:, :, :HD]], axis=1)
    values_all = jnp.concatenate([values_pre, kvall_act[:, :, HD:]], axis=1)
    mixed_pre, logsum_pre = attention_forward(heads_pre, keys_pre, values_pre, prefix_mask)
    mixed_act, logsum_act = attention_forward(heads_act, keys_all, values_all, action_mask)
    mixed_pre = mixed_pre.reshape(prefix_rows, local_heads * HD)
    mixed_act = mixed_act.reshape(action_rows, local_heads * HD)
    branch_pre, branch_act = combine(matmul(mixed_pre, outproj_pre), matmul(mixed_act, outproj_act))
    middle_pre = local_pre + branch_pre
    middle_act = local_act + branch_act
    midall_pre, midall_act, gain2_pre, gain2_act = spread(
        middle_pre, middle_act, prefix_ffn_gain, action_ffn_gain
    )
    inv2_pre = inverse_rms(midall_pre)
    inv2_act = inverse_rms(midall_act)
    normed2_pre = (midall_pre * inv2_pre * gain2_pre).astype(jnp.bfloat16)
    normed2_act = (midall_act * inv2_act * gain2_act).astype(jnp.bfloat16)
    gate_val_pre = matmul(normed2_pre, gate_pre)
    upval_pre = matmul(normed2_pre, upward_pre)
    gate_val_act = matmul(normed2_act, gate_act)
    upval_act = matmul(normed2_act, upward_act)
    hidden_pre = (jax.nn.gelu(gate_val_pre, approximate=True) * upval_pre).astype(jnp.bfloat16)
    hidden_act = (jax.nn.gelu(gate_val_act, approximate=True) * upval_act).astype(jnp.bfloat16)
    ffn_pre, ffn_act = combine(matmul(hidden_pre, downward_pre), matmul(hidden_act, downward_act))
    output_pre = middle_pre + ffn_pre
    output_act = middle_act + ffn_act
    cotall_pre, cotall_act = collect(prefix_cotangent, action_cotangent)
    grad_downward_pre = matmul_tn(hidden_pre, cotall_pre)
    grad_downward_act = matmul_tn(hidden_act, cotall_act)
    grad_gate_pre, grad_upval_pre = gelu_back(
        gate_val_pre, upval_pre, matmul_nt(cotall_pre, downward_pre)
    )
    grad_gate_act, grad_upval_act = gelu_back(
        gate_val_act, upval_act, matmul_nt(cotall_act, downward_act)
    )
    grad_gatew_pre = matmul_tn(normed2_pre, grad_gate_pre)
    grad_upward_pre = matmul_tn(normed2_pre, grad_upval_pre)
    grad_gatew_act = matmul_tn(normed2_act, grad_gate_act)
    grad_upward_act = matmul_tn(normed2_act, grad_upval_act)
    part2_pre = matmul_nt(grad_gate_pre, gate_pre) + matmul_nt(grad_upval_pre, upward_pre)
    part2_act = matmul_nt(grad_gate_act, gate_act) + matmul_nt(grad_upval_act, upward_act)
    back2_pre, back2_act, grad_gain2_pre, grad_gain2_act = norm_back(
        part2_pre,
        part2_act,
        middle_pre,
        middle_act,
        midall_pre,
        midall_act,
        inv2_pre,
        inv2_act,
        prefix_ffn_gain,
        action_ffn_gain,
    )
    resid_pre = prefix_cotangent.astype(jnp.float32) + back2_pre
    resid_act = action_cotangent.astype(jnp.float32) + back2_act
    rgrad_pre, rgrad_act = collect(resid_pre.astype(jnp.bfloat16), resid_act.astype(jnp.bfloat16))
    grad_outproj_pre = matmul_tn(mixed_pre, rgrad_pre)
    grad_outproj_act = matmul_tn(mixed_act, rgrad_act)
    gmixed_pre = (
        matmul_nt(rgrad_pre, outproj_pre)
        .astype(jnp.bfloat16)
        .reshape(episodes, prefix_len, local_heads, HD)
    )
    gmixed_act = (
        matmul_nt(rgrad_act, outproj_act)
        .astype(jnp.bfloat16)
        .reshape(episodes, action_len, local_heads, HD)
    )
    gq_pre, gk_pre, gv_pre = attention_backward(
        heads_pre, keys_pre, values_pre, prefix_mask, logsum_pre, gmixed_pre
    )
    gq_act, gk_all, gv_all = attention_backward(
        heads_act, keys_all, values_all, action_mask, logsum_act, gmixed_act
    )
    gkv_pre = jnp.concatenate(
        [gk_pre + gk_all[:, :prefix_len], gv_pre + gv_all[:, :prefix_len]], axis=2
    ).reshape(prefix_rows, 2 * HD)
    gkv_act = jnp.concatenate([gk_all[:, prefix_len:], gv_all[:, prefix_len:]], axis=2).reshape(
        action_rows, 2 * HD
    )
    kvgrad_pre, kvgrad_act = (
        lax.psum_scatter(
            gkv_pre.astype(jnp.bfloat16), "mp", scatter_dimension=1, tiled=True
        ).astype(jnp.float32),
        lax.psum_scatter(
            gkv_act.astype(jnp.bfloat16), "mp", scatter_dimension=1, tiled=True
        ).astype(jnp.float32),
    )
    kvgrad_pre = kvgrad_pre.astype(jnp.bfloat16)
    kvgrad_act = kvgrad_act.astype(jnp.bfloat16)
    qgrad_pre = gq_pre.reshape(prefix_rows, local_heads * HD).astype(jnp.bfloat16)
    qgrad_act = gq_act.reshape(action_rows, local_heads * HD).astype(jnp.bfloat16)
    grad_query_pre = matmul_tn(normed_pre, qgrad_pre)
    grad_query_act = matmul_tn(normed_act, qgrad_act)
    grad_keyval_pre = matmul_tn(normed_pre, kvgrad_pre)
    grad_keyval_act = matmul_tn(normed_act, kvgrad_act)
    part1_pre = matmul_nt(qgrad_pre, query_pre) + matmul_nt(kvgrad_pre, keyval_pre)
    part1_act = matmul_nt(qgrad_act, query_act) + matmul_nt(kvgrad_act, keyval_act)
    back1_pre, back1_act, grad_gain1_pre, grad_gain1_act = norm_back(
        part1_pre,
        part1_act,
        local_pre,
        local_act,
        inputs_pre,
        inputs_act,
        inv_pre,
        inv_act,
        prefix_attn_gain,
        action_attn_gain,
    )
    input_grad_pre = resid_pre + back1_pre
    input_grad_act = resid_act + back1_act
    (
        grad_query_pre,
        grad_keyval_pre,
        grad_outproj_pre,
        grad_gatew_pre,
        grad_upward_pre,
        grad_downward_pre,
        grad_query_act,
        grad_keyval_act,
        grad_outproj_act,
        grad_gatew_act,
        grad_upward_act,
        grad_downward_act,
    ) = (
        lax.psum_scatter(
            grad_query_pre.astype(jnp.bfloat16), "dp", scatter_dimension=0, tiled=True
        ).astype(jnp.float32),
        lax.psum_scatter(
            grad_keyval_pre.astype(jnp.bfloat16), "dp", scatter_dimension=0, tiled=True
        ).astype(jnp.float32),
        lax.psum_scatter(
            grad_outproj_pre.astype(jnp.bfloat16), "dp", scatter_dimension=1, tiled=True
        ).astype(jnp.float32),
        lax.psum_scatter(
            grad_gatew_pre.astype(jnp.bfloat16), "dp", scatter_dimension=0, tiled=True
        ).astype(jnp.float32),
        lax.psum_scatter(
            grad_upward_pre.astype(jnp.bfloat16), "dp", scatter_dimension=0, tiled=True
        ).astype(jnp.float32),
        lax.psum_scatter(
            grad_downward_pre.astype(jnp.bfloat16), "dp", scatter_dimension=1, tiled=True
        ).astype(jnp.float32),
        lax.psum_scatter(
            grad_query_act.astype(jnp.bfloat16), "dp", scatter_dimension=0, tiled=True
        ).astype(jnp.float32),
        lax.psum_scatter(
            grad_keyval_act.astype(jnp.bfloat16), "dp", scatter_dimension=0, tiled=True
        ).astype(jnp.float32),
        lax.psum_scatter(
            grad_outproj_act.astype(jnp.bfloat16), "dp", scatter_dimension=1, tiled=True
        ).astype(jnp.float32),
        lax.psum_scatter(
            grad_gatew_act.astype(jnp.bfloat16), "dp", scatter_dimension=0, tiled=True
        ).astype(jnp.float32),
        lax.psum_scatter(
            grad_upward_act.astype(jnp.bfloat16), "dp", scatter_dimension=0, tiled=True
        ).astype(jnp.float32),
        lax.psum_scatter(
            grad_downward_act.astype(jnp.bfloat16), "dp", scatter_dimension=1, tiled=True
        ).astype(jnp.float32),
    )
    grad_gain1_pre, grad_gain2_pre, grad_gain1_act, grad_gain2_act = lax.psum(
        (grad_gain1_pre, grad_gain2_pre, grad_gain1_act, grad_gain2_act), "dp"
    )
    return (
        output_pre,
        output_act,
        input_grad_pre,
        input_grad_act,
        grad_gain1_pre,
        grad_query_pre,
        grad_keyval_pre,
        grad_outproj_pre,
        grad_gain2_pre,
        grad_gatew_pre,
        grad_upward_pre,
        grad_downward_pre,
        grad_gain1_act,
        grad_query_act,
        grad_keyval_act,
        grad_outproj_act,
        grad_gain2_act,
        grad_gatew_act,
        grad_upward_act,
        grad_downward_act,
    )


def solution(mesh):
    return jax.shard_map(
        per_device,
        mesh=mesh,
        in_specs=(
            P("dp", "mp"),
            P("dp", "mp"),
            P("dp"),
            P("dp"),
            P("mp"),
            P("dp", "mp"),
            P("dp", "mp"),
            P("mp", "dp"),
            P("mp"),
            P("dp", "mp"),
            P("dp", "mp"),
            P("mp", "dp"),
            P("mp"),
            P("dp", "mp"),
            P("dp", "mp"),
            P("mp", "dp"),
            P("mp"),
            P("dp", "mp"),
            P("dp", "mp"),
            P("mp", "dp"),
            P("dp", "mp"),
            P("dp", "mp"),
        ),
        out_specs=(
            P("dp", "mp"),
            P("dp", "mp"),
            P("dp", "mp"),
            P("dp", "mp"),
            P("mp"),
            P("dp", "mp"),
            P("dp", "mp"),
            P("mp", "dp"),
            P("mp"),
            P("dp", "mp"),
            P("dp", "mp"),
            P("mp", "dp"),
            P("mp"),
            P("dp", "mp"),
            P("dp", "mp"),
            P("mp", "dp"),
            P("mp"),
            P("dp", "mp"),
            P("dp", "mp"),
            P("mp", "dp"),
        ),
        check_vma=False,
    )
```

profile of v0, /device:TPU:0, one launch (start us, length us, event | category | flops | bytes accessed | tf_op | source)
XLA Modules:
  0.0 2218.9 jit_solution(10477381731673856872)
XLA Ops:
  38.8 47.8 %all-gather.19.cloned.1.call-done = f32[816,2048]{1,0:T(8,128)} async-done(((f32[816,512]{1,0:T(8,128)}), f32[816,2048]{1,0:T(8,128)}) %all-gather.19.cloned.1.call-update) | async-done | bytes 6684688 | tf_op jit(solution)/shard_map/all_gather | solution.py:37
  126.4 23.0 %all-gather.23.cloned.1.call-done = bf16[512,2048]{1,0:T(8,128)(2,1)} async-done(((bf16[512,256]{1,0:T(8,128)(2,1)}), bf16[512,2048]{1,0:T(8,128)(2,1)}) %all-gather.23.cloned.1.call-update) | async-done | bytes 2097168 | tf_op jit(solution)/shard_map/all_gather | solution.py:200
  204.0 69.0 %reduce-scatter.31.cloned.1.call-done = f32[816,512]{1,0:T(8,128)} async-done(((f32[816,2048]{1,0:T(8,128)}), f32[816,512]{1,0:T(8,128)}) %reduce-scatter.31.cloned.1.call-update) | async-done | bytes 1671184 | tf_op jit(solution)/shard_map/reduce_scatter | solution.py:46
  333.5 28.1 %all-gather.39.cloned.1.call-done = bf16[1024,1024]{1,0:T(8,128)(2,1)} async-done(((bf16[128,1024]{1,0:T(8,128)(2,1)}), bf16[1024,1024]{1,0:T(8,128)(2,1)}) %all-gather.39.cloned.1.call-update) | async-done | bytes 2097168 | tf_op jit(solution)/shard_map/all_gather | solution.py:208
  363.6 29.8 %all-gather.41.cloned.1.call-done = bf16[1024,1024]{1,0:T(8,128)(2,1)} async-done(((bf16[1024,128]{1,0:T(8,128)(2,1)}), bf16[1024,1024]{1,0:T(8,128)(2,1)}) %all-gather.41.cloned.1.call-update) | async-done | bytes 2097168 | tf_op jit(solution)/shard_map/all_gather | solution.py:209
  398.8 69.7 %all-gather.25.cloned.1.call-done = f32[816,2048]{1,0:T(8,128)} async-done(((f32[816,512]{1,0:T(8,128)}), f32[816,2048]{1,0:T(8,128)}) %all-gather.25.cloned.1.call-update) | async-done | bytes 6684688 | tf_op jit(solution)/shard_map/all_gather | solution.py:37
  474.0 147.2 %all-gather.27.cloned.1.call-done = bf16[2048,4096]{1,0:T(8,128)(2,1)} async-done(((bf16[256,4096]{1,0:T(8,128)(2,1)}), bf16[2048,4096]{1,0:T(8,128)(2,1)}) %all-gather.27.cloned.1.call-update) | async-done | bytes 16777232 | tf_op jit(solution)/shard_map/all_gather | solution.py:201
  621.2 20.3 fusion.127
  641.5 130.8 %all-gather.29.cloned.1.call-done = bf16[2048,4096]{1,0:T(8,128)(2,1)} async-done(((bf16[256,4096]{1,0:T(8,128)(2,1)}), bf16[2048,4096]{1,0:T(8,128)(2,1)}) %all-gather.29.cloned.1.call-update) | async-done | bytes 16777232 | tf_op jit(solution)/shard_map/all_gather | solution.py:202
  772.3 20.3 fusion.128
  792.6 25.3 %all-gather.43.cloned.1.call-done = bf16[816,2048]{1,0:T(8,128)(2,1)} async-done(((bf16[816,512]{1,0:T(8,128)(2,1)}), bf16[816,2048]{1,0:T(8,128)(2,1)}) %all-gather.43.cloned.1.call-update) | async-done | bytes 3342352 | tf_op jit(solution)/shard_map/all_gather | solution.py:53
  817.8 153.4 %all-gather.31.cloned.1.call-done = bf16[4096,2048]{1,0:T(8,128)(2,1)} async-done(((bf16[4096,256]{1,0:T(8,128)(2,1)}), bf16[4096,2048]{1,0:T(8,128)(2,1)}) %all-gather.31.cloned.1.call-update) | async-done | bytes 16777232 | tf_op jit(solution)/shard_map/all_gather | solution.py:203
  971.2 31.7 %multiply_convert_fusion = (bf16[816,4096]{1,0:T(8,128)(2,1)}, bf16[816,4096]{1,0:T(8,128)(2,1)S(1)}, bf16[816,4096]{1,0:T(8,128)(2,1)}) fusion(f32[816,4096]{1,0:T(8,128)} %fusion.127, f32[816,4096]{1,0:T(8,128)} %fusion.128, bf16[816,2048]{1,0:T(8,128)(2,1)} %all-gather.43.cloned.1.call-done, bf16[4096,2048]{1,0:T(8,128)(2,1)} %all-gather.31.cloned.1.call-done), kind=kOutput, calls=%fused_computation.12 | convolution fusion | flops 13777108992 | bytes 66912256 | tf_op jit(solution)/shard_map/dot_general | solution.py:26
  1003.0 20.5 fusion.134
  1023.5 21.8 add_convert_fusion.1
  1047.6 41.8 %reduce-scatter.39.cloned.1.call-done = bf16[816,512]{1,0:T(8,128)(2,1)} async-done(((bf16[816,2048]{1,0:T(8,128)(2,1)}), bf16[816,512]{1,0:T(8,128)(2,1)}) %reduce-scatter.39.cloned.1.call-update) | async-done | bytes 835600 | tf_op jit(solution)/shard_map/reduce_scatter | solution.py:133
  1117.1 32.2 %all-gather.45.cloned.1.call-done = bf16[816,2048]{1,0:T(8,128)(2,1)} async-done(((bf16[816,512]{1,0:T(8,128)(2,1)}), bf16[816,2048]{1,0:T(8,128)(2,1)}) %all-gather.45.cloned.1.call-update) | async-done | bytes 3342352 | tf_op jit(solution)/shard_map/all_gather | solution.py:53
  1183.8 22.5 %reduce-scatter.67.cloned.1.call-done = bf16[128,816]{1,0:T(8,128)(2,1)} async-done(((bf16[512,816]{1,0:T(8,128)(2,1)}), bf16[128,816]{1,0:T(8,128)(2,1)}) %reduce-scatter.67.cloned.1.call-update) | async-done | bytes 208912
  1255.5 23.3 %convolution_convert_fusion.2 = bf16[2048,4096]{1,0:T(8,128)(2,1)} fusion(bf16[816,2048]{1,0:T(8,128)(2,1)S(1)} %copy-done.20, bf16[816,4096]{1,0:T(8,128)(2,1)} %copy-done.104), kind=kOutput, calls=%fused_computation.4 | convolution fusion | flops 13698596864 | bytes 26804224 | tf_op jit(solution)/shard_map/dot_general | solution.py:20
  1278.9 23.3 %convolution_convert_fusion.1 = bf16[2048,4096]{1,0:T(8,128)(2,1)} fusion(bf16[816,2048]{1,0:T(8,128)(2,1)S(1)} %copy-done.20, bf16[816,4096]{1,0:T(8,128)(2,1)} %get-tuple-element.36), kind=kOutput, calls=%fused_computation.3 | convolution fusion | flops 13698596864 | bytes 26804224 | tf_op jit(solution)/shard_map/dot_general | solution.py:20
  1304.2 23.4 %convolution_convert_fusion = bf16[4096,2048]{1,0:T(8,128)(2,1)} fusion(bf16[816,4096]{1,0:T(8,128)(2,1)} %get-tuple-element.38, bf16[816,2048]{1,0:T(8,128)(2,1)S(1)} %copy-done.101), kind=kOutput, calls=%fused_computation.2 | convolution fusion | flops 13698596864 | bytes 26804224 | tf_op jit(solution)/shard_map/dot_general | solution.py:20
  1344.2 31.8 %reduce-scatter.61.cloned.1.call-done = bf16[128,128]{1,0:T(8,128)(2,1)} async-done(((bf16[1024,128]{1,0:T(8,128)(2,1)}), bf16[128,128]{1,0:T(8,128)(2,1)}) %reduce-scatter.61.cloned.1.call-update) | async-done | bytes 32784 | tf_op jit(solution)/shard_map/reduce_scatter | solution.py:386
  1377.3 31.4 %reduce-scatter.71.cloned.1.call-done = bf16[128,512]{1,0:T(8,128)(2,1)} async-done(((bf16[1024,512]{1,0:T(8,128)(2,1)}), bf16[128,512]{1,0:T(8,128)(2,1)}) %reduce-scatter.71.cloned.1.call-update) | async-done | bytes 131088
  1410.5 31.7 %reduce-scatter.59.cloned.1.call-done = bf16[128,512]{1,0:T(8,128)(2,1)} async-done(((bf16[1024,512]{1,0:T(8,128)(2,1)}), bf16[128,512]{1,0:T(8,128)(2,1)}) %reduce-scatter.59.cloned.1.call-update) | async-done | bytes 131088 | tf_op jit(solution)/shard_map/reduce_scatter | solution.py:383
  1443.8 30.5 %reduce-scatter.49.cloned.1.call-done = bf16[256,128]{1,0:T(8,128)(2,1)} async-done(((bf16[2048,128]{1,0:T(8,128)(2,1)}), bf16[256,128]{1,0:T(8,128)(2,1)}) %reduce-scatter.49.cloned.1.call-update) | async-done | bytes 65552 | tf_op jit(solution)/shard_map/reduce_scatter | solution.py:368
  1475.8 35.4 %reduce-scatter.47.cloned.1.call-done = bf16[256,512]{1,0:T(8,128)(2,1)} async-done(((bf16[2048,512]{1,0:T(8,128)(2,1)}), bf16[256,512]{1,0:T(8,128)(2,1)}) %reduce-scatter.47.cloned.1.call-update) | async-done | bytes 262160 | tf_op jit(solution)/shard_map/reduce_scatter | solution.py:365
  1513.0 34.7 %reduce-scatter.51.cloned.1.call-done = bf16[512,256]{1,0:T(8,128)(2,1)} async-done(((bf16[512,2048]{1,0:T(8,128)(2,1)}), bf16[512,256]{1,0:T(8,128)(2,1)}) %reduce-scatter.51.cloned.1.call-update) | async-done | bytes 262160 | tf_op jit(solution)/shard_map/reduce_scatter | solution.py:371
  1549.5 46.1 %reduce-scatter.43.cloned.1.call-done = bf16[816,512]{1,0:T(8,128)(2,1)} async-done(((bf16[816,2048]{1,0:T(8,128)(2,1)}), bf16[816,512]{1,0:T(8,128)(2,1)}) %reduce-scatter.43.cloned.1.call-update) | async-done | bytes 835600 | tf_op jit(solution)/shard_map/reduce_scatter | solution.py:133
  1624.3 74.9 %reduce-scatter.33.cloned.1.call-done = f32[816,512]{1,0:T(8,128)} async-done(((f32[816,2048]{1,0:T(8,128)}), f32[816,512]{1,0:T(8,128)}) %reduce-scatter.33.cloned.1.call-update) | async-done | bytes 1671184 | tf_op jit(solution)/shard_map/reduce_scatter | solution.py:46
  1703.1 166.9 %reduce-scatter.53.cloned.1.call-done = bf16[256,4096]{1,0:T(8,128)(2,1)} async-done(((bf16[2048,4096]{1,0:T(8,128)(2,1)}), bf16[256,4096]{1,0:T(8,128)(2,1)}) %reduce-scatter.53.cloned.1.call-update) | async-done | bytes 2097168 | tf_op jit(solution)/shard_map/reduce_scatter | solution.py:374
  1874.1 165.0 %reduce-scatter.55.cloned.1.call-done = bf16[256,4096]{1,0:T(8,128)(2,1)} async-done(((bf16[2048,4096]{1,0:T(8,128)(2,1)}), bf16[256,4096]{1,0:T(8,128)(2,1)}) %reduce-scatter.55.cloned.1.call-update) | async-done | bytes 2097168 | tf_op jit(solution)/shard_map/reduce_scatter | solution.py:377
  2043.2 164.8 %reduce-scatter.57.cloned.1.call-done = bf16[4096,256]{1,0:T(8,128)(2,1)} async-done(((bf16[4096,2048]{1,0:T(8,128)(2,1)}), bf16[4096,256]{1,0:T(8,128)(2,1)}) %reduce-scatter.57.cloned.1.call-update) | async-done | bytes 2097168 | tf_op jit(solution)/shard_map/reduce_scatter | solution.py:380
  (423 shorter events, 383.0 us)
Async XLA Ops:
  9.8 107.5 %all-gather.21.cloned.1.call-start = ((), (), s32[]{:S(2)}) async-start(), calls=%async_computation.23 | async-start | bytes 2359296 | tf_op jit(solution)/shard_map/all_gather | solution.py:198
  10.6 138.7 %all-gather.23.cloned.1.call-start = ((), (), s32[]{:S(2)}) async-start(), calls=%async_computation.24 | async-start | bytes 2359296 | tf_op jit(solution)/shard_map/all_gather | solution.py:200
  11.3 185.0 %all-gather.33.cloned.1.call-start = ((), (), s32[]{:S(2)}) async-start(), calls=%async_computation.31 | async-start | bytes 1179648 | tf_op jit(solution)/shard_map/all_gather | solution.py:204
  11.9 187.8 %all-gather.35.cloned.1.call-start = ((), (), s32[]{:S(2)}) async-start(), calls=%async_computation.32 | async-start | bytes 1179648 | tf_op jit(solution)/shard_map/all_gather | solution.py:206
  12.5 260.5 %reduce-scatter.31.cloned.1.call-start = ((), (), s32[]{:S(2)}) async-start(), calls=%async_computation.25 | async-start | bytes 8355840 | tf_op jit(solution)/shard_map/reduce_scatter | solution.py:46
  155.6 147.1 %reduce-scatter.35.cloned.1.call-start = ((), (), s32[]{:S(2)}) async-start(), calls=%async_computation.33 | async-start | bytes 286720 | tf_op jit(solution)/shard_map/reduce_scatter | solution.py:47
  201.9 129.3 %all-gather.37.cloned.1.call-start = ((), (), s32[]{:S(2)}) async-start(), calls=%async_computation.34 | async-start | bytes 2359296 | tf_op jit(solution)/shard_map/all_gather | solution.py:207
  202.7 158.9 %all-gather.39.cloned.1.call-start = ((), (), s32[]{:S(2)}) async-start(), calls=%async_computation.35 | async-start | bytes 2359296 | tf_op jit(solution)/shard_map/all_gather | solution.py:208
  203.4 190.1 %all-gather.41.cloned.1.call-start = ((), (), s32[]{:S(2)}) async-start(), calls=%async_computation.36 | async-start | bytes 2359296 | tf_op jit(solution)/shard_map/all_gather | solution.py:209
  204.0 264.6 %all-gather.25.cloned.1.call-start = ((), (), s32[]{:S(2)}) async-start(), calls=%async_computation.26 | async-start | bytes 8355840 | tf_op jit(solution)/shard_map/all_gather | solution.py:37
  276.0 345.3 %all-gather.27.cloned.1.call-start = ((), (), s32[]{:S(2)}) async-start(), calls=%async_computation.27 | async-start | bytes 18874368 | tf_op jit(solution)/shard_map/all_gather | solution.py:201
  276.5 495.7 %all-gather.29.cloned.1.call-start = ((), (), s32[]{:S(2)}) async-start(), calls=%async_computation.28 | async-start | bytes 18874368 | tf_op jit(solution)/shard_map/all_gather | solution.py:202
  277.3 540.6 %all-gather.43.cloned.1.call-start = ((), (), s32[]{:S(2)}) async-start(), calls=%async_computation.38 | async-start | bytes 4177920 | tf_op jit(solution)/shard_map/all_gather | solution.py:53
  277.9 693.4 %all-gather.31.cloned.1.call-start = ((), (), s32[]{:S(2)}) async-start(), calls=%async_computation.29 | async-start | bytes 18874368 | tf_op jit(solution)/shard_map/all_gather | solution.py:203
  278.5 767.0 %reduce-scatter.41.cloned.1.call-start = ((), (), s32[]{:S(2)}) async-start(), calls=%async_computation.41 | async-start | bytes 143360 | tf_op jit(solution)/shard_map/reduce_scatter | solution.py:136
  398.8 690.6 %reduce-scatter.39.cloned.1.call-start = ((), (), s32[]{:S(2)}) async-start(), calls=%async_computation.39 | async-start | bytes 4177920 | tf_op jit(solution)/shard_map/reduce_scatter | solution.py:133
  1165.9 161.8 %reduce-scatter.73.cloned.1.call-start = ((), (), s32[]{:S(2)}) async-start(), calls=%async_computation.57 | async-start | bytes 2359296
  1169.3 160.4 %reduce-scatter.63.cloned.1.call-start = ((), (), s32[]{:S(2)}) async-start(), calls=%async_computation.52 | async-start | bytes 2359296 | tf_op jit(solution)/shard_map/reduce_scatter | solution.py:392
  1171.5 160.2 %reduce-scatter.65.cloned.1.call-start = ((), (), s32[]{:S(2)}) async-start(), calls=%async_computation.53 | async-start | bytes 2359296 | tf_op jit(solution)/shard_map/reduce_scatter | solution.py:395
  1173.7 169.0 %reduce-scatter.45.cloned.1.call-start = ((), (), s32[]{:S(2)}) async-start(), calls=%async_computation.43 | async-start | bytes 143360 | tf_op jit(solution)/shard_map/reduce_scatter | solution.py:136
  1178.3 197.6 %reduce-scatter.61.cloned.1.call-start = ((), (), s32[]{:S(2)}) async-start(), calls=%async_computation.51 | async-start | bytes 294912 | tf_op jit(solution)/shard_map/reduce_scatter | solution.py:386
  1180.1 228.5 %reduce-scatter.71.cloned.1.call-start = ((), (), s32[]{:S(2)}) async-start(), calls=%async_computation.56 | async-start | bytes 1179648
  1182.1 260.1 %reduce-scatter.59.cloned.1.call-start = ((), (), s32[]{:S(2)}) async-start(), calls=%async_computation.50 | async-start | bytes 1179648 | tf_op jit(solution)/shard_map/reduce_scatter | solution.py:383
  1183.6 290.8 %reduce-scatter.49.cloned.1.call-start = ((), (), s32[]{:S(2)}) async-start(), calls=%async_computation.45 | async-start | bytes 589824 | tf_op jit(solution)/shard_map/reduce_scatter | solution.py:368
  1210.3 300.9 %reduce-scatter.47.cloned.1.call-start = ((), (), s32[]{:S(2)}) async-start(), calls=%async_computation.44 | async-start | bytes 2359296 | tf_op jit(solution)/shard_map/reduce_scatter | solution.py:365
  1218.3 329.4 %reduce-scatter.51.cloned.1.call-start = ((), (), s32[]{:S(2)}) async-start(), calls=%async_computation.46 | async-start | bytes 2359296 | tf_op jit(solution)/shard_map/reduce_scatter | solution.py:371
  1224.1 371.5 %reduce-scatter.43.cloned.1.call-start = ((), (), s32[]{:S(2)}) async-start(), calls=%async_computation.42 | async-start | bytes 4177920 | tf_op jit(solution)/shard_map/reduce_scatter | solution.py:133
  1230.6 392.0 %reduce-scatter.37.cloned.1.call-start = ((), (), s32[]{:S(2)}) async-start(), calls=%async_computation.37 | async-start | bytes 286720 | tf_op jit(solution)/shard_map/reduce_scatter | solution.py:47
  1233.4 465.9 %reduce-scatter.33.cloned.1.call-start = ((), (), s32[]{:S(2)}) async-start(), calls=%async_computation.30 | async-start | bytes 8355840 | tf_op jit(solution)/shard_map/reduce_scatter | solution.py:46
  1253.6 616.3 %reduce-scatter.53.cloned.1.call-start = ((), (), s32[]{:S(2)}) async-start(), calls=%async_computation.47 | async-start | bytes 18874368 | tf_op jit(solution)/shard_map/reduce_scatter | solution.py:374
  1278.8 760.2 %reduce-scatter.55.cloned.1.call-start = ((), (), s32[]{:S(2)}) async-start(), calls=%async_computation.48 | async-start | bytes 18874368 | tf_op jit(solution)/shard_map/reduce_scatter | solution.py:377
  1302.3 905.7 %reduce-scatter.57.cloned.1.call-start = ((), (), s32[]{:S(2)}) async-start(), calls=%async_computation.49 | async-start | bytes 18874368 | tf_op jit(solution)/shard_map/reduce_scatter | solution.py:380
  (111 other events, 6616.1 us)
Sparse Core Ops, SparseCore 0:
  10.5 76.1 all-gather.18
  88.2 29.0 all-gather.20
  119.0 30.3 all-gather.22
  200.1 72.8 reduce-scatter.30
  276.4 24.0 reduce-scatter.34
  302.1 29.0 all-gather.36
  332.9 28.5 all-gather.38
  363.1 30.3 all-gather.40
  396.0 72.4 all-gather.24
  470.1 151.0 all-gather.26
  622.9 149.3 all-gather.28
  774.1 43.6 all-gather.42
  819.4 151.8 all-gather.30
  1045.5 43.7 reduce-scatter.38
  1103.8 45.3 all-gather.44
  1152.8 23.8 reduce-scatter.68
  1179.4 26.8 reduce-scatter.66
  1208.6 35.7 reduce-scatter.72
  1246.8 34.3 reduce-scatter.62
  1283.5 34.4 reduce-scatter.64
  1345.5 30.3 reduce-scatter.60
  1378.2 30.4 reduce-scatter.70
  1411.5 30.6 reduce-scatter.58
  1445.1 29.1 reduce-scatter.48
  1477.2 33.9 reduce-scatter.46
  1513.4 34.3 reduce-scatter.50
  1551.4 44.2 reduce-scatter.42
  1598.4 24.0 reduce-scatter.36
  1625.7 73.4 reduce-scatter.32
  1701.7 168.1 reduce-scatter.52
  1872.4 166.5 reduce-scatter.54
  2041.4 166.5 reduce-scatter.56
  (4 shorter events, 87.1 us)
where the time goes:
time: 2230 us; the launch traced here: 2220 us
  waiting for transfers between devices  1680 us (75%)
  matrix products  284 us (13%)
  blocking collectives  151 us (7%)
  other arithmetic  61 us (3%)
    reduce_scatter x1, waiting for transfers between devices, per_device(): lax.psum_scatter(grad_gatew_pre.astype(jnp.bfloat16), 'dp', scatter_dimen...  167 us
    reduce_scatter x1, waiting for transfers between devices, per_device(): lax.psum_scatter(grad_upward_pre.astype(jnp.bfloat16), 'dp', scatter_dime...  165 us
    reduce_scatter x1, waiting for transfers between devices, per_device(): lax.psum_scatter(grad_downward_pre.astype(jnp.bfloat16), 'dp', scatter_di...  165 us
    all_gather x1, waiting for transfers between devices, per_device(): lax.all_gather(prefix_down_proj, 'dp', axis=1, tiled=True)  153 us
    all_gather x1, waiting for transfers between devices, per_device(): lax.all_gather(prefix_gate_proj, 'dp', axis=0, tiled=True)  147 us
    reduce_scatter x2, waiting for transfers between devices, combine(): lax.psum_scatter(first, 'mp', scatter_dimension=1, tiled=True)  144 us
    all_gather x1, waiting for transfers between devices, per_device(): lax.all_gather(prefix_up_proj, 'dp', axis=0, tiled=True)  131 us
    all_gather x2, waiting for transfers between devices, spread(): lax.all_gather(first, 'mp', axis=1, tiled=True)  118 us
  transfers between devices with their start and end apart: 36, of which 28 were waited for; matrix products, arithmetic and copies ran while one was open for 15% of the time, Pallas kernels for 0%

commit v1 on v0

v1 whole, which is shorter than its diff:
```python
import jax
import jax.numpy as jnp
from jax import lax
from jax.sharding import PartitionSpec as P

HD = 256
IMG = 256
CAMS = 3
EPSILON = 1e-06
MASKED = -1e30
BF = jnp.bfloat16
F32 = jnp.float32


def mm(a, b):
    return jnp.dot(a, b, preferred_element_type=F32)


def mm_tn(a, b):
    return lax.dot_general(a, b, (((0,), (0,)), ((), ())), preferred_element_type=F32)


def mm_nt(a, b):
    return lax.dot_general(a, b, (((1,), (1,)), ((), ())), preferred_element_type=F32)


def pad_rows(a, rows):
    return jnp.pad(a, ((0, rows - a.shape[0]), (0, 0)))


def swap(a, axis, size, step):
    return lax.ppermute(a, axis, [(i, i ^ step) for i in range(size)])


def exchange(a, axis):
    return lax.all_to_all(a, axis, 0, 0, tiled=True)


def copies(a, k):
    return jnp.broadcast_to(a[None], (k,) + a.shape)


def spread_blocks(block, k):
    if k == 4:
        half = block.shape[0] // 2
        first = swap(block, "mp", k, 1)
        second = swap(block, "mp", k, 2)
        low = swap(second[:half], "mp", k, 1)
        high = swap(first[half:], "mp", k, 2)
        return [block, first, second, jnp.concatenate([low, high], axis=0)]
    return [block] + [swap(block, "mp", k, s) for s in range(1, k)]


def collect_blocks(parts, k):
    total = parts[0].astype(F32)
    if k == 4:
        half = parts[0].shape[0] // 2
        low = swap(parts[3][:half], "mp", k, 1)
        high = swap(parts[3][half:], "mp", k, 2)
        first_low = swap(parts[1][:half], "mp", k, 1)
        second_high = swap(parts[2][half:], "mp", k, 2)
        second_low = swap(
            (parts[2][:half].astype(F32) + low.astype(F32)).astype(BF), "mp", k, 2
        )
        first_high = swap(
            (parts[1][half:].astype(F32) + high.astype(F32)).astype(BF), "mp", k, 1
        )
        lower = total[:half] + first_low.astype(F32) + second_low.astype(F32)
        upper = total[half:] + first_high.astype(F32) + second_high.astype(F32)
        return jnp.concatenate([lower.astype(BF), upper.astype(BF)], axis=0)
    for s in range(1, k):
        total = total + swap(parts[s], "mp", k, s).astype(F32)
    return total.astype(BF)


def inverse_rms(x):
    return lax.rsqrt(jnp.mean(x * x, axis=1, keepdims=True) + EPSILON)


def norm_back(grad, x, inv, gain):
    inner = jnp.sum(grad * gain * x, axis=1, keepdims=True)
    back = inv * gain * grad - x * inv**3 * inner / x.shape[1]
    return back, jnp.sum(grad * x * inv, axis=0)


def scores_of(queries, keys, mask):
    scores = jnp.einsum("qhd,kd->hqk", queries, keys, preferred_element_type=F32) * HD ** (-0.5)
    return jnp.where(mask[None, None, :], scores, MASKED)


def attend(queries, keys, values, mask):
    scores = scores_of(queries, keys, mask)
    highest = jnp.max(scores, axis=-1, keepdims=True)
    terms = jnp.exp(scores - highest)
    totals = jnp.sum(terms, axis=-1, keepdims=True)
    low = (terms / totals).astype(BF)
    mixed = jnp.einsum("hqk,kd->qhd", low, values, preferred_element_type=F32)
    return mixed.astype(BF), highest + jnp.log(totals)


def attend_back(queries, keys, values, mask, log_totals, grad_mixed):
    weights = jnp.exp(scores_of(queries, keys, mask) - log_totals)
    grad_attn = jnp.einsum("qhd,kd->hqk", grad_mixed, values, preferred_element_type=F32)
    inner = jnp.sum(weights * grad_attn, axis=-1, keepdims=True)
    grad_scores = (weights * (grad_attn - inner)).astype(BF)
    factor = HD ** (-0.5)
    gq = jnp.einsum("hqk,kd->qhd", grad_scores, keys, preferred_element_type=F32) * factor
    gk = jnp.einsum("hqk,qhd->kd", grad_scores, queries, preferred_element_type=F32) * factor
    gv = jnp.einsum("hqk,qhd->kd", weights.astype(BF), grad_mixed, preferred_element_type=F32)
    return gq, gk, gv


def gelu_both(gate, up, grad_hidden):
    product, pullback = jax.vjp(
        lambda a, b: jax.nn.gelu(a, approximate=True) * b, gate, up
    )
    grad_gate, grad_up = pullback(grad_hidden)
    return product.astype(BF), jnp.concatenate([grad_gate, grad_up], axis=1).astype(BF)


def unit_blocks(gate, up, down, n):
    depth, units = gate.shape[0], gate.shape[1] // n
    gate = gate.reshape(depth, n, units).transpose(1, 0, 2)
    up = up.reshape(depth, n, units).transpose(1, 0, 2)
    down = down.reshape(n, units, depth).transpose(0, 2, 1)
    return jnp.concatenate([gate, up], axis=2), down


def unblock(gate_up, down):
    n, depth, units = down.shape
    gate = gate_up[:, :, :units].transpose(1, 0, 2).reshape(depth, n * units)
    up = gate_up[:, :, units:].transpose(1, 0, 2).reshape(depth, n * units)
    down = down.transpose(0, 2, 1).reshape(n * units, depth)
    return gate.astype(F32), up.astype(F32), down.astype(F32)


def solution(mesh):
    n, k = mesh.shape["dp"], mesh.shape["mp"]

    def per_device(
        prefix_tokens,
        action_tokens,
        camera_counts,
        text_lengths,
        prefix_attn_gain,
        prefix_query_proj,
        prefix_kv_proj,
        prefix_out_proj,
        prefix_ffn_gain,
        prefix_gate_proj,
        prefix_up_proj,
        prefix_down_proj,
        action_attn_gain,
        action_query_proj,
        action_kv_proj,
        action_out_proj,
        action_ffn_gain,
        action_gate_proj,
        action_up_proj,
        action_down_proj,
        prefix_cotangent,
        action_cotangent,
    ):
        mine = lax.axis_index("mp")
        rows, wide = prefix_tokens.shape
        arows, awide = action_tokens.shape
        block = -(-rows // (16 * k)) * 16
        padded = block * k
        apad = -(-arows // 64) * 64
        width, awidth = wide * k, awide * k
        fold = apad * awidth // width
        heads = prefix_query_proj.shape[1] // HD
        qcols = heads * HD
        kvcols = prefix_kv_proj.shape[1]
        depth, adepth = prefix_query_proj.shape[0], action_query_proj.shape[0]

        with jax.named_scope("attention_weights"):
            qkv_pre = jnp.concatenate([prefix_query_proj, prefix_kv_proj], axis=1)
            qkv_act = jnp.concatenate([action_query_proj, action_kv_proj], axis=1)
            out_local = jnp.concatenate([prefix_out_proj.T, action_out_proj.T], axis=0)
            wqkv_pre = lax.all_gather(qkv_pre, "dp", axis=0, tiled=True)
            rest = jnp.concatenate(
                [out_local, jnp.pad(qkv_act, ((0, 0), (0, 0)))[:, :qcols]], axis=0
            )
            rest = lax.all_gather(rest, "dp", axis=0).reshape(n, depth + 2 * adepth, qcols)
            wkv_act = lax.all_gather(qkv_act[:, qcols:], "dp", axis=0, tiled=True)
            wout_pre = rest[:, :depth].reshape(n * depth, qcols)
            wout_act = rest[:, depth : depth + adepth].reshape(n * adepth, qcols)
            wq_act = rest[:, depth + adepth :].reshape(n * adepth, qcols)

        with jax.named_scope("token_features"):
            gains = jnp.concatenate(
                [prefix_attn_gain, prefix_ffn_gain, action_attn_gain, action_ffn_gain]
            )[None]
            gains = exchange(copies(gains, k), "mp")[:, 0]
            gain_pre = gains[:, :wide].reshape(1, width)
            gain2_pre = gains[:, wide : 2 * wide].reshape(1, width)
            gain_act = gains[:, 2 * wide : 2 * wide + awide].reshape(1, awidth)
            gain2_act = gains[:, 2 * wide + awide :].reshape(1, awidth)
            x_act = pad_rows(action_tokens, apad)
            x_all = jnp.concatenate(
                [pad_rows(prefix_tokens, padded), x_act.reshape(-1, wide)], axis=0
            )
            x_all = exchange(copies(x_all, k), "mp")
            x_pre = x_all[:, :padded].transpose(1, 0, 2).reshape(padded, width).astype(F32)
            x_act = (
                x_all[:, padded:]
                .reshape(k, apad, awide)
                .transpose(1, 0, 2)
                .reshape(apad, awidth)
                .astype(F32)
            )

        with jax.named_scope("cotangents"):
            g_act = pad_rows(action_cotangent, apad)
            g_all = jnp.concatenate(
                [
                    pad_rows(prefix_cotangent, padded).reshape(k, block, wide),
                    copies(g_act.reshape(-1, wide), k),
                ],
                axis=1,
            )
            g_all = exchange(g_all, "mp")
            g_pre = g_all[:, :block].transpose(1, 0, 2).reshape(block, width)
            g_act = (
                g_all[:, block:].reshape(k, apad, awide).transpose(1, 0, 2).reshape(apad, awidth)
            )
            gall_pre = lax.all_gather(g_pre, "dp", axis=0, tiled=True)
            gall_act = lax.all_gather(g_act, "dp", axis=0, tiled=True)

        with jax.named_scope("unit_weights"):
            gu_local, dt_local = unit_blocks(prefix_gate_proj, prefix_up_proj, prefix_down_proj, n)
            units = dt_local.shape[2]
            dt_own = exchange(dt_local, "dp").reshape(width, units)
            gu_own = exchange(gu_local, "dp").reshape(width, 2 * units)
            dts = spread_blocks(dt_own, k)
            gus = spread_blocks(gu_own, k)
            gu_act, dt_act = unit_blocks(action_gate_proj, action_up_proj, action_down_proj, n)
            aunits = dt_act.shape[2]
            w_act = exchange(jnp.concatenate([gu_act, dt_act], axis=2), "dp")
            w_act = w_act.reshape(awidth, 3 * aunits)
            gu_act, dt_act = w_act[:, : 2 * aunits], w_act[:, 2 * aunits :]

        with jax.named_scope("attention"):
            mask_pre = jnp.arange(padded, dtype=jnp.int32)
            text = CAMS * IMG
            mask_pre = (mask_pre < camera_counts[0] * IMG) | (
                (mask_pre >= text) & (mask_pre < text + text_lengths[0])
            )
            mask_all = jnp.concatenate([mask_pre, jnp.arange(apad) < arows])
            inv_pre, inv_act = inverse_rms(x_pre), inverse_rms(x_act)
            normed_pre = (x_pre * inv_pre * gain_pre).astype(BF)
            normed_act = (x_act * inv_act * gain_act).astype(BF)
            qkv_p = mm(normed_pre, wqkv_pre).astype(BF)
            q_act = mm(normed_act, wq_act).astype(BF)
            kv_a = mm(normed_act, wkv_act).astype(BF)
            kv = jnp.concatenate([qkv_p[:, qcols:], kv_a], axis=0)
            kv = exchange(copies(kv, k), "mp").transpose(1, 0, 2).reshape(padded + apad, k * kvcols)
            keys, values = kv[:, :HD], kv[:, HD:]
            q_pre = qkv_p[:, :qcols].reshape(padded, heads, HD)
            q_act = q_act.reshape(apad, heads, HD)
            mixed_pre, log_pre = attend(q_pre, keys[:padded], values[:padded], mask_pre)
            mixed_act, log_act = attend(q_act, keys, values, mask_all)
            mixed_pre = mixed_pre.reshape(padded, qcols)
            mixed_act = mixed_act.reshape(apad, qcols)
            branch_pre = mm_nt(mixed_pre, wout_pre).astype(BF).reshape(k, block, width)
            branch_act = mm_nt(mixed_act, wout_act).astype(BF).reshape(fold, width)
            branch = exchange(
                jnp.concatenate([branch_pre, copies(branch_act, k)], axis=1), "mp"
            ).astype(F32)
            branch = jnp.sum(branch, axis=0)
            xrow_pre = lax.dynamic_slice_in_dim(x_pre, mine * block, block, 0)
            middle_pre = xrow_pre + branch[:block]
            middle_act = x_act + branch[block:].reshape(apad, awidth)
            inv2_pre, inv2_act = inverse_rms(middle_pre), inverse_rms(middle_act)
            normed2_pre = (middle_pre * inv2_pre * gain2_pre).astype(BF)
            normed2_act = (middle_act * inv2_act * gain2_act).astype(BF)
            nall_pre = lax.all_gather(normed2_pre, "dp", axis=0, tiled=True)
            nall_act = lax.all_gather(normed2_act, "dp", axis=0, tiled=True)

        with jax.named_scope("geglu"):
            hiddens, grads = [], []
            for gu, dt in zip(gus, dts):
                grad_hidden = mm(gall_pre, dt)
                both = mm(nall_pre, gu)
                hidden, grad = gelu_both(both[:, :units], both[:, units:], grad_hidden)
                hiddens.append(hidden)
                grads.append(grad)
            gn2 = sum(mm_nt(grad, gu) for grad, gu in zip(grads, gus)).astype(BF)
            gn2 = lax.psum_scatter(gn2, "dp", scatter_dimension=0, tiled=True)
            gw_dt = [mm_tn(gall_pre, hidden).astype(BF) for hidden in hiddens]
            gw_gu = [mm_tn(nall_pre, grad).astype(BF) for grad in grads]
            ffn = sum(mm_nt(hidden, dt) for hidden, dt in zip(hiddens, dts)).astype(BF)
            ffn = lax.psum_scatter(ffn, "dp", scatter_dimension=0, tiled=True)
            dgrad = exchange(collect_blocks(gw_dt, k).reshape(n, depth, units), "dp")
            gugrad = exchange(collect_blocks(gw_gu, k).reshape(n, depth, 2 * units), "dp")

            both = mm(nall_act, gu_act)
            hidden, grad = gelu_both(both[:, :aunits], both[:, aunits:], mm(gall_act, dt_act))
            part = jnp.concatenate([mm_nt(hidden, dt_act), mm_nt(grad, gu_act)], axis=1).astype(BF)
            gw_act = jnp.concatenate([mm_tn(nall_act, grad), mm_tn(gall_act, hidden)], axis=1)
            gw_act = exchange(gw_act.astype(BF).reshape(n, adepth, 3 * aunits), "dp")
            part = lax.psum_scatter(part, "dp", scatter_dimension=0, tiled=True)
            part = jnp.concatenate(
                [
                    part[:, :awidth].reshape(apad, k, awide).transpose(1, 0, 2),
                    copies(part[:, awidth:], k),
                ],
                axis=2,
            )
            part = jnp.sum(exchange(part, "mp").astype(F32), axis=0)
            output_act = (
                lax.dynamic_slice_in_dim(middle_act, mine * awide, awide, 1) + part[:, :awide]
            )[:arows]
            gn2_act = part[:, awide:]
            out_pre = (middle_pre + ffn.astype(F32)).astype(BF)
            out_pre = exchange(out_pre.reshape(block, k, wide).transpose(1, 0, 2), "mp")
            output_pre = out_pre.reshape(padded, wide)[:rows].astype(F32)

        with jax.named_scope("middle_norm"):
            back2_pre, gg2_pre = norm_back(gn2.astype(F32), middle_pre, inv2_pre, gain2_pre)
            back2_act, gg2_act = norm_back(gn2_act, middle_act, inv2_act, gain2_act)
            resid_pre = g_pre.astype(F32) + back2_pre
            resid_act = g_act.astype(F32) + back2_act
            gb_pre = exchange(copies(resid_pre.astype(BF), k), "mp").reshape(padded, width)
            gb_act = resid_act.astype(BF)

        with jax.named_scope("attention_back"):
            gm_pre = mm(gb_pre, wout_pre).astype(BF).reshape(padded, heads, HD)
            gm_act = mm(gb_act, wout_act).astype(BF).reshape(apad, heads, HD)
            gq_pre, gk_pre, gv_pre = attend_back(
                q_pre, keys[:padded], values[:padded], mask_pre, log_pre, gm_pre
            )
            gq_act, gk_all, gv_all = attend_back(q_act, keys, values, mask_all, log_act, gm_act)
            gk = jnp.concatenate([gk_pre + gk_all[:padded], gk_all[padded:]], axis=0)
            gv = jnp.concatenate([gv_pre + gv_all[:padded], gv_all[padded:]], axis=0)
            gkv = jnp.concatenate([gk, gv], axis=1).astype(BF)
            gkv = exchange(gkv.reshape(padded + apad, k, kvcols).transpose(1, 0, 2), "mp")
            gkv = jnp.sum(gkv.astype(F32), axis=0).astype(BF)
            gq_pre = gq_pre.reshape(padded, qcols).astype(BF)
            gq_act = gq_act.reshape(apad, qcols).astype(BF)
            gqkv_pre = jnp.concatenate([gq_pre, gkv[:padded]], axis=1)
            gqkv_act = jnp.concatenate([gq_act, gkv[padded:]], axis=1)
            gn_pre = mm_nt(gqkv_pre, wqkv_pre).astype(BF).reshape(k, block, width)
            gn_act = mm_nt(gq_act, wq_act) + mm_nt(gkv[padded:], wkv_act)
            gn = jnp.concatenate(
                [gn_pre, copies(gn_act.astype(BF).reshape(fold, width), k)], axis=1
            )
            gn = jnp.sum(exchange(gn, "mp").astype(F32), axis=0)
            invrow = lax.dynamic_slice_in_dim(inv_pre, mine * block, block, 0)
            back_pre, gg_pre = norm_back(gn[:block], xrow_pre, invrow, gain_pre)
            back_act, gg_act = norm_back(
                gn[block:].reshape(apad, awidth), x_act, inv_act, gain_act
            )
            in_pre = (resid_pre + back_pre).astype(BF)
            in_pre = exchange(in_pre.reshape(block, k, wide).transpose(1, 0, 2), "mp")
            in_pre = in_pre.reshape(padded, wide)[:rows].astype(F32)
            in_act = lax.dynamic_slice_in_dim(resid_act + back_act, mine * awide, awide, 1)[:arows]

        with jax.named_scope("attention_weight_grads"):
            go_pre = mm_tn(gb_pre, mixed_pre).astype(BF).reshape(n, depth, qcols)
            go_act = mm_tn(gb_act, mixed_act).astype(BF).reshape(n, adepth, qcols)
            go = jnp.concatenate([go_pre, go_act], axis=1).reshape(-1, qcols)
            go = lax.psum_scatter(go, "dp", scatter_dimension=0, tiled=True).astype(F32)
            gw_pre = mm_tn(normed_pre, gqkv_pre).astype(BF).reshape(n, depth, -1)
            gw_a = mm_tn(normed_act, gqkv_act).astype(BF).reshape(n, adepth, -1)
            gw = jnp.concatenate([gw_pre, gw_a], axis=1).reshape(-1, qcols + kvcols)
            gw = lax.psum_scatter(gw, "dp", scatter_dimension=0, tiled=True).astype(F32)

        with jax.named_scope("gain_grads"):
            once = (mine == 0).astype(F32)
            gg = jnp.concatenate([gg_pre, gg2_pre, gg_act * once, gg2_act * once])
            gg = lax.psum(gg, ("dp", "mp"))
            gg_pre = lax.dynamic_slice_in_dim(gg, mine * wide, wide)
            gg2_pre = lax.dynamic_slice_in_dim(gg, width + mine * wide, wide)
            gg_act = lax.dynamic_slice_in_dim(gg, 2 * width + mine * awide, awide)
            gg2_act = lax.dynamic_slice_in_dim(gg, 2 * width + awidth + mine * awide, awide)

        with jax.named_scope("unit_weight_grads"):
            gate_pre, up_pre, down_pre = unblock(gugrad, dgrad)
            gate_act, up_act, down_act = unblock(gw_act[:, :, : 2 * aunits], gw_act[:, :, 2 * aunits :])
        return (
            output_pre,
            output_act,
            in_pre,
            in_act,
            gg_pre,
            gw[:depth, :qcols],
            gw[:depth, qcols:],
            go[:depth].T,
            gg2_pre,
            gate_pre,
            up_pre,
            down_pre,
            gg_act,
            gw[depth:, :qcols],
            gw[depth:, qcols:],
            go[depth:].T,
            gg2_act,
            gate_act,
            up_act,
            down_act,
        )

    split, rowsplit, whole = P("dp", "mp"), P("mp", "dp"), P("mp")
    weights = (whole, split, split, rowsplit, whole, split, split, rowsplit)
    return jax.shard_map(
        per_device,
        mesh=mesh,
        in_specs=(split, split, P("dp"), P("dp")) + weights + weights + (split, split),
        out_specs=(split, split, split, split) + weights + weights,
        check_vma=False,
    )
```

time: 2230 us -> 1450 us (0.65)
  waiting for transfers between devices: 1680 us -> 724 us
  starting transfers between devices: 2.5 us -> 95.4 us
  local copies, waits for them, and re-layouts: 21.8 us -> 114 us
  blocking collectives: 151 us -> 70.8 us
  matrix products: 284 us -> 325 us
  other arithmetic: 61 us -> 95.8 us
    reduce_scatter x18 -> x4, waiting for transfers between devices: 902 us -> 0.04 us  [the longest x1 0.02 us: per_device(): part = lax.psum_scatter(part, 'dp', scatter_dimension=0, tiled=True)]
    all_gather x14 -> x6, waiting for transfers between devices: 716 us -> 0.05 us  [the longest x1 0.02 us: per_device(): gall_act = lax.all_gather(g_act, 'dp', axis=0, tiled=True)]
    all_to_all x0 -> x16, waiting for transfers between devices: none -> 591 us  [exchange(): return lax.all_to_all(a, axis, 0, 0, tiled=True)]
    ppermute x0 -> x20, waiting for transfers between devices: none -> 133 us  [swap(): return lax.ppermute(a, axis, [(i, i ^ step) for i in range(size)])]
    all_gather x12 -> x1, blocking collectives: 117 us -> 16.6 us  [per_device(): wkv_act = lax.all_gather(qkv_act[:, qcols:], 'dp', axis=0, tiled=True)]
    all_to_all x0 -> x16, starting transfers between devices: none -> 71.4 us  [exchange(): return lax.all_to_all(a, axis, 0, 0, tiled=True)]
    unnamed x40 -> x12, waiting for transfers between devices: 63 us -> 0.18 us
    dot_general x48 -> x56, matrix products: 284 us -> 325 us  [the longest x15 112 us: mm_nt(): lax.dot_general(a, b, (((1,), (1,)), ((), ())), preferred_element_type=F32)]
  transfers between devices with their start and end apart: 36 -> 47, of which waited for: 28 -> 20; matrix products, arithmetic and copies ran while one was open for 15% -> 34% of each run, Pallas kernels for 0% -> 0%
where the time goes in v1:
time: 1450 us; the launch traced here: 1440 us
  waiting for transfers between devices  724 us (50%)
  matrix products  325 us (22%)
  local copies, waits for them, and re-layouts  114 us (8%)
  other arithmetic  95.8 us (7%)
  starting transfers between devices  95.4 us (7%)
  blocking collectives  70.8 us (5%)
  between operations  17.4 us (1%)
    all_to_all x16, waiting for transfers between devices, exchange(): return lax.all_to_all(a, axis, 0, 0, tiled=True)  591 us
    ppermute x20, waiting for transfers between devices, swap(): return lax.ppermute(a, axis, [(i, i ^ step) for i in range(size)])  133 us
    dot_general x15, matrix products, mm_nt(): lax.dot_general(a, b, (((1,), (1,)), ((), ())), preferred_element_type=F32)  112 us
    dot_general x15, matrix products, mm(): return jnp.dot(a, b, preferred_element_type=F32)  111 us
    dot_general x14, matrix products, mm_tn(): lax.dot_general(a, b, (((0,), (0,)), ((), ())), preferred_element_type=F32)  87.6 us
    all_to_all x16, starting transfers between devices, exchange(): return lax.all_to_all(a, axis, 0, 0, tiled=True)  71.4 us
    psum x1, blocking collectives, per_device(): gg = lax.psum(gg, ('dp', 'mp'))  38.5 us
    unnamed x273, local copies, waits for them, and re-layouts  35.9 us
  transfers between devices with their start and end apart: 47, of which 20 were waited for; matrix products, arithmetic and copies ran while one was open for 34% of the time, Pallas kernels for 0%

profile of v1, /device:TPU:0, one launch (start us, length us, event | category | flops | bytes accessed | tf_op | source)
XLA Modules:
  0.0 1442.2 jit_solution(5727543926037477674)
XLA Ops:
  29.8 16.6 %all_gather.25 = bf16[1024,128]{1,0:T(8,128)(2,1)} all-gather(bf16[128,128]{1,0:T(8,128)(2,1)} %param.36), channel_id=1, replica_groups=mesh['dp'=8,'mp'=4] {'dp'}, dimensions={0}, use_global_device_ids=true | all-gather | bytes 294912 | tf_op jit(solution)/shard_map/attention_weights/all_gather | solution.py:186
  48.4 16.9 %all-to-all-done = bf16[4,864,512]{2,1,0:T(8,128)(2,1)S(1)} async-done(((bf16[4,864,512]{2,1,0:T(8,128)(2,1)}), bf16[4,864,512]{2,1,0:T(8,128)(2,1)S(1)}, u32[]{:S(2)}, u32[]{:S(2)}) %all-to-all-start) | async-done | bytes 3538976 | tf_op jit(solution)/shard_map/token_features/all_to_all | solution.py:36
  124.0 44.0 %all-to-all-done.3 = bf16[4,240,2048]{2,1,0:T(8,128)(2,1)} async-done(((bf16[4,240,2048]{2,1,0:T(8,128)(2,1)}), bf16[4,240,2048]{2,1,0:T(8,128)(2,1)}, u32[]{:S(2)}, u32[]{:S(2)}) %all-to-all-start.3) | async-done | bytes 3932192 | tf_op jit(solution)/shard_map/attention/all_to_all | solution.py:36
  174.1 15.7 %all_to_all.85 = bf16[4,240,512]{2,1,0:T(8,128)(2,1)S(1)} all-to-all(bf16[4,240,512]{2,1,0:T(8,128)(2,1)S(1)} %pad_maximum_fusion.23), channel_id=1, replica_groups=mesh['dp'=8,'mp'=4] {'mp'}, dimensions={0} | all-to-all | bytes 1966080 | tf_op jit(solution)/shard_map/cotangents/all_to_all | solution.py:36
  212.2 149.7 %all-to-all-done.4 = bf16[8,256,1024]{1,2,0:T(8,128)(2,1)} async-done(((bf16[8,256,1024]{1,2,0:T(8,128)(2,1)}), bf16[8,256,1024]{1,2,0:T(8,128)(2,1)}, u32[]{:S(2)}, u32[]{:S(2)}) %all-to-all-start.4) | async-done | bytes 4194336 | tf_op jit(solution)/shard_map/unit_weights/all_to_all | solution.py:36
  375.0 87.6 %all-to-all-done.5 = bf16[8,256,512]{1,2,0:T(8,128)(2,1)S(1)} async-done(((bf16[8,256,512]{1,2,0:T(8,128)(2,1)}), bf16[8,256,512]{1,2,0:T(8,128)(2,1)S(1)}, u32[]{:S(2)}, u32[]{:S(2)}) %all-to-all-start.5) | async-done | bytes 2097184 | tf_op jit(solution)/shard_map/unit_weights/all_to_all | solution.py:36
  473.4 38.3 %collective-permute-done.3 = bf16[2048,512]{1,0:T(8,128)(2,1)} collective-permute-done((bf16[2048,512]{1,0:T(8,128)(2,1)}, bf16[2048,512]{1,0:T(8,128)(2,1)}, u32[]{:S(2)}, u32[]{:S(2)}) %collective-permute-start.3) | collective-permute-done | bytes 2097184 | tf_op jit(solution)/shard_map/unit_weights/ppermute | solution.py:32
  526.9 13.4 collective-permute-done.6
  553.1 29.0 %collective-permute-done.4 = bf16[1024,1024]{1,0:T(8,128)(2,1)} collective-permute-done((bf16[1024,1024]{1,0:T(8,128)(2,1)}, bf16[1024,1024]{1,0:T(8,128)(2,1)}, u32[]{:S(2)}, u32[]{:S(2)}) %collective-permute-start.4) | collective-permute-done | bytes 2097184 | tf_op jit(solution)/shard_map/unit_weights/ppermute | solution.py:32
  588.7 13.6 fusion.160
  602.3 12.1 fusion.18
  614.4 12.5 fusion.48
  626.9 12.3 fusion.162
  639.1 12.2 fusion.164
  651.4 12.4 fusion.166
  663.7 11.7 fusion.25
  675.4 9.9 fusion.32
  685.3 14.2 fusion.47
  699.5 12.1 fusion.46
  711.6 11.0 fusion.39
  724.4 20.1 %add_convert_fusion = bf16[1664,2048]{1,0:T(8,128)(2,1)} fusion(f32[1664,2048]{1,0:T(8,128)} %fusion.46, f32[1664,2048]{1,0:T(8,128)} %fusion.48, f32[1664,2048]{1,0:T(8,128)} %fusion.47, bf16[2048,1024]{1,0:T(8,128)(2,1)} %constant_dynamic-update-slice_fusion, bf16[1664,512]{0,1:T(8,128)(2,1)S(1)} %get-tuple-element.33, ...), kind=kOutput, calls=%fused_computation | convolution fusion | flops 6999769088 | bytes 55312384 | tf_op jit(solution)/shard_map/geglu/dot_general | solution.py:24
  809.7 19.5 %add_convert_fusion.1 = bf16[1664,2048]{1,0:T(8,128)(2,1)} fusion(f32[1664,2048]{1,0:T(8,128)} %fusion.165, f32[1664,2048]{1,0:T(8,128)} %fusion.161, f32[1664,2048]{1,0:T(8,128)} %fusion.163, bf16[1664,512]{0,1:T(8,128)(2,1)S(1)} %copy-done.39, bf16[2048,512]{1,0:T(8,128)(2,1)} %constant_dynamic-update-slice_fusion.2), kind=kOutput, calls=%fused_computation.1 | convolution fusion | flops 3503292416 | bytes 51511296 | tf_op jit(solution)/shard_map/geglu/dot_general | solution.py:24
  863.6 10.6 convolution_convert_fusion.2
  894.3 52.2 %all-to-all-done.10 = bf16[4,208,2048]{2,1,0:T(8,128)(2,1)} async-done(((bf16[4,208,2048]{2,1,0:T(8,128)(2,1)}), bf16[4,208,2048]{2,1,0:T(8,128)(2,1)}, u32[]{:S(2)}, u32[]{:S(2)}) %all-to-all-start.10) | async-done | bytes 3407904 | tf_op jit(solution)/shard_map/middle_norm/all_to_all | solution.py:36
  984.4 85.4 %all-to-all-done.11 = bf16[4,896,128]{2,1,0:T(8,128)(2,1)S(1)} async-done(((bf16[4,896,128]{2,1,0:T(8,128)(2,1)}), bf16[4,896,128]{2,1,0:T(8,128)(2,1)S(1)}, u32[]{:S(2)}, u32[]{:S(2)}) %all-to-all-start.11) | async-done | bytes 917536 | tf_op jit(solution)/shard_map/attention_back/all_to_all | solution.py:36
  1074.6 11.5 convolution_convert_fusion.1
  1117.3 19.7 %all-to-all-done.15 = bf16[8,256,512]{2,1,0:T(8,128)(2,1)} async-done(((bf16[8,256,512]{2,1,0:T(8,128)(2,1)}), bf16[8,256,512]{2,1,0:T(8,128)(2,1)}, u32[]{:S(2)}, u32[]{:S(2)}) %all-to-all-start.15) | async-done | bytes 2097184 | tf_op jit(solution)/shard_map/geglu/all_to_all | solution.py:36
  1142.1 11.1 convert_convert_fusion
  1153.2 49.1 %collective-permute-done.10 = bf16[1024,1024]{1,0:T(8,128)(2,1)} collective-permute-done((bf16[1024,1024]{1,0:T(8,128)(2,1)}, bf16[1024,1024]{1,0:T(8,128)(2,1)}, u32[]{:S(2)}, u32[]{:S(2)}) %collective-permute-start.10) | collective-permute-done | bytes 2097184 | tf_op jit(solution)/shard_map/geglu/ppermute | solution.py:32
  1209.5 13.4 all-to-all-done.12
  1264.1 94.7 %all-to-all-done.14 = bf16[8,256,1024]{2,1,0:T(8,128)(2,1)} async-done(((bf16[8,256,1024]{2,1,0:T(8,128)(2,1)}), bf16[8,256,1024]{2,1,0:T(8,128)(2,1)}, u32[]{:S(2)}, u32[]{:S(2)}) %all-to-all-start.14) | async-done | bytes 4194336 | tf_op jit(solution)/shard_map/geglu/all_to_all | solution.py:36
  1371.8 38.5 %psum.7 = f32[6144]{0:T(1024)S(1)} all-reduce(f32[6144]{0:T(1024)S(1)} %pad_maximum_fusion.35), channel_id=1, replica_groups=mesh['dp'=8,'mp'=4] {'dp','mp'}, use_global_device_ids=true, to_apply=%region_25.26 | all-reduce | flops 6144 | bytes 49152 | tf_op jit(solution)/shard_map/gain_grads/psum | solution.py:373
  (555 shorter events, 454.1 us)
Async XLA Ops:
  7.2 69.8 %all-gather.8.cloned.1.call-start = ((), (), s32[]{:S(2)}) async-start(), calls=%async_computation.22 | async-start | bytes 2949120 | tf_op jit(solution)/shard_map/attention_weights/all_gather | solution.py:181
  26.1 80.3 %all-gather.18.cloned.1.call-start = ((), (), s32[]{:S(2)}) async-start(), calls=%async_computation.31 | async-start | bytes 4718592 | tf_op jit(solution)/shard_map/attention_weights/all_gather | solution.py:185
  123.9 422.5 %all-gather.12.cloned.1.call-start = ((), (), s32[]{:S(2)}) async-start(), calls=%async_computation.25 | async-start | bytes 1179648 | tf_op jit(solution)/shard_map/attention/all_gather | solution.py:279
  172.7 375.4 %all-gather.14.cloned.1.call-start = ((), (), s32[]{:S(2)}) async-start(), calls=%async_computation.26 | async-start | bytes 1179648 | tf_op jit(solution)/shard_map/cotangents/all_gather | solution.py:229
  190.7 398.0 %all-gather.10.cloned.1.call-start = ((), (), s32[]{:S(2)}) async-start(), calls=%async_computation.23 | async-start | bytes 7667712 | tf_op jit(solution)/shard_map/attention/all_gather | solution.py:278
  206.1 155.7 %all-to-all-start.4 = ((bf16[8,256,1024]{1,2,0:T(8,128)(2,1)}), bf16[8,256,1024]{1,2,0:T(8,128)(2,1)}, u32[]{:S(2)}, u32[]{:S(2)}) async-start(bf16[8,256,1024]{1,2,0:T(8,128)(2,1)} %pad_maximum_fusion), calls=%async_computation.4 | async-start | bytes 8388608 | tf_op jit(solution)/shard_map/unit_weights/all_to_all | solution.py:36
  211.0 391.3 %all-gather.16.cloned.1.call-start = ((), (), s32[]{:S(2)}) async-start(), calls=%async_computation.28 | async-start | bytes 7667712 | tf_op jit(solution)/shard_map/cotangents/all_gather | solution.py:228
  361.8 100.8 %all-to-all-start.5 = ((bf16[8,256,512]{1,2,0:T(8,128)(2,1)}), bf16[8,256,512]{1,2,0:T(8,128)(2,1)S(1)}, u32[]{:S(2)}, u32[]{:S(2)}) async-start(bf16[8,256,512]{1,2,0:T(8,128)(2,1)} %bitcast.420), calls=%async_computation.5 | async-start | bytes 4194304 | tf_op jit(solution)/shard_map/unit_weights/all_to_all | solution.py:36
  372.1 147.0 %collective-permute-start.2 = (bf16[2048,1024]{1,0:T(8,128)(2,1)}, bf16[2048,1024]{1,0:T(8,128)(2,1)}, u32[]{:S(2)}, u32[]{:S(2)}) collective-permute-start(bf16[2048,1024]{1,0:T(8,128)(2,1)} %bitcast.399), channel_id=1, source_target_pairs={{0,2},{1,3},{2,0},{3,1},{4,6},{5,7},{6,4},{7,5},{8,10},{9,11},{10,... | collective-permute-start | bytes 12582920 | tf_op jit(solution)/shard_map/unit_weights/ppermute | solution.py:32
  373.5 149.3 %collective-permute-start = (bf16[2048,1024]{1,0:T(8,128)(2,1)}, bf16[2048,1024]{1,0:T(8,128)(2,1)}, u32[]{:S(2)}, u32[]{:S(2)}) collective-permute-start(bf16[2048,1024]{1,0:T(8,128)(2,1)} %bitcast.400), channel_id=1, source_target_pairs={{0,1},{1,0},{2,3},{3,2},{4,5},{5,4},{6,7},{7,6},{8,9},{9,8},{10,11... | collective-permute-start | bytes 12582920 | tf_op jit(solution)/shard_map/unit_weights/ppermute | solution.py:32
  473.4 271.9 %reduce-scatter.10.cloned.1.call-start = ((), (), s32[]{:S(2)}) async-start(), calls=%async_computation.27 | async-start | bytes 2359296 | tf_op jit(solution)/shard_map/geglu/reduce_scatter | solution.py:303
  552.7 299.8 %reduce-scatter.12.cloned.1.call-start = ((), (), s32[]{:S(2)}) async-start(), calls=%async_computation.29 | async-start | bytes 7667712 | tf_op jit(solution)/shard_map/geglu/reduce_scatter | solution.py:290
  751.0 508.0 %reduce-scatter.8.cloned.1.call-start = ((), (), s32[]{:S(2)}) async-start(), calls=%async_computation.24 | async-start | bytes 7667712 | tf_op jit(solution)/shard_map/geglu/reduce_scatter | solution.py:294
  774.8 110.8 %collective-permute-start.17 = (bf16[1024,512]{1,0:T(8,128)(2,1)}, bf16[1024,512]{1,0:T(8,128)(2,1)}, u32[]{:S(2)}, u32[]{:S(2)}) collective-permute-start(bf16[1024,512]{1,0:T(8,128)(2,1)} %get-tuple-element.55), channel_id=1, source_target_pairs={{0,2},{1,3},{2,0},{3,1},{4,6},{5,7},{6,4},{7,5},{8,10},{9,11},{10,... | collective-permute-start | bytes 3145736 | tf_op jit(solution)/shard_map/geglu/ppermute | solution.py:32
  776.2 114.1 %collective-permute-start.15 = (bf16[1024,512]{1,0:T(8,128)(2,1)}, bf16[1024,512]{1,0:T(8,128)(2,1)}, u32[]{:S(2)}, u32[]{:S(2)}) collective-permute-start(bf16[1024,512]{1,0:T(8,128)(2,1)} %get-tuple-element.54), channel_id=1, source_target_pairs={{0,1},{1,0},{2,3},{3,2},{4,5},{5,4},{6,7},{7,6},{8,9},{9,8},{10,11... | collective-permute-start | bytes 3145736 | tf_op jit(solution)/shard_map/geglu/ppermute | solution.py:32
  783.7 183.1 %collective-permute-start.14 = (bf16[1024,512]{1,0:T(8,128)(2,1)}, bf16[1024,512]{1,0:T(8,128)(2,1)}, u32[]{:S(2)}, u32[]{:S(2)}) collective-permute-start(bf16[1024,512]{1,0:T(8,128)(2,1)} %slice.390), channel_id=1, source_target_pairs={{0,1},{1,0},{2,3},{3,2},{4,5},{5,4},{6,7},{7,6},{8,9},{9,8},{10,11... | collective-permute-start | bytes 3145736 | tf_op jit(solution)/shard_map/geglu/ppermute | solution.py:32
  838.6 128.6 %collective-permute-start.19 = (bf16[1024,512]{1,0:T(8,128)(2,1)}, bf16[1024,512]{1,0:T(8,128)(2,1)}, u32[]{:S(2)}, u32[]{:S(2)}) collective-permute-start(bf16[1024,512]{1,0:T(8,128)(2,1)} %slice.396), channel_id=1, source_target_pairs={{0,2},{1,3},{2,0},{3,1},{4,6},{5,7},{6,4},{7,5},{8,10},{9,11},{10,... | collective-permute-start | bytes 3145736 | tf_op jit(solution)/shard_map/geglu/ppermute | solution.py:32
  850.9 237.1 %collective-permute-start.11 = (bf16[1024,1024]{1,0:T(8,128)(2,1)}, bf16[1024,1024]{1,0:T(8,128)(2,1)}, u32[]{:S(2)}, u32[]{:S(2)}) collective-permute-start(bf16[1024,1024]{1,0:T(8,128)(2,1)} %get-tuple-element.51), channel_id=1, source_target_pairs={{0,2},{1,3},{2,0},{3,1},{4,6},{5,7},{6,4},{7,5},{8,10},{9,11},{10,... | collective-permute-start | bytes 6291464 | tf_op jit(solution)/shard_map/geglu/ppermute | solution.py:32
  858.7 87.7 %all-to-all-start.10 = ((bf16[4,208,2048]{2,1,0:T(8,128)(2,1)}), bf16[4,208,2048]{2,1,0:T(8,128)(2,1)}, u32[]{:S(2)}, u32[]{:S(2)}) async-start(bf16[4,208,2048]{2,1,0:T(8,128)(2,1)} %broadcast_in_dim.113), calls=%async_computation.13 | async-start | bytes 6815744 | tf_op jit(solution)/shard_map/middle_norm/all_to_all | solution.py:36
  888.3 90.3 %collective-permute-start.18 = (bf16[1024,512]{1,0:T(8,128)(2,1)}, bf16[1024,512]{1,0:T(8,128)(2,1)}, u32[]{:S(2)}, u32[]{:S(2)}) collective-permute-start(bf16[1024,512]{1,0:T(8,128)(2,1)} %add_convert_fusion.4), channel_id=1, source_target_pairs={{0,1},{1,0},{2,3},{3,2},{4,5},{5,4},{6,7},{7,6},{8,9},{9,8},{10,11... | collective-permute-start | bytes 3145736 | tf_op jit(solution)/shard_map/geglu/ppermute | solution.py:32
  892.8 85.8 %collective-permute-start.16 = (bf16[1024,512]{1,0:T(8,128)(2,1)}, bf16[1024,512]{1,0:T(8,128)(2,1)}, u32[]{:S(2)}, u32[]{:S(2)}) collective-permute-start(bf16[1024,512]{1,0:T(8,128)(2,1)} %add_convert_fusion.5), channel_id=1, source_target_pairs={{0,2},{1,3},{2,0},{3,1},{4,6},{5,7},{6,4},{7,5},{8,10},{9,11},{10,... | collective-permute-start | bytes 3145736 | tf_op jit(solution)/shard_map/geglu/ppermute | solution.py:32
  966.8 127.4 %collective-permute-start.9 = (bf16[1024,1024]{1,0:T(8,128)(2,1)}, bf16[1024,1024]{1,0:T(8,128)(2,1)}, u32[]{:S(2)}, u32[]{:S(2)}) collective-permute-start(bf16[1024,1024]{1,0:T(8,128)(2,1)} %get-tuple-element.50), channel_id=1, source_target_pairs={{0,1},{1,0},{2,3},{3,2},{4,5},{5,4},{6,7},{7,6},{8,9},{9,8},{10,11... | collective-permute-start | bytes 6291464 | tf_op jit(solution)/shard_map/geglu/ppermute | solution.py:32
  967.1 186.1 %collective-permute-start.8 = (bf16[1024,1024]{1,0:T(8,128)(2,1)}, bf16[1024,1024]{1,0:T(8,128)(2,1)}, u32[]{:S(2)}, u32[]{:S(2)}) collective-permute-start(bf16[1024,1024]{1,0:T(8,128)(2,1)} %slice.380), channel_id=1, source_target_pairs={{0,1},{1,0},{2,3},{3,2},{4,5},{5,4},{6,7},{7,6},{8,9},{9,8},{10,11... | collective-permute-start | bytes 6291464 | tf_op jit(solution)/shard_map/geglu/ppermute | solution.py:32
  975.1 94.7 %all-to-all-start.11 = ((bf16[4,896,128]{2,1,0:T(8,128)(2,1)}), bf16[4,896,128]{2,1,0:T(8,128)(2,1)S(1)}, u32[]{:S(2)}, u32[]{:S(2)}) async-start(bf16[4,896,128]{2,1,0:T(8,128)(2,1)} %maximum_bitcast_fusion), calls=%async_computation.14 | async-start | bytes 1835008 | tf_op jit(solution)/shard_map/attention_back/all_to_all | solution.py:36
  1069.8 67.3 %all-to-all-start.15 = ((bf16[8,256,512]{2,1,0:T(8,128)(2,1)}), bf16[8,256,512]{2,1,0:T(8,128)(2,1)}, u32[]{:S(2)}, u32[]{:S(2)}) async-start(bf16[8,256,512]{2,1,0:T(8,128)(2,1)} %bitcast.384), calls=%async_computation.19 | async-start | bytes 4194304 | tf_op jit(solution)/shard_map/geglu/all_to_all | solution.py:36
  1074.5 351.8 %reduce-scatter.16.cloned.1.call-start = ((), (), s32[]{:S(2)}) async-start(), calls=%async_computation.32 | async-start | bytes 3538944
  1087.5 65.7 %collective-permute-start.13 = (bf16[1024,1024]{1,0:T(8,128)(2,1)}, bf16[1024,1024]{1,0:T(8,128)(2,1)}, u32[]{:S(2)}, u32[]{:S(2)}) collective-permute-start(bf16[1024,1024]{1,0:T(8,128)(2,1)} %slice.386), channel_id=1, source_target_pairs={{0,2},{1,3},{2,0},{3,1},{4,6},{5,7},{6,4},{7,5},{8,10},{9,11},{10,... | collective-permute-start | bytes 6291464 | tf_op jit(solution)/shard_map/geglu/ppermute | solution.py:32
  1092.9 60.3 %collective-permute-start.12 = (bf16[1024,1024]{1,0:T(8,128)(2,1)}, bf16[1024,1024]{1,0:T(8,128)(2,1)}, u32[]{:S(2)}, u32[]{:S(2)}) collective-permute-start(bf16[1024,1024]{1,0:T(8,128)(2,1)} %add_convert_fusion.2), channel_id=1, source_target_pairs={{0,1},{1,0},{2,3},{3,2},{4,5},{5,4},{6,7},{7,6},{8,9},{9,8},{10,11... | collective-permute-start | bytes 6291464 | tf_op jit(solution)/shard_map/geglu/ppermute | solution.py:32
  1098.1 104.2 %collective-permute-start.10 = (bf16[1024,1024]{1,0:T(8,128)(2,1)}, bf16[1024,1024]{1,0:T(8,128)(2,1)}, u32[]{:S(2)}, u32[]{:S(2)}) collective-permute-start(bf16[1024,1024]{1,0:T(8,128)(2,1)} %add_convert_fusion.3), channel_id=1, source_target_pairs={{0,2},{1,3},{2,0},{3,1},{4,6},{5,7},{6,4},{7,5},{8,10},{9,11},{10,... | collective-permute-start | bytes 6291464 | tf_op jit(solution)/shard_map/geglu/ppermute | solution.py:32
  1137.1 85.8 %all-to-all-start.12 = ((bf16[4,240,2048]{2,1,0:T(8,128)(2,1)}), bf16[4,240,2048]{2,1,0:T(8,128)(2,1)}, u32[]{:S(2)}, u32[]{:S(2)}) async-start(bf16[4,240,2048]{2,1,0:T(8,128)(2,1)} %pad_maximum_fusion.3), calls=%async_computation.15 | async-start | bytes 7864320 | tf_op jit(solution)/shard_map/attention_back/all_to_all | solution.py:36
  1222.9 135.9 %all-to-all-start.14 = ((bf16[8,256,1024]{2,1,0:T(8,128)(2,1)}), bf16[8,256,1024]{2,1,0:T(8,128)(2,1)}, u32[]{:S(2)}, u32[]{:S(2)}) async-start(bf16[8,256,1024]{2,1,0:T(8,128)(2,1)} %bitcast.376), calls=%async_computation.18 | async-start | bytes 8388608 | tf_op jit(solution)/shard_map/geglu/all_to_all | solution.py:36
  1227.8 201.3 %reduce-scatter.14.cloned.1.call-start = ((), (), s32[]{:S(2)}) async-start(), calls=%async_computation.30 | async-start | bytes 4423680 | tf_op jit(solution)/shard_map/attention_weight_grads/reduce_scatter | solution.py:368
  (143 other events, 1767.6 us)
Sparse Core Ops, SparseCore 0:
  10.2 38.6 all-gather.7
  51.1 46.1 all-gather.17
  172.8 22.3 all-gather.11
  197.3 23.8 all-gather.13
  222.7 138.7 all-gather.9
  362.9 107.8 all-gather.15
  552.8 36.4 reduce-scatter.9
  744.7 77.4 reduce-scatter.11
  829.4 77.3 reduce-scatter.7
  1105.2 46.7 reduce-scatter.15
  1237.7 101.6 reduce-scatter.13

commit v2 on v1

v2 whole, which is shorter than its diff:
```python
import functools

import jax
import jax.numpy as jnp
from jax import lax
from jax.experimental import pallas as pl
from jax.experimental.pallas import tpu as pltpu
from jax.sharding import PartitionSpec as P

HD = 256
IMG = 256
CAMS = 3
EPSILON = 1e-06
MASKED = -1e30
BF = jnp.bfloat16
F32 = jnp.float32
SLOPE = 0.7978845608028654
CUBE = 0.044715
VMEM = 56 * 2**20
BRIEF = pl.CostEstimate(flops=1, bytes_accessed=1, transcendentals=0)


def dot(a, b, over_a, over_b):
    return lax.dot_general(a, b, (((over_a,), (over_b,)), ((), ())), preferred_element_type=F32)


def mm(a, b):
    return dot(a, b, 1, 0)


def mm_tn(a, b):
    return dot(a, b, 0, 0)


def mm_nt(a, b):
    return dot(a, b, 1, 1)


def gelu_parts(gate, up, grad_hidden):
    square = gate * gate
    tanh = jnp.tanh(SLOPE * gate * (1.0 + CUBE * square))
    half = 0.5 * (1.0 + tanh)
    act = gate * half
    slope = half + 0.5 * gate * (1.0 - tanh * tanh) * (SLOPE * (1.0 + 3.0 * CUBE * square))
    return act * up, grad_hidden * up * slope, grad_hidden * act


def geglu_kernel(n_ref, g_ref, gate_up_ref, down_ref, hidden_ref, grad_ref):
    units = down_ref.shape[1]
    rows = n_ref.shape[0] * n_ref.shape[1]
    width = n_ref.shape[2]
    both = mm(n_ref[...].reshape(rows, width), gate_up_ref[...])
    grad_hidden = mm(g_ref[...].reshape(rows, width), down_ref[...])
    hidden, grad_gate, grad_up = gelu_parts(both[:, :units], both[:, units:], grad_hidden)
    hidden_ref[...] = hidden.astype(BF)
    grad_ref[:, :units] = grad_gate.astype(BF)
    grad_ref[:, units:] = grad_up.astype(BF)


def geglu(normed, cots, weights, block, step=2):
    n, _, width = normed.shape
    units = weights.shape[1] // 3
    rows = step * block
    return pl.pallas_call(
        geglu_kernel,
        grid=(n // step,),
        in_specs=[
            pl.BlockSpec((step, block, width), lambda i: (i, 0, 0)),
            pl.BlockSpec((step, block, width), lambda i: (i, 0, 0)),
            pl.BlockSpec((width, 2 * units), lambda i: (0, 0)),
            pl.BlockSpec((width, units), lambda i: (0, 2)),
        ],
        out_specs=[
            pl.BlockSpec((rows, units), lambda i: (i, 0)),
            pl.BlockSpec((rows, 2 * units), lambda i: (i, 0)),
        ],
        out_shape=[
            jax.ShapeDtypeStruct((n * block, units), BF),
            jax.ShapeDtypeStruct((n * block, 2 * units), BF),
        ],
        compiler_params=pltpu.CompilerParams(vmem_limit_bytes=VMEM),
        cost_estimate=BRIEF,
        name="geglu",
    )(normed, cots, weights, weights)


def contract_kernel(count, *refs):
    out = refs[-1]
    total = mm_nt(refs[0][...], refs[count][...])
    for s in range(1, count):
        total += mm_nt(refs[s][...], refs[count + s][...])
    if len(refs) > 2 * count + 1:
        total += refs[2 * count][...]
    out[...] = total.astype(out.dtype)


def contract(parts, weights, column, tile, cols, base=None, kind=BF):
    count, rows = len(parts), parts[0].shape[0]
    width = weights[0].shape[0]
    bases = [] if base is None else [base]
    return pl.pallas_call(
        functools.partial(contract_kernel, count),
        grid=(width // cols, rows // tile),
        in_specs=[pl.BlockSpec((tile, part.shape[1]), lambda j, i: (i, 0)) for part in parts]
        + [pl.BlockSpec((cols, part.shape[1]), lambda j, i: (j, column)) for part in parts]
        + [pl.BlockSpec((tile, cols), lambda j, i: (i, j))] * len(bases),
        out_specs=pl.BlockSpec((tile, cols), lambda j, i: (i, j)),
        out_shape=jax.ShapeDtypeStruct((rows, width), kind),
        compiler_params=pltpu.CompilerParams(vmem_limit_bytes=VMEM),
        cost_estimate=BRIEF,
        name="contract",
    )(*parts, *weights, *bases)


def weight_grad_kernel(n_ref, g_ref, grad_ref, hidden_ref, out_ref):
    rows, cols = n_ref.shape[0] * n_ref.shape[1], n_ref.shape[2]
    units = hidden_ref.shape[1]
    out_ref[:, : 2 * units] = mm_tn(n_ref[...].reshape(rows, cols), grad_ref[...]).astype(BF)
    out_ref[:, 2 * units :] = mm_tn(g_ref[...].reshape(rows, cols), hidden_ref[...]).astype(BF)


def weight_grad(normed, cots, grad, hidden, block, cols=512):
    n, _, width = normed.shape
    units = hidden.shape[1]
    rows = n * block
    return pl.pallas_call(
        weight_grad_kernel,
        grid=(width // cols,),
        in_specs=[
            pl.BlockSpec((n, block, cols), lambda i: (0, 0, i)),
            pl.BlockSpec((n, block, cols), lambda i: (0, 0, i)),
            pl.BlockSpec((rows, 2 * units), lambda i: (0, 0)),
            pl.BlockSpec((rows, units), lambda i: (0, 0)),
        ],
        out_specs=pl.BlockSpec((cols, 3 * units), lambda i: (i, 0)),
        out_shape=jax.ShapeDtypeStruct((width, 3 * units), BF),
        compiler_params=pltpu.CompilerParams(vmem_limit_bytes=VMEM),
        cost_estimate=BRIEF,
        name="weight_grad",
    )(normed, cots, grad, hidden)


def pad_rows(a, rows):
    return jnp.pad(a, ((0, rows - a.shape[0]), (0, 0)))


def swap(a, axis, size, step):
    return lax.ppermute(a, axis, [(i, i ^ step) for i in range(size)])


def exchange(a):
    return lax.all_to_all(a, "dp", 0, 0, tiled=True)


def everyones(a, k):
    return [a] + [swap(a, "mp", k, s) for s in range(1, k)]


def placed(parts, mine, axis):
    size = parts[0].shape[axis]
    shape = list(parts[0].shape)
    shape[axis] *= len(parts)
    whole = jnp.zeros(shape, parts[0].dtype)
    for s, part in enumerate(parts):
        whole = lax.dynamic_update_slice_in_dim(whole, part, (mine ^ s) * size, axis)
    return whole


def handed(a, mine, k, axis):
    size = a.shape[axis] // k
    cut = [lax.dynamic_slice_in_dim(a, (mine ^ s) * size, size, axis) for s in range(k)]
    return [cut[0]] + [swap(cut[s], "mp", k, s) for s in range(1, k)]


def total(parts):
    return sum(part.astype(F32) for part in parts)


def butterfly_sum(a, n):
    step = 1
    while step < n:
        a = a + swap(a, "dp", n, step)
        step *= 2
    return a


class Halving:
    def __init__(self, a, n, me):
        self.a, self.n, self.me, self.step = a, n, me, 1
        self.send()

    def send(self):
        if self.step == self.n:
            return
        a = self.a
        pairs = a.reshape((a.shape[0] // 2, 2) + a.shape[1:])
        bit = (self.me // self.step) % 2
        self.keep = lax.dynamic_index_in_dim(pairs, bit, 1, keepdims=False)
        send = lax.dynamic_index_in_dim(pairs, 1 - bit, 1, keepdims=False)
        self.got = swap(send, "dp", self.n, self.step)

    def take(self, order):
        if self.step == self.n:
            return
        self.a = (self.keep.astype(F32) + order(self.got).astype(F32)).astype(BF)
        self.step *= 2
        self.send()

    def result(self, order):
        while self.step < self.n:
            self.take(order)
        return self.a[0]


class Spread:
    def __init__(self, block, k):
        self.k = k
        if k == 4:
            self.blocks = [block, swap(block, "mp", k, 1), swap(block, "mp", k, 2)]
        else:
            self.blocks = everyones(block, k)

    def arrive(self, order):
        self.blocks[1:] = order(*self.blocks[1:])
        if self.k == 4:
            half = self.blocks[0].shape[0] // 2
            self.low = swap(self.blocks[2][:half], "mp", 4, 1)
            self.high = swap(self.blocks[1][half:], "mp", 4, 2)

    def last(self, order):
        if self.k == 4:
            self.blocks.append(order(jnp.concatenate(order(self.low, self.high), axis=0)))


class Collect:
    def __init__(self, k):
        self.k, self.parts, self.got = k, {}, {}

    def put(self, s, part):
        self.parts[s] = part
        half = part.shape[0] // 2
        if self.k != 4:
            if s:
                self.got[s] = swap(part, "mp", self.k, s)
        elif s == 3:
            self.low = swap(part[:half], "mp", 4, 1)
            self.high = swap(part[half:], "mp", 4, 2)
        elif s == 1:
            self.got["first_low"] = swap(part[:half], "mp", 4, 1)
        elif s == 2:
            self.got["second_high"] = swap(part[half:], "mp", 4, 2)

    def receive(self, order, *names):
        for name in names:
            if name in self.got:
                self.got[name] = order(self.got[name])

    def far(self, order):
        if self.k == 4:
            self.low, self.high = order(self.low, self.high)

    def near(self, order):
        if self.k == 4:
            half = self.low.shape[0]
            low, high = order(
                total([self.parts[2][:half], self.low]).astype(BF),
                total([self.parts[1][half:], self.high]).astype(BF),
            )
            self.got["second_low"] = swap(low, "mp", 4, 2)
            self.got["first_high"] = swap(high, "mp", 4, 1)

    def result(self, order):
        own, got = self.parts[0], self.got
        if self.k != 4:
            return order(total([own, *order(*got.values())]).astype(BF))
        self.receive(order, "first_low", "second_high", "second_low", "first_high")
        half = self.low.shape[0]
        lower = total([own[:half], got["first_low"], got["second_low"]]).astype(BF)
        upper = total([own[half:], got["second_high"], got["first_high"]]).astype(BF)
        return order(jnp.concatenate([lower, upper], axis=0))


def inverse_rms(x):
    return lax.rsqrt(jnp.mean(x * x, axis=1, keepdims=True) + EPSILON)


def norm_back(grad, x, inv, gain):
    inner = jnp.sum(grad * gain * x, axis=1, keepdims=True)
    back = inv * gain * grad - x * inv**3 * inner / x.shape[1]
    return back, jnp.sum(grad * x * inv, axis=0)


def key_weights(queries, keys, cameras, texts, padded, tail):
    scores = mm_nt(queries, keys) * HD ** (-0.5)
    place = lax.broadcasted_iota(jnp.int32, scores.shape, 1)
    text = CAMS * IMG
    seen = (place < cameras * IMG) | ((place >= text) & (place < text + texts))
    if keys.shape[0] > padded:
        seen = seen | ((place >= padded) & (place < padded + tail))
    scores = jnp.where(seen, scores, MASKED)
    terms = jnp.exp(scores - jnp.max(scores, axis=1, keepdims=True))
    return terms / jnp.sum(terms, axis=1, keepdims=True)


def attend_kernel(padded, tail, cams_ref, texts_ref, q_ref, k_ref, v_ref, mixed_ref):
    weights = key_weights(q_ref[...], k_ref[...], cams_ref[0], texts_ref[0], padded, tail)
    mixed_ref[...] = mm(weights.astype(BF), v_ref[...]).astype(BF)


def attend(cameras, texts, queries, kv, heads, padded, tail, tiles):
    rows, keys = queries.shape[0], kv.shape[0]
    tile = rows // tiles
    return pl.pallas_call(
        functools.partial(attend_kernel, padded, tail),
        grid=(heads, tiles),
        in_specs=[
            pl.BlockSpec(memory_space=pltpu.SMEM),
            pl.BlockSpec(memory_space=pltpu.SMEM),
            pl.BlockSpec((tile, HD), lambda h, i: (i, h)),
            pl.BlockSpec((keys, HD), lambda h, i: (0, 0)),
            pl.BlockSpec((keys, HD), lambda h, i: (0, 1)),
        ],
        out_specs=pl.BlockSpec((tile, HD), lambda h, i: (i, h)),
        out_shape=jax.ShapeDtypeStruct((rows, heads * HD), BF),
        compiler_params=pltpu.CompilerParams(vmem_limit_bytes=VMEM),
        cost_estimate=BRIEF,
        name="attend",
    )(cameras, texts, queries, kv, kv)


def attend_back_kernel(
    padded, tail, cams_ref, texts_ref, q_ref, gm_ref, k_ref, v_ref, start_ref, gq_ref, gkv_ref, sum_ref
):
    first = (pl.program_id(0) == 0) & (pl.program_id(1) == 0)
    last = (pl.program_id(0) == pl.num_programs(0) - 1) & (
        pl.program_id(1) == pl.num_programs(1) - 1
    )
    keys = k_ref.shape[0]

    @pl.when(first)
    def _():
        sum_ref[...] = start_ref[...]

    queries, grad_mixed = q_ref[...], gm_ref[...]
    weights = key_weights(queries, k_ref[...], cams_ref[0], texts_ref[0], padded, tail)
    grad = mm_nt(grad_mixed, v_ref[...])
    inner = jnp.sum(weights * grad, axis=1, keepdims=True)
    grad = (weights * (grad - inner)).astype(BF)
    gq_ref[...] = (mm(grad, k_ref[...]) * HD ** (-0.5)).astype(BF)
    sum_ref[:keys, :HD] += mm_tn(grad, queries) * HD ** (-0.5)
    sum_ref[:keys, HD:] += mm_tn(weights.astype(BF), grad_mixed)

    @pl.when(last)
    def _():
        gkv_ref[...] = sum_ref[...].astype(gkv_ref.dtype)


def attend_back(cameras, texts, queries, grad_mixed, kv, start, kind, heads, padded, tail, tiles, keys):
    rows = queries.shape[0]
    tile = rows // tiles
    return pl.pallas_call(
        functools.partial(attend_back_kernel, padded, tail),
        grid=(heads, tiles),
        in_specs=[
            pl.BlockSpec(memory_space=pltpu.SMEM),
            pl.BlockSpec(memory_space=pltpu.SMEM),
            pl.BlockSpec((tile, HD), lambda h, i: (i, h)),
            pl.BlockSpec((tile, HD), lambda h, i: (i, h)),
            pl.BlockSpec((keys, HD), lambda h, i: (0, 0)),
            pl.BlockSpec((keys, HD), lambda h, i: (0, 1)),
            pl.BlockSpec(start.shape, lambda h, i: (0, 0)),
        ],
        out_specs=[
            pl.BlockSpec((tile, HD), lambda h, i: (i, h)),
            pl.BlockSpec(start.shape, lambda h, i: (0, 0)),
        ],
        out_shape=[
            jax.ShapeDtypeStruct((rows, heads * HD), BF),
            jax.ShapeDtypeStruct(start.shape, kind),
        ],
        scratch_shapes=[pltpu.VMEM(start.shape, F32)],
        compiler_params=pltpu.CompilerParams(vmem_limit_bytes=VMEM),
        cost_estimate=BRIEF,
        name="attend_back",
    )(cameras, texts, queries, grad_mixed, kv, kv, start)


def pair_grad_kernel(pre_ref, by_pre_ref, act_ref, by_act_ref, out_ref):
    depth = pre_ref.shape[1]
    out_ref[0, :depth] = mm_tn(pre_ref[...], by_pre_ref[...]).astype(BF)
    act = act_ref[...] if len(act_ref.shape) == 2 else act_ref[0]
    out_ref[0, depth:] = mm_tn(act, by_act_ref[...]).astype(BF)


def pair_grad(pre, by_pre, act, by_act, n):
    depth, adepth, cols = pre.shape[1] // n, act.shape[1] // n, by_pre.shape[1]
    act_spec = pl.BlockSpec((act.shape[0], adepth), lambda i: (0, i))
    if adepth % 128:
        act = act.reshape(-1, n, adepth).transpose(1, 0, 2)
        act_spec = pl.BlockSpec((1,) + act.shape[1:], lambda i: (i, 0, 0))
    return pl.pallas_call(
        pair_grad_kernel,
        grid=(n,),
        in_specs=[
            pl.BlockSpec((pre.shape[0], depth), lambda i: (0, i)),
            pl.BlockSpec(by_pre.shape, lambda i: (0, 0)),
            act_spec,
            pl.BlockSpec(by_act.shape, lambda i: (0, 0)),
        ],
        out_specs=pl.BlockSpec((1, depth + adepth, cols), lambda i: (i, 0, 0)),
        out_shape=jax.ShapeDtypeStruct((n, depth + adepth, cols), BF),
        compiler_params=pltpu.CompilerParams(vmem_limit_bytes=VMEM),
        cost_estimate=BRIEF,
        name="pair_grad",
    )(pre, by_pre, act, by_act)


def cuts_of(sizes):
    at = 0
    for size in sizes:
        yield slice(at, at + size)
        at += size


def pack_kernel(sizes, gate_ref, up_ref, down_ref, *outs):
    for units, cut, out in zip(sizes, cuts_of(sizes), outs):
        out[0, :, :units] = gate_ref[:, cut]
        out[0, :, units : 2 * units] = up_ref[:, cut]
        out[0, :, 2 * units :] = down_ref[cut, :].astype(F32).T.astype(BF)


def unit_blocks(gate, up, down, n, sizes):
    depth, block = gate.shape[0], gate.shape[1] // n
    if block % 128:
        return [
            jnp.concatenate(
                [
                    gate.reshape(depth, n, block).transpose(1, 0, 2),
                    up.reshape(depth, n, block).transpose(1, 0, 2),
                    down.reshape(n, block, depth).transpose(0, 2, 1),
                ],
                axis=2,
            )
        ]
    return pl.pallas_call(
        functools.partial(pack_kernel, sizes),
        grid=(n,),
        in_specs=[
            pl.BlockSpec((depth, block), lambda i: (0, i)),
            pl.BlockSpec((depth, block), lambda i: (0, i)),
            pl.BlockSpec((block, depth), lambda i: (i, 0)),
        ],
        out_specs=[pl.BlockSpec((1, depth, 3 * units), lambda i: (i, 0, 0)) for units in sizes],
        out_shape=[jax.ShapeDtypeStruct((n, depth, 3 * units), BF) for units in sizes],
        compiler_params=pltpu.CompilerParams(vmem_limit_bytes=VMEM),
        cost_estimate=BRIEF,
        name="pack",
    )(gate, up, down)


def beside(blocks, units):
    n, rows, cols = blocks.shape
    groups = 3 * units // cols
    each = -(-rows // (16 * groups)) * 16
    blocks = jnp.pad(blocks, ((0, 0), (0, each * groups - rows), (0, 0)))
    return jnp.concatenate(jnp.split(blocks, groups, axis=1), axis=2)


def apart(blocks, units, rows):
    groups = blocks.shape[2] // (3 * units)
    return jnp.concatenate(jnp.split(blocks, groups, axis=2), axis=1)[:, :rows]


def unpack_kernel(*refs):
    parts, (gate_ref, up_ref, down_ref) = refs[:-3], refs[-3:]
    sizes = [part.shape[2] // 3 for part in parts]
    for units, cut, part in zip(sizes, cuts_of(sizes), parts):
        gate_ref[:, cut] = part[0, :, :units].astype(F32)
        up_ref[:, cut] = part[0, :, units : 2 * units].astype(F32)
        down_ref[cut, :] = part[0, :, 2 * units :].astype(F32).T


def unblock(parts, depth=None):
    n = parts[0].shape[0]
    depth = depth or parts[0].shape[1]
    block = sum(part.shape[2] // 3 for part in parts)
    if block % 128:
        part = parts[0][:, :depth]
        gate = part[:, :, :block].transpose(1, 0, 2).reshape(depth, n * block)
        up = part[:, :, block : 2 * block].transpose(1, 0, 2).reshape(depth, n * block)
        down = part[:, :, 2 * block :].transpose(0, 2, 1).reshape(n * block, depth)
        return gate.astype(F32), up.astype(F32), down.astype(F32)
    return pl.pallas_call(
        unpack_kernel,
        grid=(n,),
        in_specs=[
            pl.BlockSpec((1, depth, part.shape[2]), lambda i: (i, 0, 0)) for part in parts
        ],
        out_specs=[
            pl.BlockSpec((depth, block), lambda i: (0, i)),
            pl.BlockSpec((depth, block), lambda i: (0, i)),
            pl.BlockSpec((block, depth), lambda i: (i, 0)),
        ],
        out_shape=[
            jax.ShapeDtypeStruct((depth, n * block), F32),
            jax.ShapeDtypeStruct((depth, n * block), F32),
            jax.ShapeDtypeStruct((n * block, depth), F32),
        ],
        compiler_params=pltpu.CompilerParams(vmem_limit_bytes=VMEM),
        cost_estimate=BRIEF,
        name="unpack",
    )(*parts)


class Order:
    def __init__(self):
        self.token = jnp.zeros((8, 128), F32)

    def __call__(self, *values):
        *values, self.token = lax.optimization_barrier(values + (self.token,))
        return values[0] if len(values) == 1 else tuple(values)


def solution(mesh):
    n, k = mesh.shape["dp"], mesh.shape["mp"]

    def per_device(
        prefix_tokens,
        action_tokens,
        camera_counts,
        text_lengths,
        prefix_attn_gain,
        prefix_query_proj,
        prefix_kv_proj,
        prefix_out_proj,
        prefix_ffn_gain,
        prefix_gate_proj,
        prefix_up_proj,
        prefix_down_proj,
        action_attn_gain,
        action_query_proj,
        action_kv_proj,
        action_out_proj,
        action_ffn_gain,
        action_gate_proj,
        action_up_proj,
        action_down_proj,
        prefix_cotangent,
        action_cotangent,
    ):
        mine, me = lax.axis_index("mp"), lax.axis_index("dp")
        rows, wide = prefix_tokens.shape
        arows, awide = action_tokens.shape
        block = -(-rows // (16 * k)) * 16
        padded = block * k
        apad = -(-arows // 64) * 64
        width, awidth = wide * k, awide * k
        fold = apad * awidth // width
        heads = prefix_query_proj.shape[1] // HD
        qcols = heads * HD
        kvcols = prefix_kv_proj.shape[1]
        depth, adepth = prefix_query_proj.shape[0], action_query_proj.shape[0]
        units = prefix_gate_proj.shape[1] // n
        sizes = [units // 2] * 2 if units % 256 == 0 else [units]
        pieces = len(sizes)

        order = Order()

        with jax.named_scope("token_features"):
            x_act = pad_rows(action_tokens, apad)
            x_all = jnp.concatenate(
                [pad_rows(prefix_tokens, padded), x_act.reshape(-1, wide)], axis=0
            )
            x_all = everyones(order(x_all), k)
            gains = jnp.concatenate(
                [prefix_attn_gain, prefix_ffn_gain, action_attn_gain, action_ffn_gain]
            )[None]
            gains = everyones(gains, k)

        with jax.named_scope("cotangents"):
            g_act = everyones(pad_rows(action_cotangent, apad), k)
            g_pre = handed(pad_rows(prefix_cotangent, padded), mine, k, 0)

        with jax.named_scope("attention_weights"):
            qkv_pre = jnp.concatenate([prefix_query_proj, prefix_kv_proj], axis=1)
            wqkv_pre = lax.all_gather(order(qkv_pre), "dp", axis=0, tiled=True)
            group = qcols // kvcols
            wout_pre = lax.all_gather(order(prefix_out_proj.T), "dp", axis=0, tiled=True)
            rest = jnp.concatenate(
                [action_out_proj.T, action_query_proj]
                + [jnp.concatenate(jnp.split(action_kv_proj, group, axis=0), axis=1)],
                axis=0,
            )

        with jax.named_scope("unit_weights"):
            packed = list(
                unit_blocks(prefix_gate_proj, prefix_up_proj, prefix_down_proj, n, sizes)
            )
            own = [exchange(order(packed[0])).reshape(width, 3 * sizes[0])]

        with jax.named_scope("token_features"):
            g_pre = placed(order(*g_pre), mine, 1)
            g_act = placed(order(*g_act), mine, 1)
            g_rows = order(jnp.concatenate([g_pre, g_act.reshape(fold, width)], axis=0))
            gall = lax.all_gather(g_rows, "dp", axis=0)
            gains = placed(order(*gains), mine, 0)
            gain_pre = gains[:, :wide].reshape(1, width)
            gain2_pre = gains[:, wide : 2 * wide].reshape(1, width)
            gain_act = gains[:, 2 * wide : 2 * wide + awide].reshape(1, awidth)
            gain2_act = gains[:, 2 * wide + awide :].reshape(1, awidth)
            x_all = order(*x_all)
            x_pre = order(placed([x[:padded] for x in x_all], mine, 1)).astype(F32)
            x_act = placed([x[padded:].reshape(apad, awide) for x in x_all], mine, 1).astype(F32)

        with jax.named_scope("attention"):
            inv_pre = inverse_rms(x_pre)
            normed_pre = order((x_pre * inv_pre * gain_pre).astype(BF))
            qkv_p = order(mm(normed_pre, order(wqkv_pre)).astype(BF))
            kv_p = everyones(qkv_p[:, qcols:], k)
            kv_p = placed(order(*kv_p), mine, 1)
            tiles = k
            mixed_pre = order(
                attend(camera_counts, text_lengths, qkv_p, kv_p, heads, padded, 0, tiles)
            )
            own[0] = order(own[0])
            branch_pre = order(mm_nt(mixed_pre, order(wout_pre)).astype(BF))
            branch_pre = handed(branch_pre, mine, k, 0)

            xrow_pre = lax.dynamic_slice_in_dim(x_pre, mine * block, block, 0)
            middle_pre = xrow_pre + total(order(*branch_pre))
            inv2_pre = inverse_rms(middle_pre)
            normed2_pre = order((middle_pre * inv2_pre * gain2_pre).astype(BF))
            nall = lax.all_gather(normed2_pre, "dp", axis=0)

            spread = [Spread(order(own[0]), k)]
            aunits = action_gate_proj.shape[1] // n
            [w_act] = unit_blocks(action_gate_proj, action_up_proj, action_down_proj, n, [aunits])
            w_act = exchange(order(w_act))
            rest = lax.all_gather(order(rest), "dp", axis=0)
            spread[0].arrive(order)

        with jax.named_scope("geglu"):
            w_act = order(w_act).reshape(awidth, 3 * aunits)
            gu_act, dt_act = w_act[:, : 2 * aunits], w_act[:, 2 * aunits :]
            gall, nall = order(gall, nall)
            if pieces == 2:
                own.append(exchange(order(packed[1])).reshape(width, 3 * sizes[1]))
            hiddens = [[None] * k for _ in range(pieces)]
            grads = [[None] * k for _ in range(pieces)]
            collects = [Collect(k) for _ in range(pieces)]
            outward = list(range(k - 1, -1, -1))

            def forward(c, s):
                hidden, grad = geglu(order(nall), gall, spread[c].blocks[s], block)
                hiddens[c][s], grads[c][s] = order(hidden, grad)

            def backward(c, s):
                part = weight_grad(order(nall), gall, grads[c][s], hiddens[c][s], block)
                return order(part)

            for s in range(k if k != 4 else 3):
                forward(0, s)
            spread[0].last(order)
            if k == 4:
                forward(0, 3)

            rest = order(rest)
            wout_act = rest[:, :adepth].reshape(n * adepth, qcols)
            wq_act = rest[:, adepth : 2 * adepth].reshape(n * adepth, qcols)
            wkv_act = jnp.concatenate(
                jnp.split(rest[:, 2 * adepth :], group, axis=2), axis=1
            ).reshape(n * adepth, kvcols)
            inv_act = inverse_rms(x_act)
            normed_act = (x_act * inv_act * gain_act).astype(BF)
            q_act, kv_a = order(mm(normed_act, wq_act).astype(BF), mm(normed_act, wkv_act).astype(BF))
            kv_a = everyones(kv_a, k)
            parts = [None] * k
            parts[1] = backward(0, 1)
            kv_a = placed(order(*kv_a), mine, 1)
            kv_all = order(jnp.concatenate([kv_p, kv_a], axis=0))
            mixed_act = order(
                attend(camera_counts, text_lengths, q_act, kv_all, heads, padded, arows, 1)
            )
            branch_act = everyones(order(mm_nt(mixed_act, wout_act).astype(BF)), k)
            parts[2] = backward(0, 2)
            middle_act = x_act + total(order(*branch_act))
            inv2_act = inverse_rms(middle_act)
            normed2_act = order((middle_act * inv2_act * gain2_act).astype(BF))
            nall_act = lax.all_gather(normed2_act, "dp", axis=0, tiled=True)
            if pieces == 2:
                own[1] = order(own[1])
                spread.append(Spread(own[1], k))
            parts[0] = backward(0, 0)
            if pieces == 2:
                forward(1, 0)

            gall_act = gall[:, block:].reshape(n * apad, awidth)
            both = mm(order(nall_act), gu_act)
            hidden, grad_gate, grad_up = gelu_parts(
                both[:, :aunits], both[:, aunits:], mm(gall_act, dt_act)
            )
            hidden = hidden.astype(BF)
            grad = jnp.concatenate([grad_gate, grad_up], axis=1).astype(BF)
            part = jnp.concatenate([mm_nt(hidden, dt_act), mm_nt(grad, gu_act)], axis=1).astype(BF)
            part = order(part)

            tile = n * block // 4
            gn2 = ffn = None
            if pieces == 2:
                gn2 = order(
                    contract([order(grads[0][0])] + grads[0][1:], spread[0].blocks, 0, tile, 1024, None, F32)
                )
                spread[1].arrive(order)
            halving = Halving(part.reshape(n, apad, 2 * awidth), n, me)
            for s in range(3, k):
                parts[s] = backward(0, s)
            for s in outward:
                collects[0].put(s, parts[s])
            halving.take(order)
            if pieces == 2:
                for s in range(1, k if k != 4 else 3):
                    forward(1, s)
                halving.take(order)
                spread[1].last(order)
                if k == 4:
                    forward(1, 3)
            halving.take(order)
            collects[0].far(order)
            part = halving.result(order)
            out_act = handed(part[:, :awidth], mine, k, 1)
            gn2_act = everyones(part[:, awidth:], k)
            last = pieces - 1
            gn2 = order(
                contract([order(grads[last][0])] + grads[last][1:], spread[last].blocks, 0, tile, 1024, gn2)
            )
            gn2 = lax.psum_scatter(gn2, "dp", scatter_dimension=0, tiled=True)
            collects[0].near(order)
            collects[0].receive(order, "first_low", "second_high")
            gn2_act, out_act = order(*gn2_act), order(*out_act)
            flat = [weights for piece in spread for weights in piece.blocks]
            flat_hiddens = [hidden for piece in hiddens for hidden in piece]
            ffn = order(contract([order(flat_hiddens[0])] + flat_hiddens[1:], flat, 2, tile, 1024))
            ffn = lax.psum_scatter(ffn, "dp", scatter_dimension=0, tiled=True)
            parts = {}
            if pieces == 2:
                parts = {s: backward(1, s) for s in outward}
            back = [collects[0].result(order).reshape(n, depth, 3 * sizes[0])]
            gw_act = jnp.concatenate([mm_tn(nall_act, grad), mm_tn(gall_act, hidden)], axis=1)
            gw_act = gw_act.astype(BF).reshape(n, adepth, 3 * aunits)
            back[0] = exchange(order(jnp.concatenate([back[0], beside(gw_act, sizes[0])], axis=1)))

        with jax.named_scope("middle_norm"):
            back2_pre, gg2_pre = norm_back(order(gn2).astype(F32), middle_pre, inv2_pre, gain2_pre)
            resid_pre = g_pre.astype(F32) + back2_pre
            gb_pre = everyones(order(resid_pre.astype(BF)), k)
            for s in parts:
                collects[1].put(s, order(parts[s]))

            gn2_act, out_act = total(gn2_act), total(out_act)
            output_act = (
                lax.dynamic_slice_in_dim(middle_act, mine * awide, awide, 1) + out_act
            )[:arows]
            back2_act, gg2_act = norm_back(order(gn2_act), middle_act, inv2_act, gain2_act)
            resid_act = g_act.astype(F32) + back2_act
            gb_act = resid_act.astype(BF)
            gm_act = order(mm(gb_act, wout_act).astype(BF))
            start = jnp.zeros((padded + apad, 2 * HD), F32)
            gq_act, start = order(
                *attend_back(
                    camera_counts, text_lengths, q_act, gm_act, kv_all, start, F32,
                    heads, padded, arows, 1, padded + apad,
                )
            )
            gb_pre = placed(order(*gb_pre), mine, 0)
            back[0] = order(back[0])
            if pieces == 2:
                collects[1].far(order)
                collects[1].near(order)

        with jax.named_scope("attention_back"):
            gm_pre = order(mm(gb_pre, wout_pre).astype(BF))
            gq_pre, gkv = order(
                *attend_back(
                    camera_counts, text_lengths, qkv_p, gm_pre, kv_p, start, BF,
                    heads, padded, 0, tiles, padded,
                )
            )
            gkv = handed(gkv, mine, k, 1)
            go = order(pair_grad(gb_pre, mixed_pre, gb_act, mixed_act, n)).reshape(-1, qcols)
            go = lax.psum_scatter(go, "dp", scatter_dimension=0, tiled=True)
            gkv = total(order(*gkv)).astype(BF)
            gqkv_pre = order(jnp.concatenate([gq_pre, gkv[:padded]], axis=1))
            gqkv_act = jnp.concatenate([gq_act, gkv[padded:]], axis=1)
            gn_pre = order(mm_nt(gqkv_pre, wqkv_pre).astype(BF))
            gn_pre = handed(gn_pre, mine, k, 0)
            gn_act = (mm_nt(gq_act, wq_act) + mm_nt(gkv[padded:], wkv_act)).astype(BF)
            gn_act = everyones(order(gn_act), k)

        with jax.named_scope("query_key_value_grads"):
            gw = order(pair_grad(order(normed_pre), gqkv_pre, normed_act, gqkv_act, n))
            gw = gw.reshape(-1, qcols + kvcols)
            gw = lax.psum_scatter(gw, "dp", scatter_dimension=0, tiled=True)
            if pieces == 2:
                back1 = collects[1].result(order).reshape(n, depth, 3 * sizes[1])
                back.append(exchange(order(back1)))

        with jax.named_scope("input_grads"):
            gn_pre = total(order(*gn_pre))
            invrow = lax.dynamic_slice_in_dim(inv_pre, mine * block, block, 0)
            back_pre, gg_pre = norm_back(gn_pre, xrow_pre, invrow, gain_pre)
            in_pre = order((resid_pre + back_pre).astype(BF))
            in_pre = handed(in_pre, mine, k, 1)
            out_pre = order((middle_pre + order(ffn).astype(F32)).astype(BF))
            out_pre = handed(out_pre, mine, k, 1)
            gn_act = total(order(*gn_act))
            back_act, gg_act = norm_back(gn_act, x_act, inv_act, gain_act)
            in_act = lax.dynamic_slice_in_dim(resid_act + back_act, mine * awide, awide, 1)[:arows]

        with jax.named_scope("gain_grads"):

            def gain_sum(pre, act):
                pre = sum(handed(jnp.stack(pre), mine, k, 1))
                act = lax.dynamic_slice_in_dim(jnp.stack(act), mine * awide, awide, 1)
                both = butterfly_sum(order(jnp.concatenate([pre, act], axis=1)), n)
                return both[0, :wide], both[1, :wide], both[0, wide:], both[1, wide:]

            gg_pre, gg2_pre, gg_act, gg2_act = gain_sum((gg_pre, gg2_pre), (gg_act, gg2_act))

        with jax.named_scope("unit_weight_grads"):
            gw_act = apart(back[0][:, depth:], aunits, adepth)
            gate_act, up_act, down_act = unblock([gw_act])
            in_pre = placed(order(*in_pre), mine, 0)[:rows].astype(F32)
            output_pre = placed(order(*out_pre), mine, 0)[:rows].astype(F32)
            go = order(go).astype(F32)
            gw = order(gw).astype(F32)
            if pieces == 2:
                back[1] = order(back[1])
            gate_pre, up_pre, down_pre = unblock(back, depth)
            gg_pre = gg_pre + order.token[0, 0]
        return (
            output_pre,
            output_act,
            in_pre,
            in_act,
            gg_pre,
            gw[:depth, :qcols],
            gw[:depth, qcols:],
            go[:depth].T,
            gg2_pre,
            gate_pre,
            up_pre,
            down_pre,
            gg_act,
            gw[depth:, :qcols],
            gw[depth:, qcols:],
            go[depth:].T,
            gg2_act,
            gate_act,
            up_act,
            down_act,
        )

    split, rowsplit, whole = P("dp", "mp"), P("mp", "dp"), P("mp")
    weights = (whole, split, split, rowsplit, whole, split, split, rowsplit)
    return jax.shard_map(
        per_device,
        mesh=mesh,
        in_specs=(split, split, P("dp"), P("dp")) + weights + weights + (split, split),
        out_specs=(split, split, split, split) + weights + weights,
        check_vma=False,
    )
```

time: 1450 us -> 1050 us (0.72)
  waiting for transfers between devices: 724 us -> 376 us
  Pallas kernels: 0 us -> 317 us
  matrix products: 325 us -> 33.7 us
  blocking collectives: 70.8 us -> 0 us
  starting transfers between devices: 95.4 us -> 128 us
  local copies, waits for them, and re-layouts: 114 us -> 83.9 us
  other arithmetic: 95.8 us -> 76.9 us
    all_to_all x16 -> x5, waiting for transfers between devices: 591 us -> 45.1 us  [exchange(): return lax.all_to_all(a, 'dp', 0, 0, tiled=True)]
    pallas_call x0 -> x29, Pallas kernels: none -> 317 us  [the longest x8 89.1 us: weight_grad(): pl.pallas_call(weight_grad_kernel, grid=(width // cols,), in_specs=[pl.Bl...]
    dot_general x56 -> x16, matrix products: 325 us -> 33.7 us  [dot(): lax.dot_general(a, b, (((over_a,), (over_b,)), ((), ())), preferred_eleme...]
    ppermute x20 -> x77, waiting for transfers between devices: 133 us -> 318 us  [swap(): return lax.ppermute(a, axis, [(i, i ^ step) for i in range(size)])]
    ppermute x20 -> x77, starting transfers between devices: 23.2 us -> 102 us  [swap(): return lax.ppermute(a, axis, [(i, i ^ step) for i in range(size)])]
    all_to_all x16 -> x5, starting transfers between devices: 71.4 us -> 24.6 us  [exchange(): return lax.all_to_all(a, 'dp', 0, 0, tiled=True)]
    psum x1 -> x0, blocking collectives: 38.5 us -> none  [per_device(): gg = lax.psum(gg, ('dp', 'mp'))]
    convert_element_type x9 -> x0, local copies, waits for them, and re-layouts: 18.8 us -> none  [the longest x5 12.5 us: unblock(): return (gate.astype(F32), up.astype(F32), down.astype(F32))]
  transfers between devices with their start and end apart: 47 -> 92, of which waited for: 20 -> 34; matrix products, arithmetic and copies ran while one was open for 34% -> 16% of each run, Pallas kernels for 0% -> 28%
where the time goes in v2:
time: 1050 us; the launch traced here: 1030 us
  waiting for transfers between devices  376 us (36%)
  Pallas kernels  317 us (30%)
  starting transfers between devices  128 us (12%)
  local copies, waits for them, and re-layouts  83.9 us (8%)
  other arithmetic  76.9 us (7%)
  matrix products  33.7 us (3%)
  between operations  17.8 us (2%)
    ppermute x77, waiting for transfers between devices, swap(): return lax.ppermute(a, axis, [(i, i ^ step) for i in range(size)])  318 us
    ppermute x77, starting transfers between devices, swap(): return lax.ppermute(a, axis, [(i, i ^ step) for i in range(size)])  102 us
    pallas_call x8, Pallas kernels, weight_grad(): pl.pallas_call(weight_grad_kernel, grid=(width // cols,), in_specs=[pl.Bl...  89.1 us
    pallas_call x8, Pallas kernels, geglu(): pl.pallas_call(geglu_kernel, grid=(n // step,), in_specs=[pl.BlockSpec((s...  86 us
    pallas_call x3, Pallas kernels, contract(): pl.pallas_call(functools.partial(contract_kernel, count), grid=(width //...  65.8 us
    all_to_all x5, waiting for transfers between devices, exchange(): return lax.all_to_all(a, 'dp', 0, 0, tiled=True)  45.1 us
    dot_general x16, matrix products, dot(): lax.dot_general(a, b, (((over_a,), (over_b,)), ((), ())), preferred_eleme...  33.7 us
    all_to_all x5, starting transfers between devices, exchange(): return lax.all_to_all(a, 'dp', 0, 0, tiled=True)  24.6 us
  transfers between devices with their start and end apart: 92, of which 34 were waited for; matrix products, arithmetic and copies ran while one was open for 16% of the time, Pallas kernels for 28%

profile of v2, /device:TPU:0, one launch (start us, length us, event | category | flops | bytes accessed | tf_op | source)
XLA Modules:
  0.0 1033.1 jit_solution(4646448263247491019)
XLA Ops:
  45.3 35.7 %collective-permute-done.3 = f32[1,1536]{1,0:T(1,128)S(1)} collective-permute-done((f32[1,1536]{1,0:T(1,128)S(1)}, f32[1,1536]{1,0:T(1,128)S(1)}, u32[]{:S(2)}, u32[]{:S(2)}) %collective-permute-start.3) | collective-permute-done | bytes 6176 | tf_op jit(solution)/shard_map/token_features/ppermute | solution.py:148
  141.3 17.4 %collective-permute-done.15 = bf16[208,2048]{1,0:T(8,128)(2,1)S(1)} collective-permute-done((bf16[208,2048]{1,0:T(8,128)(2,1)S(1)}, bf16[208,2048]{1,0:T(8,128)(2,1)S(1)}, u32[]{:S(2)}, u32[]{:S(2)}) %collective-permute-start.15) | collective-permute-done | bytes 852000 | tf_op jit(solution)/shard_map/attention/ppermute | solution.py:148
  158.7 18.6 %collective-permute-done.16 = bf16[208,2048]{1,0:T(8,128)(2,1)S(1)} collective-permute-done((bf16[208,2048]{1,0:T(8,128)(2,1)S(1)}, bf16[208,2048]{1,0:T(8,128)(2,1)S(1)}, u32[]{:S(2)}, u32[]{:S(2)}) %collective-permute-start.16) | collective-permute-done | bytes 852000 | tf_op jit(solution)/shard_map/attention/ppermute | solution.py:148
  193.6 56.2 %collective-permute-done.18.gate_up_ref.down_ref.refs_5_.refs_9_ = bf16[2048,768]{1,0:T(8,128)(2,1)} collective-permute-done((bf16[2048,768]{1,0:T(8,128)(2,1)S(1)}, bf16[2048,768]{1,0:T(8,128)(2,1)}, u32[]{:S(2)}, u32[]{:S(2)}) %collective-permute-start.18) | collective-permute-done | bytes 3145760 | tf_op jit(solution)/shard_map/attention/ppermute | solution.py:148
  262.4 12.4 %all-gather.18.cloned.1.call-done = bf16[1664,2048]{1,0:T(8,128)(2,1)} async-done(((bf16[208,2048]{1,0:T(8,128)(2,1)}), bf16[1664,2048]{1,0:T(8,128)(2,1)}) %all-gather.18.cloned.1.call-update) | async-done | bytes 6815760 | tf_op jit(solution)/shard_map/attention/all_gather | solution.py:633
  279.8 10.8 %geglu.8 = (bf16[1664,256]{1,0:T(8,128)(2,1)}, bf16[1664,512]{1,0:T(8,128)(2,1)}) custom-call(bf16[8,208,2048]{2,1,0:T(8,128)(2,1)} %bitcast.111, bf16[8,240,2048]{2,1,0:T(8,128)(2,1)} %bitcast.94, bf16[2048,768]{1,0:T(8,128)(2,1)} %bitcast.135, bf16[2048,768]{1,0:T(8,128)(2,1)} %bitcast.136), custom_call_target="tpu_custom_call" | custom-call | flops 1 | bytes 1 | tf_op jit(solution)/shard_map/geglu/geglu/pallas_call | solution.py:64
  290.7 10.7 %geglu.9 = (bf16[1664,256]{1,0:T(8,128)(2,1)}, bf16[1664,512]{1,0:T(8,128)(2,1)}) custom-call(bf16[8,208,2048]{2,1,0:T(8,128)(2,1)} %bitcast.112, bf16[8,240,2048]{2,1,0:T(8,128)(2,1)} %bitcast.95, bf16[2048,768]{1,0:T(8,128)(2,1)} %collective-permute-done.18.gate_up_ref.down_ref.refs_5_.refs_9_, ...), custom_call_target="tpu_custom_call" | custom-call | flops 1 | bytes 1 | tf_op jit(solution)/shard_map/geglu/geglu/pallas_call | solution.py:64
  301.4 10.7 %geglu.10 = (bf16[1664,256]{1,0:T(8,128)(2,1)}, bf16[1664,512]{1,0:T(8,128)(2,1)}) custom-call(bf16[8,208,2048]{2,1,0:T(8,128)(2,1)} %bitcast.113, bf16[8,240,2048]{2,1,0:T(8,128)(2,1)} %bitcast.96, bf16[2048,768]{1,0:T(8,128)(2,1)} %collective-permute-done.19.gate_up_ref.down_ref.refs_6_.refs_10_, ...), custom_call_target="tpu_custom_call" | custom-call | flops 1 | bytes 1 | tf_op jit(solution)/shard_map/geglu/geglu/pallas_call | solution.py:64
  315.9 10.7 %geglu.11 = (bf16[1664,256]{1,0:T(8,128)(2,1)}, bf16[1664,512]{1,0:T(8,128)(2,1)}) custom-call(bf16[8,208,2048]{2,1,0:T(8,128)(2,1)} %bitcast.114, bf16[8,240,2048]{2,1,0:T(8,128)(2,1)} %bitcast.97, bf16[2048,768]{1,0:T(8,128)(2,1)} %pad_maximum_fusion.gate_up_ref.down_ref.refs_7_.refs_11_, ...), custom_call_target="tpu_custom_call" | custom-call | flops 1 | bytes 1 | tf_op jit(solution)/shard_map/geglu/geglu/pallas_call | solution.py:64
  335.8 11.0 %weight_grad.8 = bf16[2048,768]{1,0:T(8,128)(2,1)} custom-call(bf16[8,208,2048]{2,1,0:T(8,128)(2,1)} %bitcast.115, bf16[8,240,2048]{2,1,0:T(8,128)(2,1)} %bitcast.98, bf16[1664,512]{1,0:T(8,128)(2,1)} %get-tuple-element.492.grad_ref.refs_1_, bf16[1664,256]{1,0:T(8,128)(2,1)} %get-tuple-element.493.hidden_ref.refs_1_), custom_call_target="tpu_custom_call" | custom-call | flops 1 | bytes 1 | tf_op jit(solution)/shard_map/geglu/weight_grad/pallas_call | solution.py:126
  356.0 11.0 %weight_grad.9 = bf16[2048,768]{1,0:T(8,128)(2,1)} custom-call(bf16[8,208,2048]{2,1,0:T(8,128)(2,1)} %bitcast.116, bf16[8,240,2048]{2,1,0:T(8,128)(2,1)} %bitcast.99, bf16[1664,512]{1,0:T(8,128)(2,1)} %get-tuple-element.508.grad_ref.refs_2_, bf16[1664,256]{1,0:T(8,128)(2,1)} %get-tuple-element.509.hidden_ref.refs_2_), custom_call_target="tpu_custom_call" | custom-call | flops 1 | bytes 1 | tf_op jit(solution)/shard_map/geglu/weight_grad/pallas_call | solution.py:126
  376.7 11.1 %weight_grad.10 = bf16[2048,768]{1,0:T(8,128)(2,1)} custom-call(bf16[8,208,2048]{2,1,0:T(8,128)(2,1)} %bitcast.117, bf16[8,240,2048]{2,1,0:T(8,128)(2,1)} %bitcast.101, bf16[1664,512]{1,0:T(8,128)(2,1)} %get-tuple-element.536.grad_ref.refs_0_, bf16[1664,256]{1,0:T(8,128)(2,1)} %get-tuple-element.592.hidden_ref.refs_0_), custom_call_target="tpu_custom_call" | custom-call | flops 1 | bytes 1 | tf_op jit(solution)/shard_map/geglu/weight_grad/pallas_call | solution.py:126
  387.8 10.8 %geglu.12 = (bf16[1664,256]{1,0:T(8,128)(2,1)}, bf16[1664,512]{1,0:T(8,128)(2,1)}) custom-call(bf16[8,208,2048]{2,1,0:T(8,128)(2,1)} %bitcast.118, bf16[8,240,2048]{2,1,0:T(8,128)(2,1)} %bitcast.102, bf16[2048,768]{1,0:T(8,128)(2,1)} %bitcast.129, bf16[2048,768]{1,0:T(8,128)(2,1)} %bitcast.130), custom_call_target="tpu_custom_call" | custom-call | flops 1 | bytes 1 | tf_op jit(solution)/shard_map/geglu/geglu/pallas_call | solution.py:64
  407.9 21.9 %contract.3.refs_8_ = f32[1664,2048]{1,0:T(8,128)} custom-call(bf16[1664,512]{1,0:T(8,128)(2,1)} %get-tuple-element.536.grad_ref.refs_0_, bf16[1664,512]{1,0:T(8,128)(2,1)} %get-tuple-element.492.grad_ref.refs_1_, bf16[1664,512]{1,0:T(8,128)(2,1)} %get-tuple-element.508.grad_ref.refs_2_, bf16[1664,512]{1,0:T(8,128)(2,1)} %get-tuple-element.537.refs_3_.grad_ref, ...), custom_call_target="tpu_custom_call" | custom-call | flops 1 | bytes 1 | tf_op jit(solution)/shard_map/geglu/contract/pallas_call | solution.py:101
  439.8 11.0 %weight_grad.11 = bf16[2048,768]{1,0:T(8,128)(2,1)} custom-call(bf16[8,208,2048]{2,1,0:T(8,128)(2,1)} %bitcast.119, bf16[8,240,2048]{2,1,0:T(8,128)(2,1)} %bitcast.103, bf16[1664,512]{1,0:T(8,128)(2,1)} %get-tuple-element.537.refs_3_.grad_ref, bf16[1664,256]{1,0:T(8,128)(2,1)} %get-tuple-element.542.hidden_ref.refs_3_), custom_call_target="tpu_custom_call" | custom-call | flops 1 | bytes 1 | tf_op jit(solution)/shard_map/geglu/weight_grad/pallas_call | solution.py:126
  463.1 10.6 %geglu.13 = (bf16[1664,256]{1,0:T(8,128)(2,1)}, bf16[1664,512]{1,0:T(8,128)(2,1)}) custom-call(bf16[8,208,2048]{2,1,0:T(8,128)(2,1)} %bitcast.120, bf16[8,240,2048]{2,1,0:T(8,128)(2,1)} %bitcast.104, bf16[2048,768]{1,0:T(8,128)(2,1)} %collective-permute-done.29.gate_up_ref.down_ref.refs_5_.refs_13_, ...), custom_call_target="tpu_custom_call" | custom-call | flops 1 | bytes 1 | tf_op jit(solution)/shard_map/geglu/geglu/pallas_call | solution.py:64
  473.8 10.7 %geglu.14 = (bf16[1664,256]{1,0:T(8,128)(2,1)}, bf16[1664,512]{1,0:T(8,128)(2,1)}) custom-call(bf16[8,208,2048]{2,1,0:T(8,128)(2,1)} %bitcast.121, bf16[8,240,2048]{2,1,0:T(8,128)(2,1)} %bitcast.105, bf16[2048,768]{1,0:T(8,128)(2,1)} %collective-permute-done.30.gate_up_ref.down_ref.refs_6_.refs_14_, ...), custom_call_target="tpu_custom_call" | custom-call | flops 1 | bytes 1 | tf_op jit(solution)/shard_map/geglu/geglu/pallas_call | solution.py:64
  498.4 10.9 %geglu.15 = (bf16[1664,256]{1,0:T(8,128)(2,1)}, bf16[1664,512]{1,0:T(8,128)(2,1)}) custom-call(bf16[8,208,2048]{2,1,0:T(8,128)(2,1)} %bitcast.122, bf16[8,240,2048]{2,1,0:T(8,128)(2,1)} %bitcast.106, bf16[2048,768]{1,0:T(8,128)(2,1)} %pad_maximum_fusion.1.gate_up_ref.down_ref.refs_7_.refs_15_, ...), custom_call_target="tpu_custom_call" | custom-call | flops 1 | bytes 1 | tf_op jit(solution)/shard_map/geglu/geglu/pallas_call | solution.py:64
  509.9 10.9 %collective-permute-done.43 = bf16[1024,768]{1,0:T(8,128)(2,1)} collective-permute-done((bf16[1024,768]{1,0:T(8,128)(2,1)}, bf16[1024,768]{1,0:T(8,128)(2,1)}, u32[]{:S(2)}, u32[]{:S(2)}) %collective-permute-start.43) | collective-permute-done | bytes 1572896 | tf_op jit(solution)/shard_map/geglu/ppermute | solution.py:148
  524.3 22.5 %contract.4 = bf16[1664,2048]{1,0:T(8,128)(2,1)} custom-call(bf16[1664,512]{1,0:T(8,128)(2,1)} %get-tuple-element.580.refs_0_.grad_ref, bf16[1664,512]{1,0:T(8,128)(2,1)} %get-tuple-element.581.refs_1_.grad_ref, bf16[1664,512]{1,0:T(8,128)(2,1)} %get-tuple-element.582.refs_2_.grad_ref, bf16[1664,512]{1,0:T(8,128)(2,1)} %get-tuple-element.583.refs_3_.grad_ref, ...), custom_call_target="tpu_custom_call" | custom-call | flops 1 | bytes 1 | tf_op jit(solution)/shard_map/geglu/contract/pallas_call | solution.py:101
  562.1 25.0 %collective-permute-done.42 = bf16[1024,768]{1,0:T(8,128)(2,1)} collective-permute-done((bf16[1024,768]{1,0:T(8,128)(2,1)}, bf16[1024,768]{1,0:T(8,128)(2,1)}, u32[]{:S(2)}, u32[]{:S(2)}) %collective-permute-start.42) | collective-permute-done | bytes 1572896 | tf_op jit(solution)/shard_map/geglu/ppermute | solution.py:148
  599.5 21.5 %contract.5 = bf16[1664,2048]{1,0:T(8,128)(2,1)} custom-call(bf16[1664,256]{1,0:T(8,128)(2,1)} %get-tuple-element.592.hidden_ref.refs_0_, bf16[1664,256]{1,0:T(8,128)(2,1)} %get-tuple-element.493.hidden_ref.refs_1_, bf16[1664,256]{1,0:T(8,128)(2,1)} %get-tuple-element.509.hidden_ref.refs_2_, bf16[1664,256]{1,0:T(8,128)(2,1)} %get-tuple-element.542.hidden_ref.refs_3_, ...), custom_call_target="tpu_custom_call" | custom-call | flops 1 | bytes 1 | tf_op jit(solution)/shard_map/geglu/contract/pallas_call | solution.py:101
  625.9 11.6 %weight_grad.12 = bf16[2048,768]{1,0:T(8,128)(2,1)} custom-call(bf16[8,208,2048]{2,1,0:T(8,128)(2,1)} %bitcast.123, bf16[8,240,2048]{2,1,0:T(8,128)(2,1)} %bitcast.107, bf16[1664,512]{1,0:T(8,128)(2,1)} %get-tuple-element.583.refs_3_.grad_ref, bf16[1664,256]{1,0:T(8,128)(2,1)} %get-tuple-element.596.refs_7_.hidden_ref), custom_call_target="tpu_custom_call" | custom-call | flops 1 | bytes 1 | tf_op jit(solution)/shard_map/geglu/weight_grad/pallas_call | solution.py:126
  637.5 11.1 %weight_grad.13 = bf16[2048,768]{1,0:T(8,128)(2,1)} custom-call(bf16[8,208,2048]{2,1,0:T(8,128)(2,1)} %bitcast.124, bf16[8,240,2048]{2,1,0:T(8,128)(2,1)} %bitcast.108, bf16[1664,512]{1,0:T(8,128)(2,1)} %get-tuple-element.582.refs_2_.grad_ref, bf16[1664,256]{1,0:T(8,128)(2,1)} %get-tuple-element.595.refs_6_.hidden_ref), custom_call_target="tpu_custom_call" | custom-call | flops 1 | bytes 1 | tf_op jit(solution)/shard_map/geglu/weight_grad/pallas_call | solution.py:126
  648.6 11.1 %weight_grad.14 = bf16[2048,768]{1,0:T(8,128)(2,1)} custom-call(bf16[8,208,2048]{2,1,0:T(8,128)(2,1)} %bitcast.125, bf16[8,240,2048]{2,1,0:T(8,128)(2,1)} %bitcast.109, bf16[1664,512]{1,0:T(8,128)(2,1)} %get-tuple-element.581.refs_1_.grad_ref, bf16[1664,256]{1,0:T(8,128)(2,1)} %get-tuple-element.594.refs_5_.hidden_ref), custom_call_target="tpu_custom_call" | custom-call | flops 1 | bytes 1 | tf_op jit(solution)/shard_map/geglu/weight_grad/pallas_call | solution.py:126
  659.7 11.3 %weight_grad.15 = bf16[2048,768]{1,0:T(8,128)(2,1)} custom-call(bf16[8,208,2048]{2,1,0:T(8,128)(2,1)} %bitcast.126, bf16[8,240,2048]{2,1,0:T(8,128)(2,1)} %bitcast.110, bf16[1664,512]{1,0:T(8,128)(2,1)} %get-tuple-element.580.refs_0_.grad_ref, bf16[1664,256]{1,0:T(8,128)(2,1)} %get-tuple-element.593.refs_4_.hidden_ref), custom_call_target="tpu_custom_call" | custom-call | flops 1 | bytes 1 | tf_op jit(solution)/shard_map/geglu/weight_grad/pallas_call | solution.py:126
  710.3 19.8 %collective-permute-done.48 = bf16[208,2048]{1,0:T(8,128)(2,1)S(1)} collective-permute-done((bf16[208,2048]{1,0:T(8,128)(2,1)S(1)}, bf16[208,2048]{1,0:T(8,128)(2,1)S(1)}, u32[]{:S(2)}, u32[]{:S(2)}) %collective-permute-start.48) | collective-permute-done | bytes 852000 | tf_op jit(solution)/shard_map/middle_norm/ppermute | solution.py:148
  744.1 40.8 %all-to-all-done.3.refs_0_ = bf16[8,320,768]{2,1,0:T(8,128)(2,1)} async-done(((bf16[8,320,768]{2,1,0:T(8,128)(2,1)}), bf16[8,320,768]{2,1,0:T(8,128)(2,1)}, u32[]{:S(2)}, u32[]{:S(2)}) %all-to-all-start.3) | async-done | bytes 3932192 | tf_op jit(solution)/shard_map/geglu/all_to_all | solution.py:152
  796.7 12.8 %attend_back.3 = (bf16[832,512]{1,0:T(8,128)(2,1)}, bf16[896,512]{1,0:T(8,128)(2,1)}) custom-call(s32[1]{0:T(128)S(6)} %copy.113.cams_ref, s32[1]{0:T(128)S(6)} %copy.114.texts_ref, bf16[832,640]{1,0:T(8,128)(2,1)} %copy-done.30, bf16[832,512]{1,0:T(8,128)(2,1)} %convolution_convert_fusion.5.gm_ref, bf16[832,512]{1,0:T(8,128)(2,1)} %copy-done.6, ...), custom_call_target="tpu_custom_call" | custom-call | flops 1 | bytes 1 | tf_op jit(solution)/shard_map/attention_back/attend_back/pallas_call | solution.py:361
  821.1 35.3 %collective-permute-done.52 = bf16[896,128]{1,0:T(8,128)(2,1)S(1)} collective-permute-done((bf16[896,128]{1,0:T(8,128)(2,1)S(1)}, bf16[896,128]{1,0:T(8,128)(2,1)S(1)}, u32[]{:S(2)}, u32[]{:S(2)}) %collective-permute-start.52) | collective-permute-done | bytes 229408 | tf_op jit(solution)/shard_map/attention_back/ppermute | solution.py:148
  956.3 14.2 %collective-permute-done.75 = f32[2,768]{1,0:T(2,128)S(1)} collective-permute-done((f32[2,768]{1,0:T(2,128)S(1)}, f32[2,768]{1,0:T(2,128)S(1)}, u32[]{:S(2)}, u32[]{:S(2)}) %collective-permute-start.75) | collective-permute-done | bytes 6176 | tf_op jit(solution)/shard_map/gain_grads/ppermute | solution.py:148
  976.8 14.3 %collective-permute-done.76 = f32[2,768]{1,0:T(2,128)S(1)} collective-permute-done((f32[2,768]{1,0:T(2,128)S(1)}, f32[2,768]{1,0:T(2,128)S(1)}, u32[]{:S(2)}, u32[]{:S(2)}) %collective-permute-start.76) | collective-permute-done | bytes 6176 | tf_op jit(solution)/shard_map/gain_grads/ppermute | solution.py:148
  (603 shorter events, 460.9 us)
Async XLA Ops:
  7.2 88.4 %all-gather.10.cloned.1.call-start = ((), (), s32[]{:S(2)}) async-start(), calls=%async_computation.9 | async-start | bytes 2949120 | tf_op jit(solution)/shard_map/attention_weights/all_gather | solution.py:586
  12.0 119.5 %all-gather.12.cloned.1.call-start = ((), (), s32[]{:S(2)}) async-start(), calls=%async_computation.10 | async-start | bytes 2359296 | tf_op jit(solution)/shard_map/attention_weights/all_gather | solution.py:588
  12.8 249.6 %all-gather.16.cloned.1.call-start = ((), (), s32[]{:S(2)}) async-start(), calls=%async_computation.15 | async-start | bytes 8847360 | tf_op jit(solution)/shard_map/token_features/all_gather | solution.py:605
  34.5 97.0 %all-to-all-start = ((bf16[8,256,768]{2,1,0:T(8,128)(2,1)}), bf16[8,256,768]{2,1,0:T(8,128)(2,1)S(1)}, u32[]{:S(2)}, u32[]{:S(2)}) async-start(bf16[8,256,768]{2,1,0:T(8,128)(2,1)} %get-tuple-element.429), calls=%async_computation | async-start | bytes 6291456 | tf_op jit(solution)/shard_map/unit_weights/all_to_all | solution.py:152
  39.6 235.2 %all-gather.18.cloned.1.call-start = ((), (), s32[]{:S(2)}) async-start(), calls=%async_computation.16 | async-start | bytes 7667712 | tf_op jit(solution)/shard_map/attention/all_gather | solution.py:633
  180.5 146.3 %all-gather.20.cloned.1.call-start = ((), (), s32[]{:S(2)}) async-start(), calls=%async_computation.17 | async-start | bytes 2654208 | tf_op jit(solution)/shard_map/attention/all_gather | solution.py:639
  180.7 69.0 %collective-permute-start.18 = (bf16[2048,768]{1,0:T(8,128)(2,1)S(1)}, bf16[2048,768]{1,0:T(8,128)(2,1)}, u32[]{:S(2)}, u32[]{:S(2)}) collective-permute-start(bf16[2048,768]{1,0:T(8,128)(2,1)S(1)} %bitcast.133), channel_id=1, source_target_pairs={{0,1},{1,0},{2,3},{3,2},{4,5},{5,4},{6,7},{7,6},{8,9},{9,8},{10,11... | collective-permute-start | bytes 9437192 | tf_op jit(solution)/shard_map/attention/ppermute | solution.py:148
  182.0 69.2 %collective-permute-start.19 = (bf16[2048,768]{1,0:T(8,128)(2,1)S(1)}, bf16[2048,768]{1,0:T(8,128)(2,1)}, u32[]{:S(2)}, u32[]{:S(2)}) collective-permute-start(bf16[2048,768]{1,0:T(8,128)(2,1)S(1)} %bitcast.134), channel_id=1, source_target_pairs={{0,2},{1,3},{2,0},{3,1},{4,6},{5,7},{6,4},{7,5},{8,10},{9,11},{10,... | collective-permute-start | bytes 9437192 | tf_op jit(solution)/shard_map/attention/ppermute | solution.py:148
  189.3 73.0 %all-to-all-start.1 = ((bf16[8,128,384]{2,1,0:T(8,128)(2,1)}), bf16[8,128,384]{2,1,0:T(8,128)(2,1)}, u32[]{:S(2)}, u32[]{:S(2)}) async-start(bf16[8,128,384]{2,1,0:T(8,128)(2,1)} %pack.3), calls=%async_computation.1 | async-start | bytes 1572864 | tf_op jit(solution)/shard_map/attention/all_to_all | solution.py:152
  253.8 58.3 %collective-permute-start.20 = (bf16[1024,768]{1,0:T(8,128)(2,1)}, bf16[1024,768]{1,0:T(8,128)(2,1)}, u32[]{:S(2)}, u32[]{:S(2)}) collective-permute-start(bf16[1024,768]{1,0:T(8,128)(2,1)} %slice.198), channel_id=1, source_target_pairs={{0,1},{1,0},{2,3},{3,2},{4,5},{5,4},{6,7},{7,6},{8,9},{9,8},{10,11... | collective-permute-start | bytes 4718600 | tf_op jit(solution)/shard_map/attention/ppermute | solution.py:148
  256.8 55.3 %collective-permute-start.21 = (bf16[1024,768]{1,0:T(8,128)(2,1)}, bf16[1024,768]{1,0:T(8,128)(2,1)}, u32[]{:S(2)}, u32[]{:S(2)}) collective-permute-start(bf16[1024,768]{1,0:T(8,128)(2,1)} %slice.199), channel_id=1, source_target_pairs={{0,2},{1,3},{2,0},{3,1},{4,6},{5,7},{6,4},{7,5},{8,10},{9,11},{10,... | collective-permute-start | bytes 4718600 | tf_op jit(solution)/shard_map/attention/ppermute | solution.py:148
  274.7 94.1 %all-to-all-start.2 = ((bf16[8,256,768]{2,1,0:T(8,128)(2,1)}), bf16[8,256,768]{2,1,0:T(8,128)(2,1)S(1)}, u32[]{:S(2)}, u32[]{:S(2)}) async-start(bf16[8,256,768]{2,1,0:T(8,128)(2,1)} %get-tuple-element.518), calls=%async_computation.2 | async-start | bytes 6291456 | tf_op jit(solution)/shard_map/geglu/all_to_all | solution.py:152
  278.4 120.2 %all-gather.14.cloned.1.call-start = ((), (), s32[]{:S(2)}) async-start(), calls=%async_computation.11 | async-start | bytes 1179648 | tf_op jit(solution)/shard_map/geglu/all_gather | solution.py:689
  368.5 317.4 %reduce-scatter.9.cloned.1.call-start = ((), (), s32[]{:S(2)}) async-start(), calls=%async_computation.13 | async-start | bytes 7667712 | tf_op jit(solution)/shard_map/geglu/reduce_scatter | solution.py:736
  368.8 69.7 %collective-permute-start.29 = (bf16[2048,768]{1,0:T(8,128)(2,1)S(1)}, bf16[2048,768]{1,0:T(8,128)(2,1)}, u32[]{:S(2)}, u32[]{:S(2)}) collective-permute-start(bf16[2048,768]{1,0:T(8,128)(2,1)S(1)} %bitcast.127), channel_id=1, source_target_pairs={{0,1},{1,0},{2,3},{3,2},{4,5},{5,4},{6,7},{7,6},{8,9},{9,8},{10,11... | collective-permute-start | bytes 9437192 | tf_op jit(solution)/shard_map/geglu/ppermute | solution.py:148
  370.3 69.5 %collective-permute-start.30 = (bf16[2048,768]{1,0:T(8,128)(2,1)S(1)}, bf16[2048,768]{1,0:T(8,128)(2,1)}, u32[]{:S(2)}, u32[]{:S(2)}) collective-permute-start(bf16[2048,768]{1,0:T(8,128)(2,1)S(1)} %bitcast.128), channel_id=1, source_target_pairs={{0,2},{1,3},{2,0},{3,1},{4,6},{5,7},{6,4},{7,5},{8,10},{9,11},{10,... | collective-permute-start | bytes 9437192 | tf_op jit(solution)/shard_map/geglu/ppermute | solution.py:148
  459.3 61.6 %collective-permute-start.43 = (bf16[1024,768]{1,0:T(8,128)(2,1)}, bf16[1024,768]{1,0:T(8,128)(2,1)}, u32[]{:S(2)}, u32[]{:S(2)}) collective-permute-start(bf16[1024,768]{1,0:T(8,128)(2,1)} %get-tuple-element.784), channel_id=1, source_target_pairs={{0,1},{1,0},{2,3},{3,2},{4,5},{5,4},{6,7},{7,6},{8,9},{9,8},{10,11... | collective-permute-start | bytes 4718600 | tf_op jit(solution)/shard_map/geglu/ppermute | solution.py:148
  460.4 63.8 %collective-permute-start.44 = (bf16[1024,768]{1,0:T(8,128)(2,1)}, bf16[1024,768]{1,0:T(8,128)(2,1)}, u32[]{:S(2)}, u32[]{:S(2)}) collective-permute-start(bf16[1024,768]{1,0:T(8,128)(2,1)} %get-tuple-element.783), channel_id=1, source_target_pairs={{0,2},{1,3},{2,0},{3,1},{4,6},{5,7},{6,4},{7,5},{8,10},{9,11},{10,... | collective-permute-start | bytes 4718600 | tf_op jit(solution)/shard_map/geglu/ppermute | solution.py:148
  546.8 396.0 %reduce-scatter.7.cloned.1.call-start = ((), (), s32[]{:S(2)}) async-start(), calls=%async_computation.12 | async-start | bytes 7667712 | tf_op jit(solution)/shard_map/geglu/reduce_scatter | solution.py:743
  621.0 50.0 %collective-permute-start.45 = (bf16[1024,768]{1,0:T(8,128)(2,1)}, bf16[1024,768]{1,0:T(8,128)(2,1)}, u32[]{:S(2)}, u32[]{:S(2)}) collective-permute-start(bf16[1024,768]{1,0:T(8,128)(2,1)} %add_convert_fusion.7), channel_id=1, source_target_pairs={{0,2},{1,3},{2,0},{3,1},{4,6},{5,7},{6,4},{7,5},{8,10},{9,11},{10,... | collective-permute-start | bytes 4718600 | tf_op jit(solution)/shard_map/geglu/ppermute | solution.py:148
  622.5 48.5 %collective-permute-start.46 = (bf16[1024,768]{1,0:T(8,128)(2,1)}, bf16[1024,768]{1,0:T(8,128)(2,1)}, u32[]{:S(2)}, u32[]{:S(2)}) collective-permute-start(bf16[1024,768]{1,0:T(8,128)(2,1)} %add_convert_fusion.6), channel_id=1, source_target_pairs={{0,1},{1,0},{2,3},{3,2},{4,5},{5,4},{6,7},{7,6},{8,9},{9,8},{10,11... | collective-permute-start | bytes 4718600 | tf_op jit(solution)/shard_map/geglu/ppermute | solution.py:148
  677.4 107.5 %all-to-all-start.3 = ((bf16[8,320,768]{2,1,0:T(8,128)(2,1)}), bf16[8,320,768]{2,1,0:T(8,128)(2,1)}, u32[]{:S(2)}, u32[]{:S(2)}) async-start(bf16[8,320,768]{2,1,0:T(8,128)(2,1)} %fusion.7), calls=%async_computation.5 | async-start | bytes 7864320 | tf_op jit(solution)/shard_map/geglu/all_to_all | solution.py:152
  684.7 321.4 %reduce-scatter.13.cloned.1.call-start = ((), (), s32[]{:S(2)}) async-start(), calls=%async_computation.18 | async-start | bytes 3538944
  693.9 96.6 %collective-permute-start.50 = (bf16[1024,768]{1,0:T(8,128)(2,1)}, bf16[1024,768]{1,0:T(8,128)(2,1)}, u32[]{:S(2)}, u32[]{:S(2)}) collective-permute-start(bf16[1024,768]{1,0:T(8,128)(2,1)} %get-tuple-element.780), channel_id=1, source_target_pairs={{0,1},{1,0},{2,3},{3,2},{4,5},{5,4},{6,7},{7,6},{8,9},{9,8},{10,11... | collective-permute-start | bytes 4718600 | tf_op jit(solution)/shard_map/middle_norm/ppermute | solution.py:148
  695.4 95.2 %collective-permute-start.51 = (bf16[1024,768]{1,0:T(8,128)(2,1)}, bf16[1024,768]{1,0:T(8,128)(2,1)}, u32[]{:S(2)}, u32[]{:S(2)}) collective-permute-start(bf16[1024,768]{1,0:T(8,128)(2,1)} %get-tuple-element.779), channel_id=1, source_target_pairs={{0,2},{1,3},{2,0},{3,1},{4,6},{5,7},{6,4},{7,5},{8,10},{9,11},{10,... | collective-permute-start | bytes 4718600 | tf_op jit(solution)/shard_map/middle_norm/ppermute | solution.py:148
  809.6 199.3 %reduce-scatter.11.cloned.1.call-start = ((), (), s32[]{:S(2)}) async-start(), calls=%async_computation.14 | async-start | bytes 4423680 | tf_op jit(solution)/shard_map/query_key_value_grads/reduce_scatter | solution.py:802
  814.0 66.1 %collective-permute-start.58 = (bf16[1024,768]{1,0:T(8,128)(2,1)}, bf16[1024,768]{1,0:T(8,128)(2,1)}, u32[]{:S(2)}, u32[]{:S(2)}) collective-permute-start(bf16[1024,768]{1,0:T(8,128)(2,1)} %slice.226), channel_id=1, source_target_pairs={{0,1},{1,0},{2,3},{3,2},{4,5},{5,4},{6,7},{7,6},{8,9},{9,8},{10,11... | collective-permute-start | bytes 4718600 | tf_op jit(solution)/shard_map/middle_norm/ppermute | solution.py:148
  815.4 64.6 %collective-permute-start.60 = (bf16[1024,768]{1,0:T(8,128)(2,1)}, bf16[1024,768]{1,0:T(8,128)(2,1)}, u32[]{:S(2)}, u32[]{:S(2)}) collective-permute-start(bf16[1024,768]{1,0:T(8,128)(2,1)} %slice.228), channel_id=1, source_target_pairs={{0,2},{1,3},{2,0},{3,1},{4,6},{5,7},{6,4},{7,5},{8,10},{9,11},{10,... | collective-permute-start | bytes 4718600 | tf_op jit(solution)/shard_map/middle_norm/ppermute | solution.py:148
  905.2 110.0 %all-to-all-start.4 = ((bf16[8,256,768]{2,1,0:T(8,128)(2,1)}), bf16[8,256,768]{2,1,0:T(8,128)(2,1)}, u32[]{:S(2)}, u32[]{:S(2)}) async-start(bf16[8,256,768]{2,1,0:T(8,128)(2,1)} %bitcast.140), calls=%async_computation.6 | async-start | bytes 6291456 | tf_op jit(solution)/shard_map/query_key_value_grads/all_to_all | solution.py:152
  951.2 51.6 %collective-permute-start.62 = (bf16[208,512]{1,0:T(8,128)(2,1)S(1)}, bf16[208,512]{1,0:T(8,128)(2,1)S(1)}, u32[]{:S(2)}, u32[]{:S(2)}) collective-permute-start(bf16[208,512]{1,0:T(8,128)(2,1)S(1)} %get-tuple-element.801), channel_id=1, source_target_pairs={{0,1},{1,0},{2,3},{3,2},{4,5},{5,4},{6,7},{7,6},{8,9},{9,8},{10,11... | collective-permute-start | bytes 638984 | tf_op jit(solution)/shard_map/input_grads/ppermute | solution.py:148
  952.6 50.3 %collective-permute-start.63 = (bf16[208,512]{1,0:T(8,128)(2,1)S(1)}, bf16[208,512]{1,0:T(8,128)(2,1)S(1)}, u32[]{:S(2)}, u32[]{:S(2)}) collective-permute-start(bf16[208,512]{1,0:T(8,128)(2,1)S(1)} %get-tuple-element.800), channel_id=1, source_target_pairs={{0,2},{1,3},{2,0},{3,1},{4,6},{5,7},{6,4},{7,5},{8,10},{9,11},{10,... | collective-permute-start | bytes 638984 | tf_op jit(solution)/shard_map/input_grads/ppermute | solution.py:148
  953.3 49.5 %collective-permute-start.64 = (bf16[208,512]{1,0:T(8,128)(2,1)S(1)}, bf16[208,512]{1,0:T(8,128)(2,1)S(1)}, u32[]{:S(2)}, u32[]{:S(2)}) collective-permute-start(bf16[208,512]{1,0:T(8,128)(2,1)S(1)} %get-tuple-element.799), channel_id=1, source_target_pairs={{0,3},{1,2},{2,1},{3,0},{4,7},{5,6},{6,5},{7,4},{8,11},{9,10},{10,... | collective-permute-start | bytes 638984 | tf_op jit(solution)/shard_map/input_grads/ppermute | solution.py:148
  (170 other events, 2963.3 us)
Sparse Core Ops, SparseCore 0:
  12.1 40.0 all-gather.9
  53.8 68.9 all-gather.11
  124.5 78.1 all-gather.15
  204.8 69.9 all-gather.17
  276.8 49.8 all-gather.19
  368.6 29.6 all-gather.13
  546.9 79.7 reduce-scatter.8
  629.0 83.9 reduce-scatter.6
  809.7 38.9 reduce-scatter.12
  877.6 55.8 reduce-scatter.10

commit v3 on v2

--- a/solution.py
+++ b/solution.py
@@ -704,55 +704,63 @@
             part = jnp.concatenate([mm_nt(hidden, dt_act), mm_nt(grad, gu_act)], axis=1).astype(BF)
             part = order(part)
 
+            halving = Halving(part.reshape(n, apad, 2 * awidth), n, me)
+
             tile = n * block // 4
             gn2 = ffn = None
             if pieces == 2:
                 gn2 = order(
                     contract([order(grads[0][0])] + grads[0][1:], spread[0].blocks, 0, tile, 1024, None, F32)
                 )
-                spread[1].arrive(order)
-            halving = Halving(part.reshape(n, apad, 2 * awidth), n, me)
+            halving.take(order)
             for s in range(3, k):
                 parts[s] = backward(0, s)
-            for s in outward:
-                collects[0].put(s, parts[s])
             halving.take(order)
             if pieces == 2:
-                for s in range(1, k if k != 4 else 3):
+                spread[1].arrive(order)
+                forward(1, 1)
+            halving.take(order)
+            part = halving.result(order)
+            out_act = handed(part[:, :awidth], mine, k, 1)
+            gn2_act = everyones(part[:, awidth:], k)
+            if pieces == 2:
+                for s in range(2, k if k != 4 else 3):
                     forward(1, s)
-                halving.take(order)
                 spread[1].last(order)
                 if k == 4:
                     forward(1, 3)
-            halving.take(order)
-            collects[0].far(order)
-            part = halving.result(order)
-            out_act = handed(part[:, :awidth], mine, k, 1)
-            gn2_act = everyones(part[:, awidth:], k)
+            gn2_act, out_act = order(*gn2_act), order(*out_act)
+            for s in outward:
+                collects[0].put(s, order(parts[s]))
             last = pieces - 1
             gn2 = order(
                 contract([order(grads[last][0])] + grads[last][1:], spread[last].blocks, 0, tile, 1024, gn2)
             )
             gn2 = lax.psum_scatter(gn2, "dp", scatter_dimension=0, tiled=True)
-            collects[0].near(order)
-            collects[0].receive(order, "first_low", "second_high")
-            gn2_act, out_act = order(*gn2_act), order(*out_act)
+            collects[0].far(order)
             flat = [weights for piece in spread for weights in piece.blocks]
             flat_hiddens = [hidden for piece in hiddens for hidden in piece]
             ffn = order(contract([order(flat_hiddens[0])] + flat_hiddens[1:], flat, 2, tile, 1024))
             ffn = lax.psum_scatter(ffn, "dp", scatter_dimension=0, tiled=True)
             parts = {}
             if pieces == 2:
-                parts = {s: backward(1, s) for s in outward}
+                parts = {s: backward(1, s) for s in outward[:2]}
+            collects[0].receive(order, "first_low", "second_high")
+            collects[0].near(order)
+            if pieces == 2:
+                for s in outward[2:-1]:
+                    parts[s] = backward(1, s)
+
+        with jax.named_scope("middle_norm"):
+            back2_pre, gg2_pre = norm_back(order(gn2).astype(F32), middle_pre, inv2_pre, gain2_pre)
+            resid_pre = g_pre.astype(F32) + back2_pre
+            gb_pre = everyones(order(resid_pre.astype(BF)), k)
+            if pieces == 2:
+                parts[0] = backward(1, 0)
             back = [collects[0].result(order).reshape(n, depth, 3 * sizes[0])]
             gw_act = jnp.concatenate([mm_tn(nall_act, grad), mm_tn(gall_act, hidden)], axis=1)
             gw_act = gw_act.astype(BF).reshape(n, adepth, 3 * aunits)
             back[0] = exchange(order(jnp.concatenate([back[0], beside(gw_act, sizes[0])], axis=1)))
-
-        with jax.named_scope("middle_norm"):
-            back2_pre, gg2_pre = norm_back(order(gn2).astype(F32), middle_pre, inv2_pre, gain2_pre)
-            resid_pre = g_pre.astype(F32) + back2_pre
-            gb_pre = everyones(order(resid_pre.astype(BF)), k)
             for s in parts:
                 collects[1].put(s, order(parts[s]))
 
@@ -772,11 +780,6 @@
                 )
             )
             gb_pre = placed(order(*gb_pre), mine, 0)
-            back[0] = order(back[0])
-            if pieces == 2:
-                collects[1].far(order)
-                collects[1].near(order)
-
         with jax.named_scope("attention_back"):
             gm_pre = order(mm(gb_pre, wout_pre).astype(BF))
             gq_pre, gkv = order(
@@ -786,6 +789,10 @@
                 )
             )
             gkv = handed(gkv, mine, k, 1)
+            if pieces == 2:
+                collects[1].far(order)
+                collects[1].near(order)
+            back[0] = order(back[0])
             go = order(pair_grad(gb_pre, mixed_pre, gb_act, mixed_act, n)).reshape(-1, qcols)
             go = lax.psum_scatter(go, "dp", scatter_dimension=0, tiled=True)
             gkv = total(order(*gkv)).astype(BF)

time: 1050 us -> 1010 us (0.962)
  waiting for transfers between devices: 376 us -> 334 us
    all_to_all x5, waiting for transfers between devices: 45.1 us -> 14.3 us  [exchange(): return lax.all_to_all(a, 'dp', 0, 0, tiled=True)]
    ppermute x77, waiting for transfers between devices: 318 us -> 306 us  [swap(): return lax.ppermute(a, axis, [(i, i ^ step) for i in range(size)])]
  transfers between devices with their start and end apart: 92 -> 92, of which waited for: 34 -> 32; matrix products, arithmetic and copies ran while one was open for 16% -> 17% of each run, Pallas kernels for 28% -> 29%
where the time goes in v3:
time: 1010 us; the launch traced here: 995 us
  waiting for transfers between devices  334 us (33%)
  Pallas kernels  316 us (31%)
  starting transfers between devices  131 us (13%)
  local copies, waits for them, and re-layouts  85.9 us (9%)
  other arithmetic  76.9 us (8%)
  matrix products  33.5 us (3%)
  between operations  17.7 us (2%)
    ppermute x77, waiting for transfers between devices, swap(): return lax.ppermute(a, axis, [(i, i ^ step) for i in range(size)])  306 us
    ppermute x77, starting transfers between devices, swap(): return lax.ppermute(a, axis, [(i, i ^ step) for i in range(size)])  101 us
    pallas_call x8, Pallas kernels, weight_grad(): pl.pallas_call(weight_grad_kernel, grid=(width // cols,), in_specs=[pl.Bl...  88.7 us
    pallas_call x8, Pallas kernels, geglu(): pl.pallas_call(geglu_kernel, grid=(n // step,), in_specs=[pl.BlockSpec((s...  85.9 us
    pallas_call x3, Pallas kernels, contract(): pl.pallas_call(functools.partial(contract_kernel, count), grid=(width //...  66.3 us
    dot_general x16, matrix products, dot(): lax.dot_general(a, b, (((over_a,), (over_b,)), ((), ())), preferred_eleme...  33.5 us
    all_to_all x5, starting transfers between devices, exchange(): return lax.all_to_all(a, 'dp', 0, 0, tiled=True)  28 us
    unnamed x227, local copies, waits for them, and re-layouts  20.5 us
  transfers between devices with their start and end apart: 92, of which 32 were waited for; matrix products, arithmetic and copies ran while one was open for 17% of the time, Pallas kernels for 29%

profile of v3, /device:TPU:0, one launch (start us, length us, event | category | flops | bytes accessed | tf_op | source)
XLA Modules:
  0.0 994.6 jit_solution(14598710379090625616)
XLA Ops:
  45.3 35.7 %collective-permute-done.3 = f32[1,1536]{1,0:T(1,128)S(1)} collective-permute-done((f32[1,1536]{1,0:T(1,128)S(1)}, f32[1,1536]{1,0:T(1,128)S(1)}, u32[]{:S(2)}, u32[]{:S(2)}) %collective-permute-start.3) | collective-permute-done | bytes 6176 | tf_op jit(solution)/shard_map/token_features/ppermute | solution.py:148
  141.3 17.4 %collective-permute-done.15 = bf16[208,2048]{1,0:T(8,128)(2,1)S(1)} collective-permute-done((bf16[208,2048]{1,0:T(8,128)(2,1)S(1)}, bf16[208,2048]{1,0:T(8,128)(2,1)S(1)}, u32[]{:S(2)}, u32[]{:S(2)}) %collective-permute-start.15) | collective-permute-done | bytes 852000 | tf_op jit(solution)/shard_map/attention/ppermute | solution.py:148
  158.7 18.6 %collective-permute-done.16 = bf16[208,2048]{1,0:T(8,128)(2,1)S(1)} collective-permute-done((bf16[208,2048]{1,0:T(8,128)(2,1)S(1)}, bf16[208,2048]{1,0:T(8,128)(2,1)S(1)}, u32[]{:S(2)}, u32[]{:S(2)}) %collective-permute-start.16) | collective-permute-done | bytes 852000 | tf_op jit(solution)/shard_map/attention/ppermute | solution.py:148
  193.8 56.2 %collective-permute-done.18.gate_up_ref.down_ref.refs_5_.refs_9_ = bf16[2048,768]{1,0:T(8,128)(2,1)} collective-permute-done((bf16[2048,768]{1,0:T(8,128)(2,1)S(1)}, bf16[2048,768]{1,0:T(8,128)(2,1)}, u32[]{:S(2)}, u32[]{:S(2)}) %collective-permute-start.18) | collective-permute-done | bytes 3145760 | tf_op jit(solution)/shard_map/attention/ppermute | solution.py:148
  262.7 11.7 %all-gather.18.cloned.1.call-done = bf16[1664,2048]{1,0:T(8,128)(2,1)} async-done(((bf16[208,2048]{1,0:T(8,128)(2,1)}), bf16[1664,2048]{1,0:T(8,128)(2,1)}) %all-gather.18.cloned.1.call-update) | async-done | bytes 6815760 | tf_op jit(solution)/shard_map/attention/all_gather | solution.py:633
  279.5 10.9 %geglu.8 = (bf16[1664,256]{1,0:T(8,128)(2,1)}, bf16[1664,512]{1,0:T(8,128)(2,1)}) custom-call(bf16[8,208,2048]{2,1,0:T(8,128)(2,1)} %bitcast.111, bf16[8,240,2048]{2,1,0:T(8,128)(2,1)} %bitcast.94, bf16[2048,768]{1,0:T(8,128)(2,1)} %bitcast.135, bf16[2048,768]{1,0:T(8,128)(2,1)} %bitcast.136), custom_call_target="tpu_custom_call" | custom-call | flops 1 | bytes 1 | tf_op jit(solution)/shard_map/geglu/geglu/pallas_call | solution.py:64
  290.4 10.8 %geglu.9 = (bf16[1664,256]{1,0:T(8,128)(2,1)}, bf16[1664,512]{1,0:T(8,128)(2,1)}) custom-call(bf16[8,208,2048]{2,1,0:T(8,128)(2,1)} %bitcast.112, bf16[8,240,2048]{2,1,0:T(8,128)(2,1)} %bitcast.95, bf16[2048,768]{1,0:T(8,128)(2,1)} %collective-permute-done.18.gate_up_ref.down_ref.refs_5_.refs_9_, ...), custom_call_target="tpu_custom_call" | custom-call | flops 1 | bytes 1 | tf_op jit(solution)/shard_map/geglu/geglu/pallas_call | solution.py:64
  301.2 10.7 %geglu.10 = (bf16[1664,256]{1,0:T(8,128)(2,1)}, bf16[1664,512]{1,0:T(8,128)(2,1)}) custom-call(bf16[8,208,2048]{2,1,0:T(8,128)(2,1)} %bitcast.113, bf16[8,240,2048]{2,1,0:T(8,128)(2,1)} %bitcast.96, bf16[2048,768]{1,0:T(8,128)(2,1)} %collective-permute-done.19.gate_up_ref.down_ref.refs_6_.refs_10_, ...), custom_call_target="tpu_custom_call" | custom-call | flops 1 | bytes 1 | tf_op jit(solution)/shard_map/geglu/geglu/pallas_call | solution.py:64
  315.7 10.7 %geglu.11 = (bf16[1664,256]{1,0:T(8,128)(2,1)}, bf16[1664,512]{1,0:T(8,128)(2,1)}) custom-call(bf16[8,208,2048]{2,1,0:T(8,128)(2,1)} %bitcast.114, bf16[8,240,2048]{2,1,0:T(8,128)(2,1)} %bitcast.97, bf16[2048,768]{1,0:T(8,128)(2,1)} %pad_maximum_fusion.gate_up_ref.down_ref.refs_7_.refs_11_, ...), custom_call_target="tpu_custom_call" | custom-call | flops 1 | bytes 1 | tf_op jit(solution)/shard_map/geglu/geglu/pallas_call | solution.py:64
  335.5 11.0 %weight_grad.8 = bf16[2048,768]{1,0:T(8,128)(2,1)} custom-call(bf16[8,208,2048]{2,1,0:T(8,128)(2,1)} %bitcast.115, bf16[8,240,2048]{2,1,0:T(8,128)(2,1)} %bitcast.98, bf16[1664,512]{1,0:T(8,128)(2,1)} %get-tuple-element.500.grad_ref.refs_1_, bf16[1664,256]{1,0:T(8,128)(2,1)} %get-tuple-element.501.hidden_ref.refs_1_), custom_call_target="tpu_custom_call" | custom-call | flops 1 | bytes 1 | tf_op jit(solution)/shard_map/geglu/weight_grad/pallas_call | solution.py:126
  355.7 11.0 %weight_grad.9 = bf16[2048,768]{1,0:T(8,128)(2,1)} custom-call(bf16[8,208,2048]{2,1,0:T(8,128)(2,1)} %bitcast.116, bf16[8,240,2048]{2,1,0:T(8,128)(2,1)} %bitcast.99, bf16[1664,512]{1,0:T(8,128)(2,1)} %get-tuple-element.516.grad_ref.refs_2_, bf16[1664,256]{1,0:T(8,128)(2,1)} %get-tuple-element.517.hidden_ref.refs_2_), custom_call_target="tpu_custom_call" | custom-call | flops 1 | bytes 1 | tf_op jit(solution)/shard_map/geglu/weight_grad/pallas_call | solution.py:126
  376.0 11.1 %weight_grad.10 = bf16[2048,768]{1,0:T(8,128)(2,1)} custom-call(bf16[8,208,2048]{2,1,0:T(8,128)(2,1)} %bitcast.117, bf16[8,240,2048]{2,1,0:T(8,128)(2,1)} %bitcast.101, bf16[1664,512]{1,0:T(8,128)(2,1)} %get-tuple-element.544.grad_ref.refs_0_, bf16[1664,256]{1,0:T(8,128)(2,1)} %get-tuple-element.601.hidden_ref.refs_0_), custom_call_target="tpu_custom_call" | custom-call | flops 1 | bytes 1 | tf_op jit(solution)/shard_map/geglu/weight_grad/pallas_call | solution.py:126
  387.1 10.8 %geglu.12 = (bf16[1664,256]{1,0:T(8,128)(2,1)}, bf16[1664,512]{1,0:T(8,128)(2,1)}) custom-call(bf16[8,208,2048]{2,1,0:T(8,128)(2,1)} %bitcast.118, bf16[8,240,2048]{2,1,0:T(8,128)(2,1)} %bitcast.102, bf16[2048,768]{1,0:T(8,128)(2,1)} %bitcast.129, bf16[2048,768]{1,0:T(8,128)(2,1)} %bitcast.130), custom_call_target="tpu_custom_call" | custom-call | flops 1 | bytes 1 | tf_op jit(solution)/shard_map/geglu/geglu/pallas_call | solution.py:64
  407.3 22.0 %contract.3.refs_8_ = f32[1664,2048]{1,0:T(8,128)} custom-call(bf16[1664,512]{1,0:T(8,128)(2,1)} %get-tuple-element.544.grad_ref.refs_0_, bf16[1664,512]{1,0:T(8,128)(2,1)} %get-tuple-element.500.grad_ref.refs_1_, bf16[1664,512]{1,0:T(8,128)(2,1)} %get-tuple-element.516.grad_ref.refs_2_, bf16[1664,512]{1,0:T(8,128)(2,1)} %get-tuple-element.545.refs_3_.grad_ref, ...), custom_call_target="tpu_custom_call" | custom-call | flops 1 | bytes 1 | tf_op jit(solution)/shard_map/geglu/contract/pallas_call | solution.py:101
  434.6 11.0 %weight_grad.11 = bf16[2048,768]{1,0:T(8,128)(2,1)} custom-call(bf16[8,208,2048]{2,1,0:T(8,128)(2,1)} %bitcast.119, bf16[8,240,2048]{2,1,0:T(8,128)(2,1)} %bitcast.103, bf16[1664,512]{1,0:T(8,128)(2,1)} %get-tuple-element.545.refs_3_.grad_ref, bf16[1664,256]{1,0:T(8,128)(2,1)} %get-tuple-element.550.hidden_ref.refs_3_), custom_call_target="tpu_custom_call" | custom-call | flops 1 | bytes 1 | tf_op jit(solution)/shard_map/geglu/weight_grad/pallas_call | solution.py:126
  462.4 10.7 %geglu.13 = (bf16[1664,256]{1,0:T(8,128)(2,1)}, bf16[1664,512]{1,0:T(8,128)(2,1)}) custom-call(bf16[8,208,2048]{2,1,0:T(8,128)(2,1)} %bitcast.120, bf16[8,240,2048]{2,1,0:T(8,128)(2,1)} %bitcast.104, bf16[2048,768]{1,0:T(8,128)(2,1)} %collective-permute-done.31.gate_up_ref.down_ref.refs_5_.refs_13_, ...), custom_call_target="tpu_custom_call" | custom-call | flops 1 | bytes 1 | tf_op jit(solution)/shard_map/geglu/geglu/pallas_call | solution.py:64
  477.6 10.7 %geglu.14 = (bf16[1664,256]{1,0:T(8,128)(2,1)}, bf16[1664,512]{1,0:T(8,128)(2,1)}) custom-call(bf16[8,208,2048]{2,1,0:T(8,128)(2,1)} %bitcast.121, bf16[8,240,2048]{2,1,0:T(8,128)(2,1)} %bitcast.105, bf16[2048,768]{1,0:T(8,128)(2,1)} %collective-permute-done.32.gate_up_ref.down_ref.refs_6_.refs_14_, ...), custom_call_target="tpu_custom_call" | custom-call | flops 1 | bytes 1 | tf_op jit(solution)/shard_map/geglu/geglu/pallas_call | solution.py:64
  498.8 10.7 %geglu.15 = (bf16[1664,256]{1,0:T(8,128)(2,1)}, bf16[1664,512]{1,0:T(8,128)(2,1)}) custom-call(bf16[8,208,2048]{2,1,0:T(8,128)(2,1)} %bitcast.122, bf16[8,240,2048]{2,1,0:T(8,128)(2,1)} %bitcast.106, bf16[2048,768]{1,0:T(8,128)(2,1)} %pad_maximum_fusion.1.gate_up_ref.down_ref.refs_7_.refs_15_, ...), custom_call_target="tpu_custom_call" | custom-call | flops 1 | bytes 1 | tf_op jit(solution)/shard_map/geglu/geglu/pallas_call | solution.py:64
  509.5 22.5 %contract.4 = bf16[1664,2048]{1,0:T(8,128)(2,1)} custom-call(bf16[1664,512]{1,0:T(8,128)(2,1)} %get-tuple-element.593.refs_0_.grad_ref, bf16[1664,512]{1,0:T(8,128)(2,1)} %get-tuple-element.594.refs_1_.grad_ref, bf16[1664,512]{1,0:T(8,128)(2,1)} %get-tuple-element.595.refs_2_.grad_ref, bf16[1664,512]{1,0:T(8,128)(2,1)} %get-tuple-element.596.refs_3_.grad_ref, ...), custom_call_target="tpu_custom_call" | custom-call | flops 1 | bytes 1 | tf_op jit(solution)/shard_map/geglu/contract/pallas_call | solution.py:101
  537.7 27.8 %collective-permute-done.41 = bf16[1024,768]{1,0:T(8,128)(2,1)} collective-permute-done((bf16[1024,768]{1,0:T(8,128)(2,1)S(1)}, bf16[1024,768]{1,0:T(8,128)(2,1)}, u32[]{:S(2)}, u32[]{:S(2)}) %collective-permute-start.41) | collective-permute-done | bytes 1572896 | tf_op jit(solution)/shard_map/geglu/ppermute | solution.py:148
  566.6 21.7 %contract.5 = bf16[1664,2048]{1,0:T(8,128)(2,1)} custom-call(bf16[1664,256]{1,0:T(8,128)(2,1)} %get-tuple-element.601.hidden_ref.refs_0_, bf16[1664,256]{1,0:T(8,128)(2,1)} %get-tuple-element.501.hidden_ref.refs_1_, bf16[1664,256]{1,0:T(8,128)(2,1)} %get-tuple-element.517.hidden_ref.refs_2_, bf16[1664,256]{1,0:T(8,128)(2,1)} %get-tuple-element.550.hidden_ref.refs_3_, ...), custom_call_target="tpu_custom_call" | custom-call | flops 1 | bytes 1 | tf_op jit(solution)/shard_map/geglu/contract/pallas_call | solution.py:101
  595.3 11.0 %weight_grad.12 = bf16[2048,768]{1,0:T(8,128)(2,1)} custom-call(bf16[8,208,2048]{2,1,0:T(8,128)(2,1)} %bitcast.123, bf16[8,240,2048]{2,1,0:T(8,128)(2,1)} %bitcast.107, bf16[1664,512]{1,0:T(8,128)(2,1)} %get-tuple-element.596.refs_3_.grad_ref, bf16[1664,256]{1,0:T(8,128)(2,1)} %get-tuple-element.605.refs_7_.hidden_ref), custom_call_target="tpu_custom_call" | custom-call | flops 1 | bytes 1 | tf_op jit(solution)/shard_map/geglu/weight_grad/pallas_call | solution.py:126
  606.4 11.1 %weight_grad.13 = bf16[2048,768]{1,0:T(8,128)(2,1)} custom-call(bf16[8,208,2048]{2,1,0:T(8,128)(2,1)} %bitcast.124, bf16[8,240,2048]{2,1,0:T(8,128)(2,1)} %bitcast.108, bf16[1664,512]{1,0:T(8,128)(2,1)} %get-tuple-element.595.refs_2_.grad_ref, bf16[1664,256]{1,0:T(8,128)(2,1)} %get-tuple-element.604.refs_6_.hidden_ref), custom_call_target="tpu_custom_call" | custom-call | flops 1 | bytes 1 | tf_op jit(solution)/shard_map/geglu/weight_grad/pallas_call | solution.py:126
  635.2 11.3 %weight_grad.14 = bf16[2048,768]{1,0:T(8,128)(2,1)} custom-call(bf16[8,208,2048]{2,1,0:T(8,128)(2,1)} %bitcast.125, bf16[8,240,2048]{2,1,0:T(8,128)(2,1)} %bitcast.109, bf16[1664,512]{1,0:T(8,128)(2,1)} %get-tuple-element.594.refs_1_.grad_ref, bf16[1664,256]{1,0:T(8,128)(2,1)} %get-tuple-element.603.refs_5_.hidden_ref), custom_call_target="tpu_custom_call" | custom-call | flops 1 | bytes 1 | tf_op jit(solution)/shard_map/geglu/weight_grad/pallas_call | solution.py:126
  650.0 11.2 %weight_grad.15 = bf16[2048,768]{1,0:T(8,128)(2,1)} custom-call(bf16[8,208,2048]{2,1,0:T(8,128)(2,1)} %bitcast.126, bf16[8,240,2048]{2,1,0:T(8,128)(2,1)} %bitcast.110, bf16[1664,512]{1,0:T(8,128)(2,1)} %get-tuple-element.593.refs_0_.grad_ref, bf16[1664,256]{1,0:T(8,128)(2,1)} %get-tuple-element.602.refs_4_.hidden_ref), custom_call_target="tpu_custom_call" | custom-call | flops 1 | bytes 1 | tf_op jit(solution)/shard_map/middle_norm/weight_grad/pallas_call | solution.py:126
  668.4 10.7 %all-to-all-start.3 = ((bf16[8,320,768]{2,1,0:T(8,128)(2,1)}), bf16[8,320,768]{2,1,0:T(8,128)(2,1)}, u32[]{:S(2)}, u32[]{:S(2)}) async-start(bf16[8,320,768]{2,1,0:T(8,128)(2,1)} %fusion.7), calls=%async_computation.5 | async-start | bytes 7864320 | tf_op jit(solution)/shard_map/middle_norm/all_to_all | solution.py:152
  702.2 19.6 %collective-permute-done.46 = bf16[208,2048]{1,0:T(8,128)(2,1)S(1)} collective-permute-done((bf16[208,2048]{1,0:T(8,128)(2,1)}, bf16[208,2048]{1,0:T(8,128)(2,1)S(1)}, u32[]{:S(2)}, u32[]{:S(2)}) %collective-permute-start.46) | collective-permute-done | bytes 852000 | tf_op jit(solution)/shard_map/middle_norm/ppermute | solution.py:148
  741.4 12.9 %attend_back.3 = (bf16[832,512]{1,0:T(8,128)(2,1)}, bf16[896,512]{1,0:T(8,128)(2,1)}) custom-call(s32[1]{0:T(128)S(6)} %copy.113.cams_ref, s32[1]{0:T(128)S(6)} %copy.114.texts_ref, bf16[832,640]{1,0:T(8,128)(2,1)} %copy-done.28, bf16[832,512]{1,0:T(8,128)(2,1)} %convolution_convert_fusion.5.gm_ref, bf16[832,512]{1,0:T(8,128)(2,1)} %copy-done.6, ...), custom_call_target="tpu_custom_call" | custom-call | flops 1 | bytes 1 | tf_op jit(solution)/shard_map/attention_back/attend_back/pallas_call | solution.py:361
  782.9 35.3 %collective-permute-done.50 = bf16[896,128]{1,0:T(8,128)(2,1)S(1)} collective-permute-done((bf16[896,128]{1,0:T(8,128)(2,1)S(1)}, bf16[896,128]{1,0:T(8,128)(2,1)S(1)}, u32[]{:S(2)}, u32[]{:S(2)}) %collective-permute-start.50) | collective-permute-done | bytes 229408 | tf_op jit(solution)/shard_map/attention_back/ppermute | solution.py:148
  842.7 14.5 %collective-permute-done.59 = bf16[1024,768]{1,0:T(8,128)(2,1)} collective-permute-done((bf16[1024,768]{1,0:T(8,128)(2,1)}, bf16[1024,768]{1,0:T(8,128)(2,1)}, u32[]{:S(2)}, u32[]{:S(2)}) %collective-permute-start.59) | collective-permute-done | bytes 1572896 | tf_op jit(solution)/shard_map/attention_back/ppermute | solution.py:148
  886.5 17.2 %collective-permute-done.56 = bf16[208,2048]{1,0:T(8,128)(2,1)} collective-permute-done((bf16[208,2048]{1,0:T(8,128)(2,1)}, bf16[208,2048]{1,0:T(8,128)(2,1)}, u32[]{:S(2)}, u32[]{:S(2)}) %collective-permute-start.56) | collective-permute-done | bytes 852000 | tf_op jit(solution)/shard_map/attention_back/ppermute | solution.py:148
  938.6 14.3 %collective-permute-done.76 = f32[2,768]{1,0:T(2,128)S(1)} collective-permute-done((f32[2,768]{1,0:T(2,128)S(1)}, f32[2,768]{1,0:T(2,128)S(1)}, u32[]{:S(2)}, u32[]{:S(2)}) %collective-permute-start.76) | collective-permute-done | bytes 6176 | tf_op jit(solution)/shard_map/gain_grads/ppermute | solution.py:148
  (603 shorter events, 444.3 us)
Async XLA Ops:
  7.2 88.3 %all-gather.10.cloned.1.call-start = ((), (), s32[]{:S(2)}) async-start(), calls=%async_computation.9 | async-start | bytes 2949120 | tf_op jit(solution)/shard_map/attention_weights/all_gather | solution.py:586
  12.0 119.5 %all-gather.12.cloned.1.call-start = ((), (), s32[]{:S(2)}) async-start(), calls=%async_computation.10 | async-start | bytes 2359296 | tf_op jit(solution)/shard_map/attention_weights/all_gather | solution.py:588
  12.8 249.9 %all-gather.16.cloned.1.call-start = ((), (), s32[]{:S(2)}) async-start(), calls=%async_computation.15 | async-start | bytes 8847360 | tf_op jit(solution)/shard_map/token_features/all_gather | solution.py:605
  34.5 97.1 %all-to-all-start = ((bf16[8,256,768]{2,1,0:T(8,128)(2,1)}), bf16[8,256,768]{2,1,0:T(8,128)(2,1)S(1)}, u32[]{:S(2)}, u32[]{:S(2)}) async-start(bf16[8,256,768]{2,1,0:T(8,128)(2,1)} %get-tuple-element.437), calls=%async_computation | async-start | bytes 6291456 | tf_op jit(solution)/shard_map/unit_weights/all_to_all | solution.py:152
  39.6 234.8 %all-gather.18.cloned.1.call-start = ((), (), s32[]{:S(2)}) async-start(), calls=%async_computation.16 | async-start | bytes 7667712 | tf_op jit(solution)/shard_map/attention/all_gather | solution.py:633
  39.6 46.4 %collective-permute-start = (bf16[864,512]{1,0:T(8,128)(2,1)}, bf16[864,512]{1,0:T(8,128)(2,1)}, u32[]{:S(2)}, u32[]{:S(2)}) collective-permute-start(bf16[864,512]{1,0:T(8,128)(2,1)} %fusion.18), channel_id=1, source_target_pairs={{0,1},{1,0},{2,3},{3,2},{4,5},{5,4},{6,7},{7,6},{8,9},{9,8},{10,11... | collective-permute-start | bytes 2654216 | tf_op jit(solution)/shard_map/token_features/ppermute | solution.py:148
  40.2 45.8 %collective-permute-start.1 = (bf16[864,512]{1,0:T(8,128)(2,1)}, bf16[864,512]{1,0:T(8,128)(2,1)}, u32[]{:S(2)}, u32[]{:S(2)}) collective-permute-start(bf16[864,512]{1,0:T(8,128)(2,1)} %fusion.18), channel_id=1, source_target_pairs={{0,2},{1,3},{2,0},{3,1},{4,6},{5,7},{6,4},{7,5},{8,10},{9,11},{10,... | collective-permute-start | bytes 2654216 | tf_op jit(solution)/shard_map/token_features/ppermute | solution.py:148
  41.7 44.3 %collective-permute-start.2 = (bf16[864,512]{1,0:T(8,128)(2,1)}, bf16[864,512]{1,0:T(8,128)(2,1)}, u32[]{:S(2)}, u32[]{:S(2)}) collective-permute-start(bf16[864,512]{1,0:T(8,128)(2,1)} %fusion.18), channel_id=1, source_target_pairs={{0,3},{1,2},{2,1},{3,0},{4,7},{5,6},{6,5},{7,4},{8,11},{9,10},{10,... | collective-permute-start | bytes 2654216 | tf_op jit(solution)/shard_map/token_features/ppermute | solution.py:148
  180.4 146.1 %all-gather.20.cloned.1.call-start = ((), (), s32[]{:S(2)}) async-start(), calls=%async_computation.17 | async-start | bytes 2654208 | tf_op jit(solution)/shard_map/attention/all_gather | solution.py:639
  180.9 69.1 %collective-permute-start.18 = (bf16[2048,768]{1,0:T(8,128)(2,1)S(1)}, bf16[2048,768]{1,0:T(8,128)(2,1)}, u32[]{:S(2)}, u32[]{:S(2)}) collective-permute-start(bf16[2048,768]{1,0:T(8,128)(2,1)S(1)} %bitcast.133), channel_id=1, source_target_pairs={{0,1},{1,0},{2,3},{3,2},{4,5},{5,4},{6,7},{7,6},{8,9},{9,8},{10,11... | collective-permute-start | bytes 9437192 | tf_op jit(solution)/shard_map/attention/ppermute | solution.py:148
  182.2 69.2 %collective-permute-start.19 = (bf16[2048,768]{1,0:T(8,128)(2,1)S(1)}, bf16[2048,768]{1,0:T(8,128)(2,1)}, u32[]{:S(2)}, u32[]{:S(2)}) collective-permute-start(bf16[2048,768]{1,0:T(8,128)(2,1)S(1)} %bitcast.134), channel_id=1, source_target_pairs={{0,2},{1,3},{2,0},{3,1},{4,6},{5,7},{6,4},{7,5},{8,10},{9,11},{10,... | collective-permute-start | bytes 9437192 | tf_op jit(solution)/shard_map/attention/ppermute | solution.py:148
  189.5 73.1 %all-to-all-start.1 = ((bf16[8,128,384]{2,1,0:T(8,128)(2,1)}), bf16[8,128,384]{2,1,0:T(8,128)(2,1)}, u32[]{:S(2)}, u32[]{:S(2)}) async-start(bf16[8,128,384]{2,1,0:T(8,128)(2,1)} %pack.3), calls=%async_computation.1 | async-start | bytes 1572864 | tf_op jit(solution)/shard_map/attention/all_to_all | solution.py:152
  254.0 57.9 %collective-permute-start.20 = (bf16[1024,768]{1,0:T(8,128)(2,1)}, bf16[1024,768]{1,0:T(8,128)(2,1)}, u32[]{:S(2)}, u32[]{:S(2)}) collective-permute-start(bf16[1024,768]{1,0:T(8,128)(2,1)} %slice.198), channel_id=1, source_target_pairs={{0,1},{1,0},{2,3},{3,2},{4,5},{5,4},{6,7},{7,6},{8,9},{9,8},{10,11... | collective-permute-start | bytes 4718600 | tf_op jit(solution)/shard_map/attention/ppermute | solution.py:148
  257.0 54.9 %collective-permute-start.21 = (bf16[1024,768]{1,0:T(8,128)(2,1)}, bf16[1024,768]{1,0:T(8,128)(2,1)}, u32[]{:S(2)}, u32[]{:S(2)}) collective-permute-start(bf16[1024,768]{1,0:T(8,128)(2,1)} %slice.199), channel_id=1, source_target_pairs={{0,2},{1,3},{2,0},{3,1},{4,6},{5,7},{6,4},{7,5},{8,10},{9,11},{10,... | collective-permute-start | bytes 4718600 | tf_op jit(solution)/shard_map/attention/ppermute | solution.py:148
  274.4 98.6 %all-to-all-start.2 = ((bf16[8,256,768]{2,1,0:T(8,128)(2,1)}), bf16[8,256,768]{2,1,0:T(8,128)(2,1)S(1)}, u32[]{:S(2)}, u32[]{:S(2)}) async-start(bf16[8,256,768]{2,1,0:T(8,128)(2,1)} %get-tuple-element.526), calls=%async_computation.2 | async-start | bytes 6291456 | tf_op jit(solution)/shard_map/geglu/all_to_all | solution.py:152
  278.1 119.9 %all-gather.14.cloned.1.call-start = ((), (), s32[]{:S(2)}) async-start(), calls=%async_computation.11 | async-start | bytes 1179648 | tf_op jit(solution)/shard_map/geglu/all_gather | solution.py:689
  368.3 278.3 %reduce-scatter.9.cloned.1.call-start = ((), (), s32[]{:S(2)}) async-start(), calls=%async_computation.13 | async-start | bytes 7667712 | tf_op jit(solution)/shard_map/geglu/reduce_scatter | solution.py:739
  373.0 74.2 %collective-permute-start.31 = (bf16[2048,768]{1,0:T(8,128)(2,1)S(1)}, bf16[2048,768]{1,0:T(8,128)(2,1)}, u32[]{:S(2)}, u32[]{:S(2)}) collective-permute-start(bf16[2048,768]{1,0:T(8,128)(2,1)S(1)} %bitcast.127), channel_id=1, source_target_pairs={{0,1},{1,0},{2,3},{3,2},{4,5},{5,4},{6,7},{7,6},{8,9},{9,8},{10,11... | collective-permute-start | bytes 9437192 | tf_op jit(solution)/shard_map/geglu/ppermute | solution.py:148
  374.5 72.8 %collective-permute-start.32 = (bf16[2048,768]{1,0:T(8,128)(2,1)S(1)}, bf16[2048,768]{1,0:T(8,128)(2,1)}, u32[]{:S(2)}, u32[]{:S(2)}) collective-permute-start(bf16[2048,768]{1,0:T(8,128)(2,1)S(1)} %bitcast.128), channel_id=1, source_target_pairs={{0,2},{1,3},{2,0},{3,1},{4,6},{5,7},{6,4},{7,5},{8,10},{9,11},{10,... | collective-permute-start | bytes 9437192 | tf_op jit(solution)/shard_map/geglu/ppermute | solution.py:148
  532.1 379.8 %reduce-scatter.7.cloned.1.call-start = ((), (), s32[]{:S(2)}) async-start(), calls=%async_computation.12 | async-start | bytes 7667712 | tf_op jit(solution)/shard_map/geglu/reduce_scatter | solution.py:744
  668.4 103.0 %all-to-all-start.3 = ((bf16[8,320,768]{2,1,0:T(8,128)(2,1)}), bf16[8,320,768]{2,1,0:T(8,128)(2,1)}, u32[]{:S(2)}, u32[]{:S(2)}) async-start(bf16[8,320,768]{2,1,0:T(8,128)(2,1)} %fusion.7), calls=%async_computation.5 | async-start | bytes 7864320 | tf_op jit(solution)/shard_map/middle_norm/all_to_all | solution.py:152
  679.1 288.8 %reduce-scatter.13.cloned.1.call-start = ((), (), s32[]{:S(2)}) async-start(), calls=%async_computation.18 | async-start | bytes 3538944
  687.5 66.8 %collective-permute-start.53 = (bf16[1024,768]{1,0:T(8,128)(2,1)}, bf16[1024,768]{1,0:T(8,128)(2,1)}, u32[]{:S(2)}, u32[]{:S(2)}) collective-permute-start(bf16[1024,768]{1,0:T(8,128)(2,1)} %get-tuple-element.796), channel_id=1, source_target_pairs={{0,1},{1,0},{2,3},{3,2},{4,5},{5,4},{6,7},{7,6},{8,9},{9,8},{10,11... | collective-permute-start | bytes 4718600 | tf_op jit(solution)/shard_map/middle_norm/ppermute | solution.py:148
  688.8 66.0 %collective-permute-start.54 = (bf16[1024,768]{1,0:T(8,128)(2,1)}, bf16[1024,768]{1,0:T(8,128)(2,1)}, u32[]{:S(2)}, u32[]{:S(2)}) collective-permute-start(bf16[1024,768]{1,0:T(8,128)(2,1)} %get-tuple-element.795), channel_id=1, source_target_pairs={{0,2},{1,3},{2,0},{3,1},{4,6},{5,7},{6,4},{7,5},{8,10},{9,11},{10,... | collective-permute-start | bytes 4718600 | tf_op jit(solution)/shard_map/middle_norm/ppermute | solution.py:148
  771.5 199.2 %reduce-scatter.11.cloned.1.call-start = ((), (), s32[]{:S(2)}) async-start(), calls=%async_computation.14 | async-start | bytes 4423680 | tf_op jit(solution)/shard_map/query_key_value_grads/reduce_scatter | solution.py:809
  775.8 66.9 %collective-permute-start.58 = (bf16[1024,768]{1,0:T(8,128)(2,1)}, bf16[1024,768]{1,0:T(8,128)(2,1)}, u32[]{:S(2)}, u32[]{:S(2)}) collective-permute-start(bf16[1024,768]{1,0:T(8,128)(2,1)} %slice.226), channel_id=1, source_target_pairs={{0,1},{1,0},{2,3},{3,2},{4,5},{5,4},{6,7},{7,6},{8,9},{9,8},{10,11... | collective-permute-start | bytes 4718600 | tf_op jit(solution)/shard_map/middle_norm/ppermute | solution.py:148
  777.3 65.4 %collective-permute-start.60 = (bf16[1024,768]{1,0:T(8,128)(2,1)}, bf16[1024,768]{1,0:T(8,128)(2,1)}, u32[]{:S(2)}, u32[]{:S(2)}) collective-permute-start(bf16[1024,768]{1,0:T(8,128)(2,1)} %slice.228), channel_id=1, source_target_pairs={{0,2},{1,3},{2,0},{3,1},{4,6},{5,7},{6,4},{7,5},{8,10},{9,11},{10,... | collective-permute-start | bytes 4718600 | tf_op jit(solution)/shard_map/middle_norm/ppermute | solution.py:148
  779.5 43.8 %collective-permute-start.51 = (bf16[896,128]{1,0:T(8,128)(2,1)S(1)}, bf16[896,128]{1,0:T(8,128)(2,1)S(1)}, u32[]{:S(2)}, u32[]{:S(2)}) collective-permute-start(bf16[896,128]{1,0:T(8,128)(2,1)S(1)} %get-tuple-element.808), channel_id=1, source_target_pairs={{0,2},{1,3},{2,0},{3,1},{4,6},{5,7},{6,4},{7,5},{8,10},{9,11},{10,... | collective-permute-start | bytes 688136 | tf_op jit(solution)/shard_map/attention_back/ppermute | solution.py:148
  780.1 44.0 %collective-permute-start.52 = (bf16[896,128]{1,0:T(8,128)(2,1)S(1)}, bf16[896,128]{1,0:T(8,128)(2,1)S(1)}, u32[]{:S(2)}, u32[]{:S(2)}) collective-permute-start(bf16[896,128]{1,0:T(8,128)(2,1)S(1)} %get-tuple-element.807), channel_id=1, source_target_pairs={{0,3},{1,2},{2,1},{3,0},{4,7},{5,6},{6,5},{7,4},{8,11},{9,10},{10,... | collective-permute-start | bytes 688136 | tf_op jit(solution)/shard_map/attention_back/ppermute | solution.py:148
  870.2 106.8 %all-to-all-start.4 = ((bf16[8,256,768]{2,1,0:T(8,128)(2,1)}), bf16[8,256,768]{2,1,0:T(8,128)(2,1)}, u32[]{:S(2)}, u32[]{:S(2)}) async-start(bf16[8,256,768]{2,1,0:T(8,128)(2,1)} %bitcast.140), calls=%async_computation.6 | async-start | bytes 6291456 | tf_op jit(solution)/shard_map/query_key_value_grads/all_to_all | solution.py:152
  918.9 45.7 %collective-permute-start.62 = (bf16[208,512]{1,0:T(8,128)(2,1)S(1)}, bf16[208,512]{1,0:T(8,128)(2,1)S(1)}, u32[]{:S(2)}, u32[]{:S(2)}) collective-permute-start(bf16[208,512]{1,0:T(8,128)(2,1)S(1)} %get-tuple-element.817), channel_id=1, source_target_pairs={{0,1},{1,0},{2,3},{3,2},{4,5},{5,4},{6,7},{7,6},{8,9},{9,8},{10,11... | collective-permute-start | bytes 638984 | tf_op jit(solution)/shard_map/input_grads/ppermute | solution.py:148
  920.5 44.2 %collective-permute-start.63 = (bf16[208,512]{1,0:T(8,128)(2,1)S(1)}, bf16[208,512]{1,0:T(8,128)(2,1)S(1)}, u32[]{:S(2)}, u32[]{:S(2)}) collective-permute-start(bf16[208,512]{1,0:T(8,128)(2,1)S(1)} %get-tuple-element.816), channel_id=1, source_target_pairs={{0,2},{1,3},{2,0},{3,1},{4,6},{5,7},{6,4},{7,5},{8,10},{9,11},{10,... | collective-permute-start | bytes 638984 | tf_op jit(solution)/shard_map/input_grads/ppermute | solution.py:148
  (170 other events, 2962.4 us)
Sparse Core Ops, SparseCore 0:
  12.1 40.1 all-gather.9
  53.9 68.8 all-gather.11
  124.5 77.7 all-gather.15
  204.4 70.0 all-gather.17
  276.5 49.8 all-gather.19
  368.4 29.5 all-gather.13
  532.3 80.8 reduce-scatter.8
  615.5 76.0 reduce-scatter.6
  771.6 38.9 reduce-scatter.12
  839.4 52.6 reduce-scatter.10

commit v4 on v3

--- a/solution.py
+++ b/solution.py
@@ -119,7 +119,7 @@
     out_ref[:, 2 * units :] = mm_tn(g_ref[...].reshape(rows, cols), hidden_ref[...]).astype(BF)
 
 
-def weight_grad(normed, cots, grad, hidden, block, cols=512):
+def weight_grad(normed, cots, grad, hidden, block, cols=1024):
     n, _, width = normed.shape
     units = hidden.shape[1]
     rows = n * block

time: 1010 us -> 1010 us (level)
  no operation moved by 1% of the time
where the time goes in v4:
time: 1010 us; the launch traced here: 995 us
  waiting for transfers between devices  334 us (33%)
  Pallas kernels  317 us (31%)
  starting transfers between devices  129 us (13%)
  local copies, waits for them, and re-layouts  86 us (9%)
  other arithmetic  76.9 us (8%)
  matrix products  33.6 us (3%)
  between operations  17.9 us (2%)
    ppermute x77, waiting for transfers between devices, swap(): return lax.ppermute(a, axis, [(i, i ^ step) for i in range(size)])  306 us
    ppermute x77, starting transfers between devices, swap(): return lax.ppermute(a, axis, [(i, i ^ step) for i in range(size)])  101 us
    pallas_call x8, Pallas kernels, weight_grad(): pl.pallas_call(weight_grad_kernel, grid=(width // cols,), in_specs=[pl.Bl...  88.8 us
    pallas_call x8, Pallas kernels, geglu(): pl.pallas_call(geglu_kernel, grid=(n // step,), in_specs=[pl.BlockSpec((s...  86.1 us
    pallas_call x3, Pallas kernels, contract(): pl.pallas_call(functools.partial(contract_kernel, count), grid=(width //...  66.4 us
    dot_general x16, matrix products, dot(): lax.dot_general(a, b, (((over_a,), (over_b,)), ((), ())), preferred_eleme...  33.6 us
    all_to_all x5, starting transfers between devices, exchange(): return lax.all_to_all(a, 'dp', 0, 0, tiled=True)  27.8 us
    unnamed x227, local copies, waits for them, and re-layouts  20.4 us
  transfers between devices with their start and end apart: 92, of which 32 were waited for; matrix products, arithmetic and copies ran while one was open for 17% of the time, Pallas kernels for 29%

profile of v4, /device:TPU:0, one launch (start us, length us, event | category | flops | bytes accessed | tf_op | source)
XLA Modules:
  0.0 995.0 jit_solution(806702298952187386)
XLA Ops:
  45.3 35.7 %collective-permute-done.3 = f32[1,1536]{1,0:T(1,128)S(1)} collective-permute-done((f32[1,1536]{1,0:T(1,128)S(1)}, f32[1,1536]{1,0:T(1,128)S(1)}, u32[]{:S(2)}, u32[]{:S(2)}) %collective-permute-start.3) | collective-permute-done | bytes 6176 | tf_op jit(solution)/shard_map/token_features/ppermute | solution.py:148
  141.3 17.4 %collective-permute-done.15 = bf16[208,2048]{1,0:T(8,128)(2,1)S(1)} collective-permute-done((bf16[208,2048]{1,0:T(8,128)(2,1)S(1)}, bf16[208,2048]{1,0:T(8,128)(2,1)S(1)}, u32[]{:S(2)}, u32[]{:S(2)}) %collective-permute-start.15) | collective-permute-done | bytes 852000 | tf_op jit(solution)/shard_map/attention/ppermute | solution.py:148
  158.7 18.6 %collective-permute-done.16 = bf16[208,2048]{1,0:T(8,128)(2,1)S(1)} collective-permute-done((bf16[208,2048]{1,0:T(8,128)(2,1)S(1)}, bf16[208,2048]{1,0:T(8,128)(2,1)S(1)}, u32[]{:S(2)}, u32[]{:S(2)}) %collective-permute-start.16) | collective-permute-done | bytes 852000 | tf_op jit(solution)/shard_map/attention/ppermute | solution.py:148
  193.6 56.2 %collective-permute-done.18.gate_up_ref.down_ref.refs_5_.refs_9_ = bf16[2048,768]{1,0:T(8,128)(2,1)} collective-permute-done((bf16[2048,768]{1,0:T(8,128)(2,1)S(1)}, bf16[2048,768]{1,0:T(8,128)(2,1)}, u32[]{:S(2)}, u32[]{:S(2)}) %collective-permute-start.18) | collective-permute-done | bytes 3145760 | tf_op jit(solution)/shard_map/attention/ppermute | solution.py:148
  262.5 12.2 %all-gather.18.cloned.1.call-done = bf16[1664,2048]{1,0:T(8,128)(2,1)} async-done(((bf16[208,2048]{1,0:T(8,128)(2,1)}), bf16[1664,2048]{1,0:T(8,128)(2,1)}) %all-gather.18.cloned.1.call-update) | async-done | bytes 6815760 | tf_op jit(solution)/shard_map/attention/all_gather | solution.py:633
  279.8 10.9 %geglu.8 = (bf16[1664,256]{1,0:T(8,128)(2,1)}, bf16[1664,512]{1,0:T(8,128)(2,1)}) custom-call(bf16[8,208,2048]{2,1,0:T(8,128)(2,1)} %bitcast.111, bf16[8,240,2048]{2,1,0:T(8,128)(2,1)} %bitcast.94, bf16[2048,768]{1,0:T(8,128)(2,1)} %bitcast.135, bf16[2048,768]{1,0:T(8,128)(2,1)} %bitcast.136), custom_call_target="tpu_custom_call" | custom-call | flops 1 | bytes 1 | tf_op jit(solution)/shard_map/geglu/geglu/pallas_call | solution.py:64
  290.7 10.8 %geglu.9 = (bf16[1664,256]{1,0:T(8,128)(2,1)}, bf16[1664,512]{1,0:T(8,128)(2,1)}) custom-call(bf16[8,208,2048]{2,1,0:T(8,128)(2,1)} %bitcast.112, bf16[8,240,2048]{2,1,0:T(8,128)(2,1)} %bitcast.95, bf16[2048,768]{1,0:T(8,128)(2,1)} %collective-permute-done.18.gate_up_ref.down_ref.refs_5_.refs_9_, ...), custom_call_target="tpu_custom_call" | custom-call | flops 1 | bytes 1 | tf_op jit(solution)/shard_map/geglu/geglu/pallas_call | solution.py:64
  301.5 10.7 %geglu.10 = (bf16[1664,256]{1,0:T(8,128)(2,1)}, bf16[1664,512]{1,0:T(8,128)(2,1)}) custom-call(bf16[8,208,2048]{2,1,0:T(8,128)(2,1)} %bitcast.113, bf16[8,240,2048]{2,1,0:T(8,128)(2,1)} %bitcast.96, bf16[2048,768]{1,0:T(8,128)(2,1)} %collective-permute-done.19.gate_up_ref.down_ref.refs_6_.refs_10_, ...), custom_call_target="tpu_custom_call" | custom-call | flops 1 | bytes 1 | tf_op jit(solution)/shard_map/geglu/geglu/pallas_call | solution.py:64
  316.0 10.7 %geglu.11 = (bf16[1664,256]{1,0:T(8,128)(2,1)}, bf16[1664,512]{1,0:T(8,128)(2,1)}) custom-call(bf16[8,208,2048]{2,1,0:T(8,128)(2,1)} %bitcast.114, bf16[8,240,2048]{2,1,0:T(8,128)(2,1)} %bitcast.97, bf16[2048,768]{1,0:T(8,128)(2,1)} %pad_maximum_fusion.gate_up_ref.down_ref.refs_7_.refs_11_, ...), custom_call_target="tpu_custom_call" | custom-call | flops 1 | bytes 1 | tf_op jit(solution)/shard_map/geglu/geglu/pallas_call | solution.py:64
  335.8 11.0 %weight_grad.8 = bf16[2048,768]{1,0:T(8,128)(2,1)} custom-call(bf16[8,208,2048]{2,1,0:T(8,128)(2,1)} %bitcast.115, bf16[8,240,2048]{2,1,0:T(8,128)(2,1)} %bitcast.98, bf16[1664,512]{1,0:T(8,128)(2,1)} %get-tuple-element.500.grad_ref.refs_1_, bf16[1664,256]{1,0:T(8,128)(2,1)} %get-tuple-element.501.hidden_ref.refs_1_), custom_call_target="tpu_custom_call" | custom-call | flops 1 | bytes 1 | tf_op jit(solution)/shard_map/geglu/weight_grad/pallas_call | solution.py:126
  356.0 11.0 %weight_grad.9 = bf16[2048,768]{1,0:T(8,128)(2,1)} custom-call(bf16[8,208,2048]{2,1,0:T(8,128)(2,1)} %bitcast.116, bf16[8,240,2048]{2,1,0:T(8,128)(2,1)} %bitcast.99, bf16[1664,512]{1,0:T(8,128)(2,1)} %get-tuple-element.516.grad_ref.refs_2_, bf16[1664,256]{1,0:T(8,128)(2,1)} %get-tuple-element.517.hidden_ref.refs_2_), custom_call_target="tpu_custom_call" | custom-call | flops 1 | bytes 1 | tf_op jit(solution)/shard_map/geglu/weight_grad/pallas_call | solution.py:126
  376.3 11.0 %weight_grad.10 = bf16[2048,768]{1,0:T(8,128)(2,1)} custom-call(bf16[8,208,2048]{2,1,0:T(8,128)(2,1)} %bitcast.117, bf16[8,240,2048]{2,1,0:T(8,128)(2,1)} %bitcast.101, bf16[1664,512]{1,0:T(8,128)(2,1)} %get-tuple-element.544.grad_ref.refs_0_, bf16[1664,256]{1,0:T(8,128)(2,1)} %get-tuple-element.601.hidden_ref.refs_0_), custom_call_target="tpu_custom_call" | custom-call | flops 1 | bytes 1 | tf_op jit(solution)/shard_map/geglu/weight_grad/pallas_call | solution.py:126
  387.3 10.7 %geglu.12 = (bf16[1664,256]{1,0:T(8,128)(2,1)}, bf16[1664,512]{1,0:T(8,128)(2,1)}) custom-call(bf16[8,208,2048]{2,1,0:T(8,128)(2,1)} %bitcast.118, bf16[8,240,2048]{2,1,0:T(8,128)(2,1)} %bitcast.102, bf16[2048,768]{1,0:T(8,128)(2,1)} %bitcast.129, bf16[2048,768]{1,0:T(8,128)(2,1)} %bitcast.130), custom_call_target="tpu_custom_call" | custom-call | flops 1 | bytes 1 | tf_op jit(solution)/shard_map/geglu/geglu/pallas_call | solution.py:64
  407.7 22.0 %contract.3.refs_8_ = f32[1664,2048]{1,0:T(8,128)} custom-call(bf16[1664,512]{1,0:T(8,128)(2,1)} %get-tuple-element.544.grad_ref.refs_0_, bf16[1664,512]{1,0:T(8,128)(2,1)} %get-tuple-element.500.grad_ref.refs_1_, bf16[1664,512]{1,0:T(8,128)(2,1)} %get-tuple-element.516.grad_ref.refs_2_, bf16[1664,512]{1,0:T(8,128)(2,1)} %get-tuple-element.545.refs_3_.grad_ref, ...), custom_call_target="tpu_custom_call" | custom-call | flops 1 | bytes 1 | tf_op jit(solution)/shard_map/geglu/contract/pallas_call | solution.py:101
  434.9 11.0 %weight_grad.11 = bf16[2048,768]{1,0:T(8,128)(2,1)} custom-call(bf16[8,208,2048]{2,1,0:T(8,128)(2,1)} %bitcast.119, bf16[8,240,2048]{2,1,0:T(8,128)(2,1)} %bitcast.103, bf16[1664,512]{1,0:T(8,128)(2,1)} %get-tuple-element.545.refs_3_.grad_ref, bf16[1664,256]{1,0:T(8,128)(2,1)} %get-tuple-element.550.hidden_ref.refs_3_), custom_call_target="tpu_custom_call" | custom-call | flops 1 | bytes 1 | tf_op jit(solution)/shard_map/geglu/weight_grad/pallas_call | solution.py:126
  462.9 10.9 %geglu.13 = (bf16[1664,256]{1,0:T(8,128)(2,1)}, bf16[1664,512]{1,0:T(8,128)(2,1)}) custom-call(bf16[8,208,2048]{2,1,0:T(8,128)(2,1)} %bitcast.120, bf16[8,240,2048]{2,1,0:T(8,128)(2,1)} %bitcast.104, bf16[2048,768]{1,0:T(8,128)(2,1)} %collective-permute-done.31.gate_up_ref.down_ref.refs_5_.refs_13_, ...), custom_call_target="tpu_custom_call" | custom-call | flops 1 | bytes 1 | tf_op jit(solution)/shard_map/geglu/geglu/pallas_call | solution.py:64
  478.0 10.7 %geglu.14 = (bf16[1664,256]{1,0:T(8,128)(2,1)}, bf16[1664,512]{1,0:T(8,128)(2,1)}) custom-call(bf16[8,208,2048]{2,1,0:T(8,128)(2,1)} %bitcast.121, bf16[8,240,2048]{2,1,0:T(8,128)(2,1)} %bitcast.105, bf16[2048,768]{1,0:T(8,128)(2,1)} %collective-permute-done.32.gate_up_ref.down_ref.refs_6_.refs_14_, ...), custom_call_target="tpu_custom_call" | custom-call | flops 1 | bytes 1 | tf_op jit(solution)/shard_map/geglu/geglu/pallas_call | solution.py:64
  499.1 10.7 %geglu.15 = (bf16[1664,256]{1,0:T(8,128)(2,1)}, bf16[1664,512]{1,0:T(8,128)(2,1)}) custom-call(bf16[8,208,2048]{2,1,0:T(8,128)(2,1)} %bitcast.122, bf16[8,240,2048]{2,1,0:T(8,128)(2,1)} %bitcast.106, bf16[2048,768]{1,0:T(8,128)(2,1)} %pad_maximum_fusion.1.gate_up_ref.down_ref.refs_7_.refs_15_, ...), custom_call_target="tpu_custom_call" | custom-call | flops 1 | bytes 1 | tf_op jit(solution)/shard_map/geglu/geglu/pallas_call | solution.py:64
  509.8 22.5 %contract.4 = bf16[1664,2048]{1,0:T(8,128)(2,1)} custom-call(bf16[1664,512]{1,0:T(8,128)(2,1)} %get-tuple-element.593.refs_0_.grad_ref, bf16[1664,512]{1,0:T(8,128)(2,1)} %get-tuple-element.594.refs_1_.grad_ref, bf16[1664,512]{1,0:T(8,128)(2,1)} %get-tuple-element.595.refs_2_.grad_ref, bf16[1664,512]{1,0:T(8,128)(2,1)} %get-tuple-element.596.refs_3_.grad_ref, ...), custom_call_target="tpu_custom_call" | custom-call | flops 1 | bytes 1 | tf_op jit(solution)/shard_map/geglu/contract/pallas_call | solution.py:101
  538.0 27.8 %collective-permute-done.41 = bf16[1024,768]{1,0:T(8,128)(2,1)} collective-permute-done((bf16[1024,768]{1,0:T(8,128)(2,1)S(1)}, bf16[1024,768]{1,0:T(8,128)(2,1)}, u32[]{:S(2)}, u32[]{:S(2)}) %collective-permute-start.41) | collective-permute-done | bytes 1572896 | tf_op jit(solution)/shard_map/geglu/ppermute | solution.py:148
  566.9 21.9 %contract.5 = bf16[1664,2048]{1,0:T(8,128)(2,1)} custom-call(bf16[1664,256]{1,0:T(8,128)(2,1)} %get-tuple-element.601.hidden_ref.refs_0_, bf16[1664,256]{1,0:T(8,128)(2,1)} %get-tuple-element.501.hidden_ref.refs_1_, bf16[1664,256]{1,0:T(8,128)(2,1)} %get-tuple-element.517.hidden_ref.refs_2_, bf16[1664,256]{1,0:T(8,128)(2,1)} %get-tuple-element.550.hidden_ref.refs_3_, ...), custom_call_target="tpu_custom_call" | custom-call | flops 1 | bytes 1 | tf_op jit(solution)/shard_map/geglu/contract/pallas_call | solution.py:101
  595.8 11.1 %weight_grad.12 = bf16[2048,768]{1,0:T(8,128)(2,1)} custom-call(bf16[8,208,2048]{2,1,0:T(8,128)(2,1)} %bitcast.123, bf16[8,240,2048]{2,1,0:T(8,128)(2,1)} %bitcast.107, bf16[1664,512]{1,0:T(8,128)(2,1)} %get-tuple-element.596.refs_3_.grad_ref, bf16[1664,256]{1,0:T(8,128)(2,1)} %get-tuple-element.605.refs_7_.hidden_ref), custom_call_target="tpu_custom_call" | custom-call | flops 1 | bytes 1 | tf_op jit(solution)/shard_map/geglu/weight_grad/pallas_call | solution.py:126
  606.9 11.1 %weight_grad.13 = bf16[2048,768]{1,0:T(8,128)(2,1)} custom-call(bf16[8,208,2048]{2,1,0:T(8,128)(2,1)} %bitcast.124, bf16[8,240,2048]{2,1,0:T(8,128)(2,1)} %bitcast.108, bf16[1664,512]{1,0:T(8,128)(2,1)} %get-tuple-element.595.refs_2_.grad_ref, bf16[1664,256]{1,0:T(8,128)(2,1)} %get-tuple-element.604.refs_6_.hidden_ref), custom_call_target="tpu_custom_call" | custom-call | flops 1 | bytes 1 | tf_op jit(solution)/shard_map/geglu/weight_grad/pallas_call | solution.py:126
  635.8 11.4 %weight_grad.14 = bf16[2048,768]{1,0:T(8,128)(2,1)} custom-call(bf16[8,208,2048]{2,1,0:T(8,128)(2,1)} %bitcast.125, bf16[8,240,2048]{2,1,0:T(8,128)(2,1)} %bitcast.109, bf16[1664,512]{1,0:T(8,128)(2,1)} %get-tuple-element.594.refs_1_.grad_ref, bf16[1664,256]{1,0:T(8,128)(2,1)} %get-tuple-element.603.refs_5_.hidden_ref), custom_call_target="tpu_custom_call" | custom-call | flops 1 | bytes 1 | tf_op jit(solution)/shard_map/geglu/weight_grad/pallas_call | solution.py:126
  650.7 11.2 %weight_grad.15 = bf16[2048,768]{1,0:T(8,128)(2,1)} custom-call(bf16[8,208,2048]{2,1,0:T(8,128)(2,1)} %bitcast.126, bf16[8,240,2048]{2,1,0:T(8,128)(2,1)} %bitcast.110, bf16[1664,512]{1,0:T(8,128)(2,1)} %get-tuple-element.593.refs_0_.grad_ref, bf16[1664,256]{1,0:T(8,128)(2,1)} %get-tuple-element.602.refs_4_.hidden_ref), custom_call_target="tpu_custom_call" | custom-call | flops 1 | bytes 1 | tf_op jit(solution)/shard_map/middle_norm/weight_grad/pallas_call | solution.py:126
  702.5 19.7 %collective-permute-done.46 = bf16[208,2048]{1,0:T(8,128)(2,1)S(1)} collective-permute-done((bf16[208,2048]{1,0:T(8,128)(2,1)}, bf16[208,2048]{1,0:T(8,128)(2,1)S(1)}, u32[]{:S(2)}, u32[]{:S(2)}) %collective-permute-start.46) | collective-permute-done | bytes 852000 | tf_op jit(solution)/shard_map/middle_norm/ppermute | solution.py:148
  741.7 12.9 %attend_back.3 = (bf16[832,512]{1,0:T(8,128)(2,1)}, bf16[896,512]{1,0:T(8,128)(2,1)}) custom-call(s32[1]{0:T(128)S(6)} %copy.113.cams_ref, s32[1]{0:T(128)S(6)} %copy.114.texts_ref, bf16[832,640]{1,0:T(8,128)(2,1)} %copy-done.28, bf16[832,512]{1,0:T(8,128)(2,1)} %convolution_convert_fusion.5.gm_ref, bf16[832,512]{1,0:T(8,128)(2,1)} %copy-done.6, ...), custom_call_target="tpu_custom_call" | custom-call | flops 1 | bytes 1 | tf_op jit(solution)/shard_map/attention_back/attend_back/pallas_call | solution.py:361
  761.5 10.3 %all-to-all-done.3.refs_0_ = bf16[8,320,768]{2,1,0:T(8,128)(2,1)} async-done(((bf16[8,320,768]{2,1,0:T(8,128)(2,1)}), bf16[8,320,768]{2,1,0:T(8,128)(2,1)}, u32[]{:S(2)}, u32[]{:S(2)}) %all-to-all-start.3) | async-done | bytes 3932192 | tf_op jit(solution)/shard_map/middle_norm/all_to_all | solution.py:152
  783.0 35.3 %collective-permute-done.50 = bf16[896,128]{1,0:T(8,128)(2,1)S(1)} collective-permute-done((bf16[896,128]{1,0:T(8,128)(2,1)S(1)}, bf16[896,128]{1,0:T(8,128)(2,1)S(1)}, u32[]{:S(2)}, u32[]{:S(2)}) %collective-permute-start.50) | collective-permute-done | bytes 229408 | tf_op jit(solution)/shard_map/attention_back/ppermute | solution.py:148
  842.8 14.5 %collective-permute-done.59 = bf16[1024,768]{1,0:T(8,128)(2,1)} collective-permute-done((bf16[1024,768]{1,0:T(8,128)(2,1)}, bf16[1024,768]{1,0:T(8,128)(2,1)}, u32[]{:S(2)}, u32[]{:S(2)}) %collective-permute-start.59) | collective-permute-done | bytes 1572896 | tf_op jit(solution)/shard_map/attention_back/ppermute | solution.py:148
  886.8 16.9 %collective-permute-done.56 = bf16[208,2048]{1,0:T(8,128)(2,1)} collective-permute-done((bf16[208,2048]{1,0:T(8,128)(2,1)}, bf16[208,2048]{1,0:T(8,128)(2,1)}, u32[]{:S(2)}, u32[]{:S(2)}) %collective-permute-start.56) | collective-permute-done | bytes 852000 | tf_op jit(solution)/shard_map/attention_back/ppermute | solution.py:148
  938.7 14.3 %collective-permute-done.76 = f32[2,768]{1,0:T(2,128)S(1)} collective-permute-done((f32[2,768]{1,0:T(2,128)S(1)}, f32[2,768]{1,0:T(2,128)S(1)}, u32[]{:S(2)}, u32[]{:S(2)}) %collective-permute-start.76) | collective-permute-done | bytes 6176 | tf_op jit(solution)/shard_map/gain_grads/ppermute | solution.py:148
  (603 shorter events, 444.0 us)
Async XLA Ops:
  7.2 88.3 %all-gather.10.cloned.1.call-start = ((), (), s32[]{:S(2)}) async-start(), calls=%async_computation.9 | async-start | bytes 2949120 | tf_op jit(solution)/shard_map/attention_weights/all_gather | solution.py:586
  12.0 119.5 %all-gather.12.cloned.1.call-start = ((), (), s32[]{:S(2)}) async-start(), calls=%async_computation.10 | async-start | bytes 2359296 | tf_op jit(solution)/shard_map/attention_weights/all_gather | solution.py:588
  12.8 249.7 %all-gather.16.cloned.1.call-start = ((), (), s32[]{:S(2)}) async-start(), calls=%async_computation.15 | async-start | bytes 8847360 | tf_op jit(solution)/shard_map/token_features/all_gather | solution.py:605
  34.5 97.1 %all-to-all-start = ((bf16[8,256,768]{2,1,0:T(8,128)(2,1)}), bf16[8,256,768]{2,1,0:T(8,128)(2,1)S(1)}, u32[]{:S(2)}, u32[]{:S(2)}) async-start(bf16[8,256,768]{2,1,0:T(8,128)(2,1)} %get-tuple-element.437), calls=%async_computation | async-start | bytes 6291456 | tf_op jit(solution)/shard_map/unit_weights/all_to_all | solution.py:152
  39.6 235.1 %all-gather.18.cloned.1.call-start = ((), (), s32[]{:S(2)}) async-start(), calls=%async_computation.16 | async-start | bytes 7667712 | tf_op jit(solution)/shard_map/attention/all_gather | solution.py:633
  39.6 46.4 %collective-permute-start = (bf16[864,512]{1,0:T(8,128)(2,1)}, bf16[864,512]{1,0:T(8,128)(2,1)}, u32[]{:S(2)}, u32[]{:S(2)}) collective-permute-start(bf16[864,512]{1,0:T(8,128)(2,1)} %fusion.18), channel_id=1, source_target_pairs={{0,1},{1,0},{2,3},{3,2},{4,5},{5,4},{6,7},{7,6},{8,9},{9,8},{10,11... | collective-permute-start | bytes 2654216 | tf_op jit(solution)/shard_map/token_features/ppermute | solution.py:148
  40.2 45.8 %collective-permute-start.1 = (bf16[864,512]{1,0:T(8,128)(2,1)}, bf16[864,512]{1,0:T(8,128)(2,1)}, u32[]{:S(2)}, u32[]{:S(2)}) collective-permute-start(bf16[864,512]{1,0:T(8,128)(2,1)} %fusion.18), channel_id=1, source_target_pairs={{0,2},{1,3},{2,0},{3,1},{4,6},{5,7},{6,4},{7,5},{8,10},{9,11},{10,... | collective-permute-start | bytes 2654216 | tf_op jit(solution)/shard_map/token_features/ppermute | solution.py:148
  41.7 44.3 %collective-permute-start.2 = (bf16[864,512]{1,0:T(8,128)(2,1)}, bf16[864,512]{1,0:T(8,128)(2,1)}, u32[]{:S(2)}, u32[]{:S(2)}) collective-permute-start(bf16[864,512]{1,0:T(8,128)(2,1)} %fusion.18), channel_id=1, source_target_pairs={{0,3},{1,2},{2,1},{3,0},{4,7},{5,6},{6,5},{7,4},{8,11},{9,10},{10,... | collective-permute-start | bytes 2654216 | tf_op jit(solution)/shard_map/token_features/ppermute | solution.py:148
  180.4 146.4 %all-gather.20.cloned.1.call-start = ((), (), s32[]{:S(2)}) async-start(), calls=%async_computation.17 | async-start | bytes 2654208 | tf_op jit(solution)/shard_map/attention/all_gather | solution.py:639
  180.8 69.1 %collective-permute-start.18 = (bf16[2048,768]{1,0:T(8,128)(2,1)S(1)}, bf16[2048,768]{1,0:T(8,128)(2,1)}, u32[]{:S(2)}, u32[]{:S(2)}) collective-permute-start(bf16[2048,768]{1,0:T(8,128)(2,1)S(1)} %bitcast.133), channel_id=1, source_target_pairs={{0,1},{1,0},{2,3},{3,2},{4,5},{5,4},{6,7},{7,6},{8,9},{9,8},{10,11... | collective-permute-start | bytes 9437192 | tf_op jit(solution)/shard_map/attention/ppermute | solution.py:148
  182.0 69.2 %collective-permute-start.19 = (bf16[2048,768]{1,0:T(8,128)(2,1)S(1)}, bf16[2048,768]{1,0:T(8,128)(2,1)}, u32[]{:S(2)}, u32[]{:S(2)}) collective-permute-start(bf16[2048,768]{1,0:T(8,128)(2,1)S(1)} %bitcast.134), channel_id=1, source_target_pairs={{0,2},{1,3},{2,0},{3,1},{4,6},{5,7},{6,4},{7,5},{8,10},{9,11},{10,... | collective-permute-start | bytes 9437192 | tf_op jit(solution)/shard_map/attention/ppermute | solution.py:148
  189.4 73.0 %all-to-all-start.1 = ((bf16[8,128,384]{2,1,0:T(8,128)(2,1)}), bf16[8,128,384]{2,1,0:T(8,128)(2,1)}, u32[]{:S(2)}, u32[]{:S(2)}) async-start(bf16[8,128,384]{2,1,0:T(8,128)(2,1)} %pack.3), calls=%async_computation.1 | async-start | bytes 1572864 | tf_op jit(solution)/shard_map/attention/all_to_all | solution.py:152
  253.9 58.4 %collective-permute-start.20 = (bf16[1024,768]{1,0:T(8,128)(2,1)}, bf16[1024,768]{1,0:T(8,128)(2,1)}, u32[]{:S(2)}, u32[]{:S(2)}) collective-permute-start(bf16[1024,768]{1,0:T(8,128)(2,1)} %slice.198), channel_id=1, source_target_pairs={{0,1},{1,0},{2,3},{3,2},{4,5},{5,4},{6,7},{7,6},{8,9},{9,8},{10,11... | collective-permute-start | bytes 4718600 | tf_op jit(solution)/shard_map/attention/ppermute | solution.py:148
  256.9 55.3 %collective-permute-start.21 = (bf16[1024,768]{1,0:T(8,128)(2,1)}, bf16[1024,768]{1,0:T(8,128)(2,1)}, u32[]{:S(2)}, u32[]{:S(2)}) collective-permute-start(bf16[1024,768]{1,0:T(8,128)(2,1)} %slice.199), channel_id=1, source_target_pairs={{0,2},{1,3},{2,0},{3,1},{4,6},{5,7},{6,4},{7,5},{8,10},{9,11},{10,... | collective-permute-start | bytes 4718600 | tf_op jit(solution)/shard_map/attention/ppermute | solution.py:148
  274.7 98.7 %all-to-all-start.2 = ((bf16[8,256,768]{2,1,0:T(8,128)(2,1)}), bf16[8,256,768]{2,1,0:T(8,128)(2,1)S(1)}, u32[]{:S(2)}, u32[]{:S(2)}) async-start(bf16[8,256,768]{2,1,0:T(8,128)(2,1)} %get-tuple-element.526), calls=%async_computation.2 | async-start | bytes 6291456 | tf_op jit(solution)/shard_map/geglu/all_to_all | solution.py:152
  278.3 119.9 %all-gather.14.cloned.1.call-start = ((), (), s32[]{:S(2)}) async-start(), calls=%async_computation.11 | async-start | bytes 1179648 | tf_op jit(solution)/shard_map/geglu/all_gather | solution.py:689
  368.6 278.6 %reduce-scatter.9.cloned.1.call-start = ((), (), s32[]{:S(2)}) async-start(), calls=%async_computation.13 | async-start | bytes 7667712 | tf_op jit(solution)/shard_map/geglu/reduce_scatter | solution.py:739
  373.3 74.2 %collective-permute-start.31 = (bf16[2048,768]{1,0:T(8,128)(2,1)S(1)}, bf16[2048,768]{1,0:T(8,128)(2,1)}, u32[]{:S(2)}, u32[]{:S(2)}) collective-permute-start(bf16[2048,768]{1,0:T(8,128)(2,1)S(1)} %bitcast.127), channel_id=1, source_target_pairs={{0,1},{1,0},{2,3},{3,2},{4,5},{5,4},{6,7},{7,6},{8,9},{9,8},{10,11... | collective-permute-start | bytes 9437192 | tf_op jit(solution)/shard_map/geglu/ppermute | solution.py:148
  374.8 72.7 %collective-permute-start.32 = (bf16[2048,768]{1,0:T(8,128)(2,1)S(1)}, bf16[2048,768]{1,0:T(8,128)(2,1)}, u32[]{:S(2)}, u32[]{:S(2)}) collective-permute-start(bf16[2048,768]{1,0:T(8,128)(2,1)S(1)} %bitcast.128), channel_id=1, source_target_pairs={{0,2},{1,3},{2,0},{3,1},{4,6},{5,7},{6,4},{7,5},{8,10},{9,11},{10,... | collective-permute-start | bytes 9437192 | tf_op jit(solution)/shard_map/geglu/ppermute | solution.py:148
  532.5 379.6 %reduce-scatter.7.cloned.1.call-start = ((), (), s32[]{:S(2)}) async-start(), calls=%async_computation.12 | async-start | bytes 7667712 | tf_op jit(solution)/shard_map/geglu/reduce_scatter | solution.py:744
  669.1 102.6 %all-to-all-start.3 = ((bf16[8,320,768]{2,1,0:T(8,128)(2,1)}), bf16[8,320,768]{2,1,0:T(8,128)(2,1)}, u32[]{:S(2)}, u32[]{:S(2)}) async-start(bf16[8,320,768]{2,1,0:T(8,128)(2,1)} %fusion.7), calls=%async_computation.5 | async-start | bytes 7864320 | tf_op jit(solution)/shard_map/middle_norm/all_to_all | solution.py:152
  679.3 288.7 %reduce-scatter.13.cloned.1.call-start = ((), (), s32[]{:S(2)}) async-start(), calls=%async_computation.18 | async-start | bytes 3538944
  687.8 66.8 %collective-permute-start.53 = (bf16[1024,768]{1,0:T(8,128)(2,1)}, bf16[1024,768]{1,0:T(8,128)(2,1)}, u32[]{:S(2)}, u32[]{:S(2)}) collective-permute-start(bf16[1024,768]{1,0:T(8,128)(2,1)} %get-tuple-element.796), channel_id=1, source_target_pairs={{0,1},{1,0},{2,3},{3,2},{4,5},{5,4},{6,7},{7,6},{8,9},{9,8},{10,11... | collective-permute-start | bytes 4718600 | tf_op jit(solution)/shard_map/middle_norm/ppermute | solution.py:148
  689.1 66.0 %collective-permute-start.54 = (bf16[1024,768]{1,0:T(8,128)(2,1)}, bf16[1024,768]{1,0:T(8,128)(2,1)}, u32[]{:S(2)}, u32[]{:S(2)}) collective-permute-start(bf16[1024,768]{1,0:T(8,128)(2,1)} %get-tuple-element.795), channel_id=1, source_target_pairs={{0,2},{1,3},{2,0},{3,1},{4,6},{5,7},{6,4},{7,5},{8,10},{9,11},{10,... | collective-permute-start | bytes 4718600 | tf_op jit(solution)/shard_map/middle_norm/ppermute | solution.py:148
  771.8 199.1 %reduce-scatter.11.cloned.1.call-start = ((), (), s32[]{:S(2)}) async-start(), calls=%async_computation.14 | async-start | bytes 4423680 | tf_op jit(solution)/shard_map/query_key_value_grads/reduce_scatter | solution.py:809
  775.9 66.9 %collective-permute-start.58 = (bf16[1024,768]{1,0:T(8,128)(2,1)}, bf16[1024,768]{1,0:T(8,128)(2,1)}, u32[]{:S(2)}, u32[]{:S(2)}) collective-permute-start(bf16[1024,768]{1,0:T(8,128)(2,1)} %slice.226), channel_id=1, source_target_pairs={{0,1},{1,0},{2,3},{3,2},{4,5},{5,4},{6,7},{7,6},{8,9},{9,8},{10,11... | collective-permute-start | bytes 4718600 | tf_op jit(solution)/shard_map/middle_norm/ppermute | solution.py:148
  777.4 65.4 %collective-permute-start.60 = (bf16[1024,768]{1,0:T(8,128)(2,1)}, bf16[1024,768]{1,0:T(8,128)(2,1)}, u32[]{:S(2)}, u32[]{:S(2)}) collective-permute-start(bf16[1024,768]{1,0:T(8,128)(2,1)} %slice.228), channel_id=1, source_target_pairs={{0,2},{1,3},{2,0},{3,1},{4,6},{5,7},{6,4},{7,5},{8,10},{9,11},{10,... | collective-permute-start | bytes 4718600 | tf_op jit(solution)/shard_map/middle_norm/ppermute | solution.py:148
  779.7 43.8 %collective-permute-start.51 = (bf16[896,128]{1,0:T(8,128)(2,1)S(1)}, bf16[896,128]{1,0:T(8,128)(2,1)S(1)}, u32[]{:S(2)}, u32[]{:S(2)}) collective-permute-start(bf16[896,128]{1,0:T(8,128)(2,1)S(1)} %get-tuple-element.808), channel_id=1, source_target_pairs={{0,2},{1,3},{2,0},{3,1},{4,6},{5,7},{6,4},{7,5},{8,10},{9,11},{10,... | collective-permute-start | bytes 688136 | tf_op jit(solution)/shard_map/attention_back/ppermute | solution.py:148
  780.2 44.0 %collective-permute-start.52 = (bf16[896,128]{1,0:T(8,128)(2,1)S(1)}, bf16[896,128]{1,0:T(8,128)(2,1)S(1)}, u32[]{:S(2)}, u32[]{:S(2)}) collective-permute-start(bf16[896,128]{1,0:T(8,128)(2,1)S(1)} %get-tuple-element.807), channel_id=1, source_target_pairs={{0,3},{1,2},{2,1},{3,0},{4,7},{5,6},{6,5},{7,4},{8,11},{9,10},{10,... | collective-permute-start | bytes 688136 | tf_op jit(solution)/shard_map/attention_back/ppermute | solution.py:148
  870.3 106.8 %all-to-all-start.4 = ((bf16[8,256,768]{2,1,0:T(8,128)(2,1)}), bf16[8,256,768]{2,1,0:T(8,128)(2,1)}, u32[]{:S(2)}, u32[]{:S(2)}) async-start(bf16[8,256,768]{2,1,0:T(8,128)(2,1)} %bitcast.140), calls=%async_computation.6 | async-start | bytes 6291456 | tf_op jit(solution)/shard_map/query_key_value_grads/all_to_all | solution.py:152
  919.0 45.8 %collective-permute-start.62 = (bf16[208,512]{1,0:T(8,128)(2,1)S(1)}, bf16[208,512]{1,0:T(8,128)(2,1)S(1)}, u32[]{:S(2)}, u32[]{:S(2)}) collective-permute-start(bf16[208,512]{1,0:T(8,128)(2,1)S(1)} %get-tuple-element.817), channel_id=1, source_target_pairs={{0,1},{1,0},{2,3},{3,2},{4,5},{5,4},{6,7},{7,6},{8,9},{9,8},{10,11... | collective-permute-start | bytes 638984 | tf_op jit(solution)/shard_map/input_grads/ppermute | solution.py:148
  920.6 44.2 %collective-permute-start.63 = (bf16[208,512]{1,0:T(8,128)(2,1)S(1)}, bf16[208,512]{1,0:T(8,128)(2,1)S(1)}, u32[]{:S(2)}, u32[]{:S(2)}) collective-permute-start(bf16[208,512]{1,0:T(8,128)(2,1)S(1)} %get-tuple-element.816), channel_id=1, source_target_pairs={{0,2},{1,3},{2,0},{3,1},{4,6},{5,7},{6,4},{7,5},{8,10},{9,11},{10,... | collective-permute-start | bytes 638984 | tf_op jit(solution)/shard_map/input_grads/ppermute | solution.py:148
  (170 other events, 2962.3 us)
Sparse Core Ops, SparseCore 0:
  12.1 40.1 all-gather.9
  53.9 68.8 all-gather.11
  124.5 77.9 all-gather.15
  204.6 70.0 all-gather.17
  276.7 49.8 all-gather.19
  368.7 29.5 all-gather.13
  532.6 80.8 reduce-scatter.8
  615.8 76.1 reduce-scatter.6
  771.9 38.9 reduce-scatter.12
  839.5 52.4 reduce-scatter.10
